TPU v7x, 1024 devices: a whole 4x4x32 slice. The times are simulated.
1024 devices in a mesh: rep: 32 (over y, z_hi, x), exp: 32 (over z_lo, core).
Axes of the slice: x: 4, y: 4, z: 32 (z_hi: 2, z_lo: 16; z = z_hi * 16 + z_lo), core: 2. Of those that a mesh axis runs over, the one named last changes fastest.
Arguments:
- tokens: bfloat16 [64, 256, 1280], P('exp'), may hold values from -6 to 6
- slot_proj: bfloat16 [1280, 64], replicated
- in_weight: bfloat16 [64, 1280, 5120], P('exp', None, 'rep'), may hold values from -0.15625 to 0.15625
- out_weight: bfloat16 [64, 5120, 1280], P('exp', 'rep'), may hold values from -0.078125 to 0.078125
- out_grad: bfloat16 [64, 256, 1280], P('exp'), may hold values from -6 to 6
Outputs:
- mixed: bfloat16 [64, 256, 1280], P('exp')
- token_grad: bfloat16 [64, 256, 1280], P('exp')
- proj_grad: bfloat16 [1280, 64], replicated
- in_weight_grad: bfloat16 [64, 1280, 5120], P('exp', None, 'rep')
- out_weight_grad: bfloat16 [64, 5120, 1280], P('exp', 'rep')
All inputs are finite; a program needn't handle non-finite values.
Results may differ from a plain program's by a relative error of at most 0.04.
Values may be sent and summed in bfloat16 or wider, within the bound.
No kernel may reach another device: no remote copies, remote signals or barrier semaphores. Data moves between devices by JAX's collectives and lax.ppermute only.
A program may use at most 32 MiB of HBM per device.

v0:
```python
import jax
import jax.numpy as jnp
from jax import lax
from jax.sharding import PartitionSpec as P


def smooth(values):
    return jax.nn.gelu(values, approximate=True)


def bring_home(partial_value):
    summed = lax.psum(partial_value, "rep").astype(jnp.bfloat16)
    return lax.all_to_all(summed, "exp", split_axis=0, concat_axis=1, tiled=True)


def on_device(tokens, slot_proj, in_weight, out_weight, out_grad):
    logits = jnp.einsum("itd,de->ite", tokens, slot_proj, preferred_element_type=jnp.float32)
    dispatch = jax.nn.softmax(logits, axis=1)
    combine = jax.nn.softmax(logits, axis=2)
    dispatch_b = dispatch.astype(jnp.bfloat16)
    combine_b = combine.astype(jnp.bfloat16)
    slot_rows = jnp.einsum(
        "ite,itd->ied", dispatch_b, tokens, preferred_element_type=jnp.float32
    ).astype(jnp.bfloat16)
    expert_grad = jnp.einsum(
        "ite,itd->ied", combine_b, out_grad, preferred_element_type=jnp.float32
    ).astype(jnp.bfloat16)
    got_slots = lax.all_to_all(slot_rows, "exp", split_axis=1, concat_axis=0, tiled=True)
    pre_act = jnp.einsum("red,edf->ref", got_slots, in_weight, preferred_element_type=jnp.float32)
    activated, pullback = jax.vjp(smooth, pre_act)
    hidden = activated.astype(jnp.bfloat16)
    expert_out = bring_home(
        jnp.einsum("ref,efd->red", hidden, out_weight, preferred_element_type=jnp.float32)
    )
    mixed = jnp.einsum(
        "ite,ied->itd", combine_b, expert_out, preferred_element_type=jnp.float32
    ).astype(jnp.bfloat16)
    got_grads = lax.all_to_all(expert_grad, "exp", split_axis=1, concat_axis=0, tiled=True)
    combine_grad = jnp.einsum(
        "itd,ied->ite", out_grad, expert_out, preferred_element_type=jnp.float32
    )
    hidden_grad = jnp.einsum(
        "red,efd->ref", got_grads, out_weight, preferred_element_type=jnp.float32
    )
    pre_grad = pullback(hidden_grad)[0].astype(jnp.bfloat16)
    out_weight_grad = jnp.einsum(
        "ref,red->efd", hidden, got_grads, preferred_element_type=jnp.float32
    ).astype(jnp.bfloat16)
    in_weight_grad = jnp.einsum(
        "red,ref->edf", got_slots, pre_grad, preferred_element_type=jnp.float32
    ).astype(jnp.bfloat16)
    slot_grad = bring_home(
        jnp.einsum("ref,edf->red", pre_grad, in_weight, preferred_element_type=jnp.float32)
    )
    dispatch_grad = jnp.einsum(
        "itd,ied->ite", tokens, slot_grad, preferred_element_type=jnp.float32
    )
    from_dispatch = dispatch * (
        dispatch_grad - jnp.sum(dispatch * dispatch_grad, axis=1, keepdims=True)
    )
    from_combine = combine * (combine_grad - jnp.sum(combine * combine_grad, axis=2, keepdims=True))
    logit_grad = (from_dispatch + from_combine).astype(jnp.bfloat16)
    token_grad = (
        jnp.einsum("ite,ied->itd", dispatch_b, slot_grad, preferred_element_type=jnp.float32)
        + jnp.einsum("ite,de->itd", logit_grad, slot_proj, preferred_element_type=jnp.float32)
    ).astype(jnp.bfloat16)
    local_proj = jnp.einsum("itd,ite->de", tokens, logit_grad, preferred_element_type=jnp.float32)
    proj_grad = lax.psum(local_proj, "exp").astype(jnp.bfloat16)
    return (mixed, token_grad, proj_grad, in_weight_grad, out_weight_grad)


def solution(mesh):
    placed = (
        P("exp", None, None),
        P(),
        P("exp", None, "rep"),
        P("exp", "rep", None),
        P("exp", None, None),
    )
    return jax.shard_map(
        on_device,
        mesh=mesh,
        in_specs=placed,
        out_specs=(
            P("exp", None, None),
            P("exp", None, None),
            P(),
            P("exp", None, "rep"),
            P("exp", "rep", None),
        ),
        check_vma=False,
    )
```

profile of v0, /device:TPU:24, one launch (start us, length us, event | category | flops | bytes accessed | tf_op | source)
XLA Modules:
  0.0 1080.6 jit_solution(5137082371538023216)
XLA Ops:
  0.6 0.0 copy-start
  0.6 1.3 copy-done
  2.0 1.4 fusion.20
  3.4 0.0 copy-start.4
  3.4 0.8 fusion.37
  4.1 0.0 copy-start.1
  4.1 0.4 convolution_convert_fusion.4
  4.5 1.1 copy.14
  5.6 26.2 %all-to-all-start = ((bf16[2,64,1280]{2,0,1:T(2,128)(2,1)}), bf16[2,64,1280]{2,0,1:T(2,128)(2,1)S(1)}, u32[]{:S(2)}, u32[]{:S(2)}) async-start(bf16[2,64,1280]{2,0,1:T(2,128)(2,1)} %copy.14), calls=%async_computation | async-start | bytes 655360 | tf_op jit(solution)/shard_map/all_to_all | solution.py:28
  31.8 0.7 fusion.38
  32.5 0.0 copy-done.4
  32.5 0.0 copy-done.1
  32.5 0.4 convolution_convert_fusion.3
  32.8 1.1 copy.18
  33.9 35.4 %all-to-all-done = bf16[2,64,1280]{2,0,1:T(2,128)(2,1)S(1)} async-done(((bf16[2,64,1280]{2,0,1:T(2,128)(2,1)}), bf16[2,64,1280]{2,0,1:T(2,128)(2,1)S(1)}, u32[]{:S(2)}, u32[]{:S(2)}) %all-to-all-start) | async-done | bytes 327712 | tf_op jit(solution)/shard_map/all_to_all | solution.py:28
  69.3 0.0 copy-start.7
  69.3 11.9 %all-to-all-start.2 = ((bf16[2,64,1280]{2,0,1:T(2,128)(2,1)}), bf16[2,64,1280]{2,0,1:T(2,128)(2,1)}, u32[]{:S(2)}, u32[]{:S(2)}) async-start(bf16[2,64,1280]{2,0,1:T(2,128)(2,1)} %copy.18), calls=%async_computation.2 | async-start | bytes 655360 | tf_op jit(solution)/shard_map/all_to_all | solution.py:38
  81.2 0.0 copy-done.7
  81.2 0.0 copy-start.2
  81.2 2.0 copy.29
  83.2 1.8 all_to_all.55
  85.1 33.7 %all-to-all-done.2 = bf16[2,64,1280]{2,0,1:T(2,128)(2,1)} async-done(((bf16[2,64,1280]{2,0,1:T(2,128)(2,1)}), bf16[2,64,1280]{2,0,1:T(2,128)(2,1)}, u32[]{:S(2)}, u32[]{:S(2)}) %all-to-all-start.2) | async-done | bytes 327712 | tf_op jit(solution)/shard_map/all_to_all | solution.py:38
  118.7 1.9 copy.27
  120.7 1.8 all_to_all.63
  122.5 0.0 copy-done.2
  122.5 0.0 copy-start.10
  122.5 1.4 convolution_bitcast_fusion.4
  123.9 0.0 copy-done.10
  123.9 0.0 copy-start.8
  124.0 1.1 convolution_bitcast_fusion.1
  125.1 0.0 copy-done.5
  125.1 0.4 fusion.28
  125.5 0.0 copy-done.8
  125.5 1.1 convolution_bitcast_fusion
  126.6 506.0 %all-reduce.3 = (bf16[64,2,1280]{2,0,1:T(8,128)(2,1)}, bf16[64,2,1280]{2,0,1:T(8,128)(2,1)S(1)}) all-reduce(f32[64,2,1280]{2,0,1:T(8,128)} %convolution_bitcast_fusion.1, f32[64,2,1280]{2,0,1:T(8,128)} %convolution_bitcast_fusion), channel_id=1, replica_groups=mesh['rep'=32,'exp'=32] {'rep'}, use_global_device_ids=true, to_apply=%region_4.0 | all-reduce | flops 327680 | bytes 1966080 | tf_op jit(solution)/shard_map/psum | solution.py:12
  632.6 1.1 copy.20
  633.7 6.5 all-to-all-start.3
  640.2 0.0 copy-start.6
  640.2 0.0 copy-start.9
  640.2 2.1 copy.16
  642.3 35.4 %all-to-all-done.3 = bf16[64,2,1280]{2,1,0:T(2,128)(2,1)} async-done(((bf16[64,2,1280]{2,1,0:T(2,128)(2,1)}), bf16[64,2,1280]{2,1,0:T(2,128)(2,1)}, u32[]{:S(2)}, u32[]{:S(2)}) %all-to-all-start.3) | async-done | bytes 327712 | tf_op jit(solution)/shard_map/all_to_all | solution.py:13
  677.7 11.9 %all-to-all-start.1 = ((bf16[64,2,1280]{2,1,0:T(2,128)(2,1)}), bf16[64,2,1280]{2,1,0:T(2,128)(2,1)}, u32[]{:S(2)}, u32[]{:S(2)}) async-start(bf16[64,2,1280]{2,1,0:T(2,128)(2,1)} %copy.16), calls=%async_computation.1 | async-start | bytes 655360 | tf_op jit(solution)/shard_map/all_to_all | solution.py:13
  689.6 0.0 copy-done.3
  689.6 1.3 convolution_convert_fusion.2
  691.0 0.0 copy-done.6
  691.0 0.0 copy-done.9
  691.0 1.3 convolution_convert_fusion.1
  692.3 1.2 copy.26
  693.5 0.1 all_to_all.67
  693.6 0.5 convolution_bitcast_fusion.6
  694.1 3.2 fusion.30
  697.3 29.9 %all-to-all-done.1 = bf16[64,2,1280]{2,1,0:T(2,128)(2,1)} async-done(((bf16[64,2,1280]{2,1,0:T(2,128)(2,1)}), bf16[64,2,1280]{2,1,0:T(2,128)(2,1)}, u32[]{:S(2)}, u32[]{:S(2)}) %all-to-all-start.1) | async-done | bytes 327712 | tf_op jit(solution)/shard_map/all_to_all | solution.py:13
  727.2 1.2 copy.28
  728.4 0.1 all_to_all.59
  728.5 0.0 copy-start.12
  728.5 0.5 convolution_bitcast_fusion.5
  729.0 2.6 convolution_convert_fusion
  731.6 0.0 copy-done.12
  731.6 0.4 fusion.13
  732.0 0.0 copy-start.11
  732.0 1.4 convolution_bitcast_fusion.2
  733.4 343.7 %all-reduce.4 = bf16[1280,64]{0,1:T(8,128)(2,1)} all-reduce(f32[1280,64]{0,1:T(8,128)S(1)} %convolution_bitcast_fusion.2), channel_id=1, replica_groups=mesh['rep'=32,'exp'=32] {'exp'}, use_global_device_ids=true, to_apply=%region_8.0 | all-reduce | flops 81920 | bytes 491520 | tf_op jit(solution)/shard_map/psum | solution.py:68
  1077.1 0.0 copy-done.11
  1077.1 3.5 fusion.4
  (2 shorter events, 0.0 us)
Async XLA Ops:
  0.6 1.3 copy-start
  3.4 29.1 %copy-start.4 = (f32[2,256,64]{1,2,0:T(8,128)}, f32[2,256,64]{1,2,0:T(8,128)S(1)}, u32[]{:S(2)}) copy-start(f32[2,256,64]{1,2,0:T(8,128)S(1)} %fusion.20) | copy-start | bytes 393220
  4.1 28.3 %copy-start.1 = (bf16[2,256,1280]{2,1,0:T(8,128)(2,1)S(1)}, bf16[2,256,1280]{2,1,0:T(8,128)(2,1)}, u32[]{:S(2)}) copy-start(bf16[2,256,1280]{2,1,0:T(8,128)(2,1)} %param.9) | copy-start | bytes 3932164
  5.6 63.7 %all-to-all-start = ((bf16[2,64,1280]{2,0,1:T(2,128)(2,1)}), bf16[2,64,1280]{2,0,1:T(2,128)(2,1)S(1)}, u32[]{:S(2)}, u32[]{:S(2)}) async-start(bf16[2,64,1280]{2,0,1:T(2,128)(2,1)} %copy.14), calls=%async_computation | async-start | bytes 655360 | tf_op jit(solution)/shard_map/all_to_all | solution.py:28
  69.3 11.9 %copy-start.7 = (bf16[2,64,1280]{2,0,1:T(2,128)(2,1)}, bf16[2,64,1280]{2,0,1:T(2,128)(2,1)S(1)}, u32[]{:S(2)}) copy-start(bf16[2,64,1280]{2,0,1:T(2,128)(2,1)S(1)} %all-to-all-done) | copy-start | bytes 983044
  69.3 49.4 %all-to-all-start.2 = ((bf16[2,64,1280]{2,0,1:T(2,128)(2,1)}), bf16[2,64,1280]{2,0,1:T(2,128)(2,1)}, u32[]{:S(2)}, u32[]{:S(2)}) async-start(bf16[2,64,1280]{2,0,1:T(2,128)(2,1)} %copy.18), calls=%async_computation.2 | async-start | bytes 655360 | tf_op jit(solution)/shard_map/all_to_all | solution.py:38
  81.2 41.3 %copy-start.2 = (bf16[2,1280,160]{1,2,0:T(8,128)(2,1)S(1)}, bf16[2,1280,160]{1,2,0:T(8,128)(2,1)}, u32[]{:S(2)}) copy-start(bf16[2,1280,160]{1,2,0:T(8,128)(2,1)} %param.7) | copy-start | bytes 2457604
  122.5 1.5 copy-start.10
  122.5 2.6 copy-start.5
  123.9 1.6 copy-start.8
  632.6 57.0 %copy-start.3 = (bf16[64,2,1280]{2,0,1:T(8,128)(2,1)S(1)}, bf16[64,2,1280]{2,0,1:T(8,128)(2,1)}, u32[]{:S(2)}) copy-start(bf16[64,2,1280]{2,0,1:T(8,128)(2,1)} %all_to_all.55) | copy-start | bytes 983044
  633.7 44.0 %all-to-all-start.3 = ((bf16[64,2,1280]{2,1,0:T(2,128)(2,1)}), bf16[64,2,1280]{2,1,0:T(2,128)(2,1)}, u32[]{:S(2)}, u32[]{:S(2)}) async-start(bf16[64,2,1280]{2,1,0:T(2,128)(2,1)} %copy.20), calls=%async_computation.3 | async-start | bytes 655360 | tf_op jit(solution)/shard_map/all_to_all | solution.py:13
  640.2 50.7 %copy-start.6 = (bf16[64,2,1280]{2,0,1:T(8,128)(2,1)S(1)}, bf16[64,2,1280]{2,0,1:T(8,128)(2,1)}, u32[]{:S(2)}) copy-start(bf16[64,2,1280]{2,0,1:T(8,128)(2,1)} %all_to_all.63) | copy-start | bytes 983044
  640.2 50.7 %copy-start.9 = (f32[64,2,160]{2,0,1:T(8,128)S(1)}, f32[64,2,160]{2,0,1:T(8,128)}, u32[]{:S(2)}) copy-start(f32[64,2,160]{2,0,1:T(8,128)} %copy-done.8) | copy-start | bytes 245764
  677.7 49.4 %all-to-all-start.1 = ((bf16[64,2,1280]{2,1,0:T(2,128)(2,1)}), bf16[64,2,1280]{2,1,0:T(2,128)(2,1)}, u32[]{:S(2)}, u32[]{:S(2)}) async-start(bf16[64,2,1280]{2,1,0:T(2,128)(2,1)} %copy.16), calls=%async_computation.1 | async-start | bytes 655360 | tf_op jit(solution)/shard_map/all_to_all | solution.py:13
  728.5 3.1 copy-start.12
  732.0 345.0 %copy-start.11 = (bf16[1280,64]{0,1:T(8,128)(2,1)S(1)}, bf16[1280,64]{0,1:T(8,128)(2,1)}, u32[]{:S(2)}) copy-start(bf16[1280,64]{0,1:T(8,128)(2,1)} %param.6) | copy-start | bytes 491524
where the time goes:
time: 1080 us
  blocking collectives  850 us (79%)
  waiting for transfers between devices  134 us (12%)
  starting transfers between devices  56.4 us (5%)
  matrix products  20.5 us (2%)
  local copies, waits for them, and re-layouts  16.9 us (2%)
    psum x1, blocking collectives, bring_home(): summed = lax.psum(partial_value, 'rep').astype(jnp.bfloat16)  506 us
    psum x1, blocking collectives, on_device(): proj_grad = lax.psum(local_proj, 'exp').astype(jnp.bfloat16)  344 us
    all_to_all x2, waiting for transfers between devices, bring_home(): lax.all_to_all(summed, 'exp', split_axis=0, concat_axis=1, tiled=True)  65.3 us
    all_to_all x1, waiting for transfers between devices, on_device(): lax.all_to_all(slot_rows, 'exp', split_axis=1, concat_axis=0, tiled=True)  35.4 us
    all_to_all x1, waiting for transfers between devices, on_device(): lax.all_to_all(expert_grad, 'exp', split_axis=1, concat_axis=0, tiled=True)  33.7 us
    all_to_all x1, starting transfers between devices, on_device(): lax.all_to_all(slot_rows, 'exp', split_axis=1, concat_axis=0, tiled=True)  26.2 us
  transfers between devices with their start and end apart: 4, of which 4 were waited for; matrix products, arithmetic and copies ran while one was open for 1% of the time, Pallas kernels for 0%

commit v1 on v0

v1 whole, which is shorter than its diff:
```python
import jax
import jax.numpy as jnp
from jax import lax
from jax.sharding import Mesh, PartitionSpec as P

ALL = ("y", "zh", "x", "zq", "zr", "c")
PLANE = ("y", "x")
PLANE_CORES = ("y", "x", "c")
EXP = ("zq", "zr", "c")
REP = ("y", "zh", "x")
BF = jnp.bfloat16
F32 = jnp.float32


def signed(r):
    return r if r <= 8 else r - 16


def shifted(value, sign, extra=0):
    pairs = []
    for y in range(4):
        for x in range(4):
            for z in range(32):
                for c in range(2):
                    to = (z + sign * signed(4 * y + x) * (1 - 2 * c) + extra) % 32
                    source = (((y * 2 + z // 16) * 4 + x) * 16 + z % 16) * 2 + c
                    target = (((y * 2 + to // 16) * 4 + x) * 16 + to % 16) * 2 + c
                    pairs.append((source, target))
    return lax.ppermute(value, ALL, pairs)


def smooth(values):
    return jax.nn.gelu(values, approximate=True)


def picked(index, rows):
    choose = (index[:, None] == jnp.arange(rows.shape[0])[None, :]).astype(BF)
    return jnp.dot(choose, rows, preferred_element_type=F32).astype(BF)


def spread(rows):
    out = jnp.broadcast_to(rows[None], (16,) + rows.shape).reshape((32,) + rows.shape[1:])
    return lax.all_to_all(out, PLANE_CORES, 0, 0, tiled=True)


def gathered(value, axes, size):
    out = jnp.broadcast_to(value[None], (size,) + value.shape)
    return lax.all_to_all(out, axes, 0, 0, tiled=True)


def on_device(tokens, slot_proj, in_weight, out_weight, out_grad):
    width = tokens.shape[2]
    column = lax.axis_index("y") * 4 + lax.axis_index("x")
    core = lax.axis_index("c")
    z_lo = lax.axis_index("zq") * 4 + lax.axis_index("zr")
    mirror = 1 - 2 * core
    logits = jnp.einsum("itd,de->ite", tokens, slot_proj, preferred_element_type=F32)
    dispatch = jax.nn.softmax(logits, axis=1)
    combine = jax.nn.softmax(logits, axis=2)
    dispatch_b = dispatch.astype(BF)
    combine_b = combine.astype(BF)
    slot_rows = jnp.einsum("ite,itd->ied", dispatch_b, tokens, preferred_element_type=F32).astype(BF)
    expert_grad = jnp.einsum("ite,itd->ied", combine_b, out_grad, preferred_element_type=F32).astype(BF)
    both = jnp.concatenate([slot_rows.reshape(128, width), expert_grad.reshape(128, width)])
    row = jnp.arange(16)
    target = (z_lo + mirror * column) % 16
    wanted = (row // 4) % 2 * 128 + row % 2 * 64 + 4 * target + row // 8 * 2 + (row // 2) % 2
    sent = shifted(picked(wanted, both), 1)
    got = spread(sent.reshape(2, 8, width)).reshape(256, width)
    row = jnp.arange(256)
    order = (row // 2) % 32 * 8 + row // 64 * 2 + row % 2
    kinds = picked(order, got).reshape(2, 2, 64, width)
    got_slots, got_grads = kinds[0], kinds[1]
    pre_act = jnp.einsum("erd,edf->erf", got_slots, in_weight, preferred_element_type=F32)
    activated, pullback = jax.vjp(smooth, pre_act)
    hidden = activated.astype(BF)
    out_part = jnp.einsum("erf,efd->erd", hidden, out_weight, preferred_element_type=F32).astype(BF)
    hidden_grad = jnp.einsum("erd,efd->erf", got_grads, out_weight, preferred_element_type=F32)
    pre_grad = pullback(hidden_grad)[0].astype(BF)
    slot_part = jnp.einsum("erf,edf->erd", pre_grad, in_weight, preferred_element_type=F32).astype(BF)
    parts = jnp.concatenate([out_part.reshape(128, width), slot_part.reshape(128, width)])
    to, core_of = row // 16, (row // 8) % 2
    source = (mirror * (1 - 2 * core_of) * to) % 16
    order = (row // 2) % 4 * 64 + source * 4 + core_of * 2 + row % 2
    scattered = lax.all_to_all(picked(order, parts).reshape(16, 16, width), PLANE, 0, 0, tiled=True)
    summed = jnp.sum(scattered.astype(F32), axis=0).astype(BF)
    near, far = shifted(summed, -1), shifted(summed, -1, 16)
    out_weight_grad = jnp.einsum("erf,erd->efd", hidden, got_grads, preferred_element_type=F32).astype(BF)
    in_weight_grad = jnp.einsum("erd,erf->edf", got_slots, pre_grad, preferred_element_type=F32).astype(BF)
    home = (near.astype(F32) + far.astype(F32)).astype(BF)
    back = spread(home.reshape(2, 8, width)).reshape(256, width)
    expert = row % 64
    core_of = (expert // 2) % 2
    source = ((1 - 2 * core_of) * (expert // 4 - z_lo)) % 16
    order = source * 16 + core_of * 8 + row // 128 * 4 + expert % 2 * 2 + (row // 64) % 2
    results = picked(order, back).reshape(2, 2, 64, width)
    expert_out, slot_grad = results[0], results[1]
    combine_grad = jnp.einsum("itd,ied->ite", out_grad, expert_out, preferred_element_type=F32)
    dispatch_grad = jnp.einsum("itd,ied->ite", tokens, slot_grad, preferred_element_type=F32)
    from_dispatch = dispatch * (dispatch_grad - jnp.sum(dispatch * dispatch_grad, axis=1, keepdims=True))
    from_combine = combine * (combine_grad - jnp.sum(combine * combine_grad, axis=2, keepdims=True))
    logit_grad = (from_dispatch + from_combine).astype(BF)
    local_proj = jnp.einsum("itd,ite->de", tokens, logit_grad, preferred_element_type=F32)
    share = width // 16
    mine = lax.dynamic_slice_in_dim(local_proj, column * share, share, 0).astype(BF)
    mine = jnp.sum(gathered(mine, ("zr", "c"), 8).astype(F32), axis=0).astype(BF)
    mine = jnp.sum(gathered(mine, "zq", 4).astype(F32), axis=0).astype(BF)
    proj_grad = gathered(mine, PLANE, 16).reshape(width, 64)
    mixed = jnp.einsum("ite,ied->itd", combine_b, expert_out, preferred_element_type=F32).astype(BF)
    token_grad = (
        jnp.einsum("ite,ied->itd", dispatch_b, slot_grad, preferred_element_type=F32)
        + jnp.einsum("ite,de->itd", logit_grad, slot_proj, preferred_element_type=F32)
    ).astype(BF)
    return (mixed, token_grad, proj_grad, in_weight_grad, out_weight_grad)


def solution(mesh):
    fine = Mesh(mesh.devices.reshape(4, 2, 4, 4, 4, 2), ALL)
    images, first, second = P(EXP, None, None), P(EXP, None, REP), P(EXP, REP, None)
    return jax.shard_map(
        on_device,
        mesh=fine,
        in_specs=(images, P(), first, second, images),
        out_specs=(images, images, P(), first, second),
        check_vma=False,
    )
```

time: 1080 us -> 181 us (0.17)
  blocking collectives: 850 us -> 16.6 us
  waiting for transfers between devices: 134 us -> 47.5 us
  starting transfers between devices: 56.4 us -> 82.8 us
    psum x2 -> x0, blocking collectives: 850 us -> none  [the longest x1 506 us: bring_home(): summed = lax.psum(partial_value, 'rep').astype(jnp.bfloat16)]
    all_to_all x4 -> x5, waiting for transfers between devices: 134 us -> 40.3 us  [the longest x2 21.7 us: spread(): return lax.all_to_all(out, PLANE_CORES, 0, 0, tiled=True)]
    ppermute x0 -> x3, starting transfers between devices: none -> 37.8 us  [shifted(): return lax.ppermute(value, ALL, pairs)]
    all_to_all x0 -> x1, blocking collectives: none -> 16.6 us  [on_device(): lax.all_to_all(picked(order, parts).reshape(16, 16, width), PLANE, 0, 0,...]
    all_to_all x4 -> x5, starting transfers between devices: 56.4 us -> 45 us  [the longest x2 22.6 us: spread(): return lax.all_to_all(out, PLANE_CORES, 0, 0, tiled=True)]
  transfers between devices with their start and end apart: 4 -> 8, of which waited for: 4 -> 7; matrix products, arithmetic and copies ran while one was open for 1% -> 7% of each run, Pallas kernels for 0% -> 0%
where the time goes in v1:
time: 181 us; the launch traced here: 178 us
  starting transfers between devices  82.8 us (46%)
  waiting for transfers between devices  47.5 us (26%)
  matrix products  20.3 us (11%)
  blocking collectives  16.6 us (9%)
  local copies, waits for them, and re-layouts  7.83 us (4%)
  other arithmetic  2.07 us (1%)
    ppermute x3, starting transfers between devices, shifted(): return lax.ppermute(value, ALL, pairs)  37.8 us
    all_to_all x2, starting transfers between devices, spread(): return lax.all_to_all(out, PLANE_CORES, 0, 0, tiled=True)  22.6 us
    all_to_all x3, starting transfers between devices, gathered(): return lax.all_to_all(out, axes, 0, 0, tiled=True)  22.4 us
    all_to_all x2, waiting for transfers between devices, spread(): return lax.all_to_all(out, PLANE_CORES, 0, 0, tiled=True)  21.7 us
    all_to_all x3, waiting for transfers between devices, gathered(): return lax.all_to_all(out, axes, 0, 0, tiled=True)  18.6 us
    all_to_all x1, blocking collectives, on_device(): lax.all_to_all(picked(order, parts).reshape(16, 16, width), PLANE, 0, 0,...  16.6 us
    ppermute x3, waiting for transfers between devices, shifted(): return lax.ppermute(value, ALL, pairs)  7.11 us
  transfers between devices with their start and end apart: 8, of which 7 were waited for; matrix products, arithmetic and copies ran while one was open for 7% of the time, Pallas kernels for 0%

profile of v1, /device:TPU:24, one launch (start us, length us, event | category | flops | bytes accessed | tf_op | source)
XLA Modules:
  0.0 178.1 jit_solution(5623159964459801498)
XLA Ops:
  0.6 0.0 copy-start
  0.7 1.3 copy-done
  2.0 1.4 fusion.28
  3.4 0.0 copy-start.5
  3.4 0.0 copy-start.1
  3.4 0.7 fusion.86
  4.1 0.8 fusion.87
  4.9 0.4 convolution_convert_fusion.9
  5.3 0.0 copy-done.1
  5.3 0.4 convolution_convert_fusion.8
  5.6 0.0 copy-done.5
  5.6 0.2 convolution_convert_fusion.10
  5.9 20.0 %collective-permute-start = (bf16[16,1280]{1,0:T(8,128)(2,1)S(1)}, bf16[16,1280]{1,0:T(8,128)(2,1)S(1)}, u32[]{:S(2)}, u32[]{:S(2)}) collective-permute-start(bf16[16,1280]{1,0:T(8,128)(2,1)S(1)} %convolution_convert_fusion.10), channel_id=1, source_target_pairs={{0,0},{1,1},{2,2},{3,3},{4,4},{5,5},{6,6},{7,7},{8,8},{9,9},{10,10... | collective-permute-start | bytes 122888 | tf_op jit(solution)/shard_map/ppermute | solution.py:29
  25.9 1.7 collective-permute-done
  27.5 0.9 broadcast_in_dim.15
  28.4 10.4 %all-to-all-start = ((bf16[32,8,1280]{2,1,0:T(8,128)(2,1)}), bf16[32,8,1280]{2,1,0:T(8,128)(2,1)}, u32[]{:S(2)}, u32[]{:S(2)}) async-start(bf16[32,8,1280]{2,1,0:T(8,128)(2,1)} %bitcast.4), calls=%async_computation | async-start | bytes 1310720 | tf_op jit(solution)/shard_map/all_to_all | solution.py:43
  38.9 0.0 copy-start.2
  38.9 10.9 %all-to-all-done = bf16[32,8,1280]{2,1,0:T(8,128)(2,1)} async-done(((bf16[32,8,1280]{2,1,0:T(8,128)(2,1)}), bf16[32,8,1280]{2,1,0:T(8,128)(2,1)}, u32[]{:S(2)}, u32[]{:S(2)}) %all-to-all-start) | async-done | bytes 655392 | tf_op jit(solution)/shard_map/all_to_all | solution.py:43
  49.7 1.5 convolution_convert_fusion.5
  51.2 0.0 copy-start.8
  51.3 0.0 copy-start.3
  51.3 0.0 copy-start.6
  51.3 0.4 fusion.88
  51.7 0.9 copy-done.8
  52.6 0.5 fusion.36
  53.1 0.3 convolution_convert_fusion.7
  53.4 0.3 convolution_convert_fusion.6
  53.6 0.1 copy-done.10
  53.7 0.4 convolution_convert_fusion.4
  54.1 16.6 %all_to_all.30 = bf16[16,16,1280]{2,1,0:T(8,128)(2,1)S(1)} all-to-all(bf16[16,16,1280]{2,1,0:T(8,128)(2,1)S(1)} %bitcast.70), channel_id=1, replica_groups=mesh['y'=4,'zh'=2,'x'=4,'zq'=4,'zr'=4,'c'=2] {'y','x'}, dimensions={0} | all-to-all | bytes 1310720 | tf_op jit(solution)/shard_map/all_to_all | solution.py:85
  70.8 0.1 reduce_sum.74
  70.9 3.4 %collective-permute-start.1 = (bf16[16,1280]{1,0:T(8,128)(2,1)S(1)}, bf16[16,1280]{1,0:T(8,128)(2,1)S(1)}, u32[]{:S(2)}, u32[]{:S(2)}) collective-permute-start(bf16[16,1280]{1,0:T(8,128)(2,1)S(1)} %reduce_sum.74), channel_id=1, source_target_pairs={{0,0},{1,1},{2,2},{3,3},{4,4},{5,5},{6,6},{7,7},{8,8},{9,9},{10,10... | collective-permute-start | bytes 122888 | tf_op jit(solution)/shard_map/ppermute | solution.py:29
  74.3 14.4 %collective-permute-start.2 = (bf16[16,1280]{1,0:T(8,128)(2,1)S(1)}, bf16[16,1280]{1,0:T(8,128)(2,1)S(1)}, u32[]{:S(2)}, u32[]{:S(2)}) collective-permute-start(bf16[16,1280]{1,0:T(8,128)(2,1)S(1)} %reduce_sum.74), channel_id=1, source_target_pairs={{0,128},{1,129},{2,130},{3,131},{4,132},{5,133},{6,134},{7,135},{8... | collective-permute-start | bytes 122888 | tf_op jit(solution)/shard_map/ppermute | solution.py:29
  88.6 0.0 collective-permute-done.1
  88.6 5.5 %collective-permute-done.2 = bf16[16,1280]{1,0:T(8,128)(2,1)S(1)} collective-permute-done((bf16[16,1280]{1,0:T(8,128)(2,1)S(1)}, bf16[16,1280]{1,0:T(8,128)(2,1)S(1)}, u32[]{:S(2)}, u32[]{:S(2)}) %collective-permute-start.2) | collective-permute-done | bytes 40992 | tf_op jit(solution)/shard_map/ppermute | solution.py:29
  94.1 0.9 broadcast_in_dim.17
  95.0 12.2 %all-to-all-start.2 = ((bf16[32,8,1280]{2,1,0:T(8,128)(2,1)}), bf16[32,8,1280]{2,1,0:T(8,128)(2,1)S(1)}, u32[]{:S(2)}, u32[]{:S(2)}) async-start(bf16[32,8,1280]{2,1,0:T(8,128)(2,1)} %bitcast.67), calls=%async_computation.2 | async-start | bytes 1310720 | tf_op jit(solution)/shard_map/all_to_all | solution.py:43
  107.3 10.8 %all-to-all-done.2 = bf16[32,8,1280]{2,1,0:T(8,128)(2,1)S(1)} async-done(((bf16[32,8,1280]{2,1,0:T(8,128)(2,1)}), bf16[32,8,1280]{2,1,0:T(8,128)(2,1)S(1)}, u32[]{:S(2)}, u32[]{:S(2)}) %all-to-all-start.2) | async-done | bytes 655392 | tf_op jit(solution)/shard_map/all_to_all | solution.py:43
  118.1 0.4 convolution_convert_fusion.3
  118.5 0.5 convolution_bitcast_fusion.2
  119.0 0.0 copy-start.12
  119.1 0.5 convolution_bitcast_fusion.1
  119.6 0.4 copy-done.12
  120.0 0.4 fusion.13
  120.4 0.0 copy-start.4
  120.4 1.4 convolution_bitcast_fusion
  121.8 0.1 fusion.47
  121.8 0.7 broadcast_in_dim.18
  122.5 3.4 %all-to-all-start.3 = ((bf16[8,80,64]{1,2,0:T(8,128)(2,1)}), bf16[8,80,64]{1,2,0:T(8,128)(2,1)S(1)}, u32[]{:S(2)}, u32[]{:S(2)}) async-start(bf16[8,80,64]{1,2,0:T(8,128)(2,1)} %broadcast_in_dim.18), calls=%async_computation.3 | async-start | bytes 262144 | tf_op jit(solution)/shard_map/all_to_all | solution.py:48
  125.9 0.0 copy-done.7
  125.9 1.3 convolution_convert_fusion.2
  127.2 1.3 convolution_convert_fusion.1
  128.6 3.2 %fusion.42 = f32[2,256,1280]{2,1,0:T(8,128)} fusion(bf16[2,64,1280]{2,1,0:T(8,128)(2,1)S(1)} %bitcast.66, f32[2,64]{1,0:T(2,128)S(1)} %get-tuple-element.11, f32[2,256,64]{1,2,0:T(8,128)} %copy-done.5), kind=kOutput, calls=%fused_computation.67 | convolution fusion | flops 83984768 | bytes 3080704 | tf_op jit(solution)/shard_map/ite,ied->itd/dot_general | solution.py:111
  131.7 0.9 all-to-all-done.3
  132.7 0.6 broadcast_in_dim.19
  133.3 13.1 %all-to-all-start.4 = ((bf16[4,80,64]{1,2,0:T(8,128)(2,1)}), bf16[4,80,64]{1,2,0:T(8,128)(2,1)S(1)}, u32[]{:S(2)}, u32[]{:S(2)}) async-start(bf16[4,80,64]{1,2,0:T(8,128)(2,1)} %broadcast_in_dim.19), calls=%async_computation.4 | async-start | bytes 131072 | tf_op jit(solution)/shard_map/all_to_all | solution.py:48
  146.4 3.5 %fusion.4 = bf16[2,256,1280]{2,1,0:T(8,128)(2,1)} fusion(f32[2,256,1280]{2,1,0:T(8,128)} %fusion.42, f32[2,256,64]{1,2,0:T(8,128)S(1)} %fusion.13, f32[2,256,64]{1,2,0:T(8,128)S(1)} %convolution_bitcast_fusion.1, bf16[1280,64]{0,1:T(8,128)(2,1)S(1)} %copy-done.9, f32[2,256,64]{1,2,0:T(8,128)} %get-tuple-element.10, f32[2,256]{1,0:T(2,128)S(1)} %get-tuple-element.9), kind=kOutput, calls=%fused_computation.5 | convolution fusion | flops 85426752 | bytes 4491264 | tf_op jit(solution)/shard_map/ite,de->itd/dot_general | solution.py:112
  149.9 14.0 %all-to-all-done.4 = bf16[4,80,64]{1,2,0:T(8,128)(2,1)S(1)} async-done(((bf16[4,80,64]{1,2,0:T(8,128)(2,1)}), bf16[4,80,64]{1,2,0:T(8,128)(2,1)S(1)}, u32[]{:S(2)}, u32[]{:S(2)}) %all-to-all-start.4) | async-done | bytes 40992 | tf_op jit(solution)/shard_map/all_to_all | solution.py:48
  163.9 0.7 broadcast_in_dim.20
  164.7 5.9 %all-to-all-start.5 = ((bf16[16,80,64]{1,2,0:T(8,128)(2,1)}), bf16[16,80,64]{1,2,0:T(8,128)(2,1)S(1)}, u32[]{:S(2)}, u32[]{:S(2)}) async-start(bf16[16,80,64]{1,2,0:T(8,128)(2,1)} %broadcast_in_dim.20), calls=%async_computation.5 | async-start | bytes 524288 | tf_op jit(solution)/shard_map/all_to_all | solution.py:48
  170.6 2.6 %convolution_convert_fusion = bf16[2,256,1280]{2,1,0:T(8,128)(2,1)} fusion(bf16[2,64,1280]{2,1,0:T(8,128)(2,1)S(1)} %bitcast.64, f32[2,256]{1,0:T(2,128)S(1)} %get-tuple-element.9, f32[2,256,64]{1,2,0:T(8,128)} %copy-done.5), kind=kOutput, calls=%fused_computation.6 | convolution fusion | flops 84640320 | bytes 1771520 | tf_op jit(solution)/shard_map/ite,ied->itd/dot_general | solution.py:109
  173.2 3.8 %all-to-all-done.5 = bf16[16,80,64]{1,2,0:T(8,128)(2,1)S(1)} async-done(((bf16[16,80,64]{1,2,0:T(8,128)(2,1)}), bf16[16,80,64]{1,2,0:T(8,128)(2,1)S(1)}, u32[]{:S(2)}, u32[]{:S(2)}) %all-to-all-start.5) | async-done | bytes 163872 | tf_op jit(solution)/shard_map/all_to_all | solution.py:48
  177.0 0.2 copy.11
  177.2 0.9 reshape.338
  (19 shorter events, 0.2 us)
Async XLA Ops:
  0.6 1.3 copy-start
  3.4 2.2 %copy-start.5 = (f32[2,256,64]{1,2,0:T(8,128)}, f32[2,256,64]{1,2,0:T(8,128)S(1)}, u32[]{:S(2)}) copy-start(f32[2,256,64]{1,2,0:T(8,128)S(1)} %fusion.28) | copy-start | bytes 393220
  3.4 1.9 %copy-start.1 = (bf16[2,256,1280]{2,1,0:T(8,128)(2,1)S(1)}, bf16[2,256,1280]{2,1,0:T(8,128)(2,1)}, u32[]{:S(2)}) copy-start(bf16[2,256,1280]{2,1,0:T(8,128)(2,1)} %param.9) | copy-start | bytes 3932164
  5.9 21.7 %collective-permute-start = (bf16[16,1280]{1,0:T(8,128)(2,1)S(1)}, bf16[16,1280]{1,0:T(8,128)(2,1)S(1)}, u32[]{:S(2)}, u32[]{:S(2)}) collective-permute-start(bf16[16,1280]{1,0:T(8,128)(2,1)S(1)} %convolution_convert_fusion.10), channel_id=1, source_target_pairs={{0,0},{1,1},{2,2},{3,3},{4,4},{5,5},{6,6},{7,7},{8,8},{9,9},{10,10... | collective-permute-start | bytes 122888 | tf_op jit(solution)/shard_map/ppermute | solution.py:29
  28.4 21.3 %all-to-all-start = ((bf16[32,8,1280]{2,1,0:T(8,128)(2,1)}), bf16[32,8,1280]{2,1,0:T(8,128)(2,1)}, u32[]{:S(2)}, u32[]{:S(2)}) async-start(bf16[32,8,1280]{2,1,0:T(8,128)(2,1)} %bitcast.4), calls=%async_computation | async-start | bytes 1310720 | tf_op jit(solution)/shard_map/all_to_all | solution.py:43
  38.9 12.5 %copy-start.2 = (bf16[2,160,1280]{2,1,0:T(8,128)(2,1)S(1)}, bf16[2,160,1280]{2,1,0:T(8,128)(2,1)}, u32[]{:S(2)}) copy-start(bf16[2,160,1280]{2,1,0:T(8,128)(2,1)} %param.8) | copy-start | bytes 2457604
  51.2 1.4 copy-start.8
  51.3 1.8 %copy-start.3 = (bf16[128,1280]{1,0:T(8,128)(2,1)}, bf16[128,1280]{1,0:T(8,128)(2,1)S(1)}, u32[]{:S(2)}) copy-start(bf16[128,1280]{1,0:T(8,128)(2,1)S(1)} %get-tuple-element.7) | copy-start | bytes 983044
  51.3 1.8 %copy-start.6 = (bf16[128,1280]{1,0:T(8,128)(2,1)}, bf16[128,1280]{1,0:T(8,128)(2,1)S(1)}, u32[]{:S(2)}) copy-start(bf16[128,1280]{1,0:T(8,128)(2,1)S(1)} %get-tuple-element.8) | copy-start | bytes 983044
  53.1 0.6 copy-start.10
  70.9 17.8 %collective-permute-start.1 = (bf16[16,1280]{1,0:T(8,128)(2,1)S(1)}, bf16[16,1280]{1,0:T(8,128)(2,1)S(1)}, u32[]{:S(2)}, u32[]{:S(2)}) collective-permute-start(bf16[16,1280]{1,0:T(8,128)(2,1)S(1)} %reduce_sum.74), channel_id=1, source_target_pairs={{0,0},{1,1},{2,2},{3,3},{4,4},{5,5},{6,6},{7,7},{8,8},{9,9},{10,10... | collective-permute-start | bytes 122888 | tf_op jit(solution)/shard_map/ppermute | solution.py:29
  74.3 19.8 %collective-permute-start.2 = (bf16[16,1280]{1,0:T(8,128)(2,1)S(1)}, bf16[16,1280]{1,0:T(8,128)(2,1)S(1)}, u32[]{:S(2)}, u32[]{:S(2)}) collective-permute-start(bf16[16,1280]{1,0:T(8,128)(2,1)S(1)} %reduce_sum.74), channel_id=1, source_target_pairs={{0,128},{1,129},{2,130},{3,131},{4,132},{5,133},{6,134},{7,135},{8... | collective-permute-start | bytes 122888 | tf_op jit(solution)/shard_map/ppermute | solution.py:29
  95.0 23.1 %all-to-all-start.2 = ((bf16[32,8,1280]{2,1,0:T(8,128)(2,1)}), bf16[32,8,1280]{2,1,0:T(8,128)(2,1)S(1)}, u32[]{:S(2)}, u32[]{:S(2)}) async-start(bf16[32,8,1280]{2,1,0:T(8,128)(2,1)} %bitcast.67), calls=%async_computation.2 | async-start | bytes 1310720 | tf_op jit(solution)/shard_map/all_to_all | solution.py:43
  119.0 0.9 copy-start.12
  120.0 5.9 %copy-start.7 = (bf16[128,1280]{1,0:T(8,128)(2,1)S(1)}, bf16[128,1280]{1,0:T(8,128)(2,1)}, u32[]{:S(2)}) copy-start(bf16[128,1280]{1,0:T(8,128)(2,1)} %copy-done.6) | copy-start | bytes 983044
  120.4 6.9 %copy-start.4 = (bf16[128,1280]{1,0:T(8,128)(2,1)S(1)}, bf16[128,1280]{1,0:T(8,128)(2,1)}, u32[]{:S(2)}) copy-start(bf16[128,1280]{1,0:T(8,128)(2,1)} %copy-done.3) | copy-start | bytes 983044
  120.4 6.9 %copy-start.11 = (f32[2,64,160]{2,1,0:T(8,128)S(1)}, f32[2,64,160]{2,1,0:T(8,128)}, u32[]{:S(2)}) copy-start(f32[2,64,160]{2,1,0:T(8,128)} %copy-done.10) | copy-start | bytes 245764
  122.5 10.1 %all-to-all-start.3 = ((bf16[8,80,64]{1,2,0:T(8,128)(2,1)}), bf16[8,80,64]{1,2,0:T(8,128)(2,1)S(1)}, u32[]{:S(2)}, u32[]{:S(2)}) async-start(bf16[8,80,64]{1,2,0:T(8,128)(2,1)} %broadcast_in_dim.18), calls=%async_computation.3 | async-start | bytes 262144 | tf_op jit(solution)/shard_map/all_to_all | solution.py:48
  128.6 17.9 %copy-start.9 = (bf16[1280,64]{0,1:T(8,128)(2,1)S(1)}, bf16[1280,64]{0,1:T(8,128)(2,1)}, u32[]{:S(2)}) copy-start(bf16[1280,64]{0,1:T(8,128)(2,1)} %param.6) | copy-start | bytes 491524
  133.3 30.6 %all-to-all-start.4 = ((bf16[4,80,64]{1,2,0:T(8,128)(2,1)}), bf16[4,80,64]{1,2,0:T(8,128)(2,1)S(1)}, u32[]{:S(2)}, u32[]{:S(2)}) async-start(bf16[4,80,64]{1,2,0:T(8,128)(2,1)} %broadcast_in_dim.19), calls=%async_computation.4 | async-start | bytes 131072 | tf_op jit(solution)/shard_map/all_to_all | solution.py:48
  164.7 12.3 %all-to-all-start.5 = ((bf16[16,80,64]{1,2,0:T(8,128)(2,1)}), bf16[16,80,64]{1,2,0:T(8,128)(2,1)S(1)}, u32[]{:S(2)}, u32[]{:S(2)}) async-start(bf16[16,80,64]{1,2,0:T(8,128)(2,1)} %broadcast_in_dim.20), calls=%async_computation.5 | async-start | bytes 524288 | tf_op jit(solution)/shard_map/all_to_all | solution.py:48

commit v2 on v1

--- a/solution.py
+++ b/solution.py
@@ -5,7 +5,6 @@
 
 ALL = ("y", "zh", "x", "zq", "zr", "c")
 PLANE = ("y", "x")
-PLANE_CORES = ("y", "x", "c")
 EXP = ("zq", "zr", "c")
 REP = ("y", "zh", "x")
 BF = jnp.bfloat16
@@ -16,17 +15,25 @@
     return r if r <= 8 else r - 16
 
 
-def shifted(value, sign, extra=0):
+def shifted(value, shift):
     pairs = []
     for y in range(4):
         for x in range(4):
             for z in range(32):
                 for c in range(2):
-                    to = (z + sign * signed(4 * y + x) * (1 - 2 * c) + extra) % 32
+                    to = (z + shift(y, x, c)) % 32
                     source = (((y * 2 + z // 16) * 4 + x) * 16 + z % 16) * 2 + c
                     target = (((y * 2 + to // 16) * 4 + x) * 16 + to % 16) * 2 + c
                     pairs.append((source, target))
     return lax.ppermute(value, ALL, pairs)
+
+
+def out_shift(y, x, c):
+    return signed(4 * y + x) * (1 - 2 * c)
+
+
+def swapped(rows):
+    return jnp.concatenate([rows[:1], lax.ppermute(rows[1:], "c", [(0, 1), (1, 0)])])
 
 
 def smooth(values):
@@ -36,11 +43,6 @@
 def picked(index, rows):
     choose = (index[:, None] == jnp.arange(rows.shape[0])[None, :]).astype(BF)
     return jnp.dot(choose, rows, preferred_element_type=F32).astype(BF)
-
-
-def spread(rows):
-    out = jnp.broadcast_to(rows[None], (16,) + rows.shape).reshape((32,) + rows.shape[1:])
-    return lax.all_to_all(out, PLANE_CORES, 0, 0, tiled=True)
 
 
 def gathered(value, axes, size):
@@ -53,7 +55,6 @@
     column = lax.axis_index("y") * 4 + lax.axis_index("x")
     core = lax.axis_index("c")
     z_lo = lax.axis_index("zq") * 4 + lax.axis_index("zr")
-    mirror = 1 - 2 * core
     logits = jnp.einsum("itd,de->ite", tokens, slot_proj, preferred_element_type=F32)
     dispatch = jax.nn.softmax(logits, axis=1)
     combine = jax.nn.softmax(logits, axis=2)
@@ -63,10 +64,12 @@
     expert_grad = jnp.einsum("ite,itd->ied", combine_b, out_grad, preferred_element_type=F32).astype(BF)
     both = jnp.concatenate([slot_rows.reshape(128, width), expert_grad.reshape(128, width)])
     row = jnp.arange(16)
-    target = (z_lo + mirror * column) % 16
-    wanted = (row // 4) % 2 * 128 + row % 2 * 64 + 4 * target + row // 8 * 2 + (row // 2) % 2
-    sent = shifted(picked(wanted, both), 1)
-    got = spread(sent.reshape(2, 8, width)).reshape(256, width)
+    to_core = core ^ (row // 8)
+    target = (z_lo + (1 - 2 * to_core) * column) % 16
+    wanted = (row // 4) % 2 * 128 + row % 2 * 64 + 4 * target + 2 * to_core + (row // 2) % 2
+    held = swapped(picked(wanted, both).reshape(2, 8, width))
+    sent = shifted(held.reshape(16, width), out_shift)
+    got = gathered(sent, PLANE, 16).reshape(256, width)
     row = jnp.arange(256)
     order = (row // 2) % 32 * 8 + row // 64 * 2 + row % 2
     kinds = picked(order, got).reshape(2, 2, 64, width)
@@ -79,20 +82,19 @@
     pre_grad = pullback(hidden_grad)[0].astype(BF)
     slot_part = jnp.einsum("erf,edf->erd", pre_grad, in_weight, preferred_element_type=F32).astype(BF)
     parts = jnp.concatenate([out_part.reshape(128, width), slot_part.reshape(128, width)])
-    to, core_of = row // 16, (row // 8) % 2
-    source = (mirror * (1 - 2 * core_of) * to) % 16
-    order = (row // 2) % 4 * 64 + source * 4 + core_of * 2 + row % 2
+    order = (row // 2) % 4 * 64 + row // 16 * 4 + (row // 8) % 2 * 2 + row % 2
     scattered = lax.all_to_all(picked(order, parts).reshape(16, 16, width), PLANE, 0, 0, tiled=True)
     summed = jnp.sum(scattered.astype(F32), axis=0).astype(BF)
-    near, far = shifted(summed, -1), shifted(summed, -1, 16)
+    far = shifted(summed, lambda y, x, c: 16 - out_shift(y, x, c))
+    near = shifted(summed, lambda y, x, c: -out_shift(y, x, c))
     out_weight_grad = jnp.einsum("erf,erd->efd", hidden, got_grads, preferred_element_type=F32).astype(BF)
     in_weight_grad = jnp.einsum("erd,erf->edf", got_slots, pre_grad, preferred_element_type=F32).astype(BF)
     home = (near.astype(F32) + far.astype(F32)).astype(BF)
-    back = spread(home.reshape(2, 8, width)).reshape(256, width)
+    back = gathered(swapped(home.reshape(2, 8, width)).reshape(16, width), PLANE, 16).reshape(256, width)
     expert = row % 64
     core_of = (expert // 2) % 2
     source = ((1 - 2 * core_of) * (expert // 4 - z_lo)) % 16
-    order = source * 16 + core_of * 8 + row // 128 * 4 + expert % 2 * 2 + (row // 64) % 2
+    order = source * 16 + (core_of ^ core) * 8 + row // 128 * 4 + expert % 2 * 2 + (row // 64) % 2
     results = picked(order, back).reshape(2, 2, 64, width)
     expert_out, slot_grad = results[0], results[1]
     combine_grad = jnp.einsum("itd,ied->ite", out_grad, expert_out, preferred_element_type=F32)
@@ -100,12 +102,17 @@
     from_dispatch = dispatch * (dispatch_grad - jnp.sum(dispatch * dispatch_grad, axis=1, keepdims=True))
     from_combine = combine * (combine_grad - jnp.sum(combine * combine_grad, axis=2, keepdims=True))
     logit_grad = (from_dispatch + from_combine).astype(BF)
-    local_proj = jnp.einsum("itd,ite->de", tokens, logit_grad, preferred_element_type=F32)
-    share = width // 16
-    mine = lax.dynamic_slice_in_dim(local_proj, column * share, share, 0).astype(BF)
+    half = width // 2
+    local_proj = jnp.concatenate(
+        [jnp.einsum("itd,ite->de", part, logit_grad, preferred_element_type=F32)
+         for part in (tokens[:, :, :half], tokens[:, :, half:])], axis=1)
+    share = half // 4
+    mine = lax.dynamic_slice_in_dim(local_proj, lax.axis_index("y") * share, share, 0).astype(BF)
     mine = jnp.sum(gathered(mine, ("zr", "c"), 8).astype(F32), axis=0).astype(BF)
-    mine = jnp.sum(gathered(mine, "zq", 4).astype(F32), axis=0).astype(BF)
-    proj_grad = gathered(mine, PLANE, 16).reshape(width, 64)
+    mine = shifted(mine, lambda y, x, c: 4 * (0, 1, 2, -1)[x])
+    shares = gathered(mine, PLANE, 16).reshape(4, 4, share, 128)
+    sums = jnp.sum(shares.astype(F32), axis=1).astype(BF).reshape(half, 128)
+    proj_grad = jnp.concatenate([sums[:, :64], sums[:, 64:]], axis=0)
     mixed = jnp.einsum("ite,ied->itd", combine_b, expert_out, preferred_element_type=F32).astype(BF)
     token_grad = (
         jnp.einsum("ite,ied->itd", dispatch_b, slot_grad, preferred_element_type=F32)

time: 181 us -> 178 us (0.983)
  waiting for transfers between devices: 47.5 us -> 42.7 us
  other arithmetic: 2.07 us -> 5.06 us
  blocking collectives: 16.6 us -> 14.2 us
  local copies, waits for them, and re-layouts: 7.83 us -> 5.43 us
  matrix products: 20.3 us -> 22.7 us
  starting transfers between devices: 82.8 us -> 84.9 us
    all_to_all x2 -> x0, starting transfers between devices: 22.6 us -> none  [spread(): return lax.all_to_all(out, PLANE_CORES, 0, 0, tiled=True)]
    all_to_all x2 -> x0, waiting for transfers between devices: 21.7 us -> none  [spread(): return lax.all_to_all(out, PLANE_CORES, 0, 0, tiled=True)]
    all_to_all x3 -> x4, starting transfers between devices: 22.4 us -> 40.6 us  [gathered(): return lax.all_to_all(out, axes, 0, 0, tiled=True)]
    all_to_all x3 -> x4, waiting for transfers between devices: 18.6 us -> 32.4 us  [gathered(): return lax.all_to_all(out, axes, 0, 0, tiled=True)]
    ppermute x0 -> x2, starting transfers between devices: none -> 3.85 us  [swapped(): lax.ppermute(rows[1:], 'c', [(0, 1), (1, 0)])]
    dot_general x1 -> x2, matrix products: 1.37 us -> 4.45 us  [on_device(): jnp.einsum('itd,ite->de', part, logit_grad, preferred_element_type=F32)]
    ppermute x3 -> x4, starting transfers between devices: 37.8 us -> 40.5 us  [shifted(): return lax.ppermute(value, ALL, pairs)]
    all_to_all x1, blocking collectives: 16.6 us -> 14.2 us  [on_device(): lax.all_to_all(picked(order, parts).reshape(16, 16, width), PLANE, 0, 0,...]
  transfers between devices with their start and end apart: 8 -> 10, of which waited for: 7 -> 8; matrix products, arithmetic and copies ran while one was open for 7% -> 6% of each run, Pallas kernels for 0% -> 0%
where the time goes in v2:
time: 178 us; the launch traced here: 176 us
  starting transfers between devices  84.9 us (48%)
  waiting for transfers between devices  42.7 us (24%)
  matrix products  22.7 us (13%)
  blocking collectives  14.2 us (8%)
  local copies, waits for them, and re-layouts  5.43 us (3%)
  other arithmetic  5.06 us (3%)
    all_to_all x4, starting transfers between devices, gathered(): return lax.all_to_all(out, axes, 0, 0, tiled=True)  40.6 us
    ppermute x4, starting transfers between devices, shifted(): return lax.ppermute(value, ALL, pairs)  40.5 us
    all_to_all x4, waiting for transfers between devices, gathered(): return lax.all_to_all(out, axes, 0, 0, tiled=True)  32.4 us
    all_to_all x1, blocking collectives, on_device(): lax.all_to_all(picked(order, parts).reshape(16, 16, width), PLANE, 0, 0,...  14.2 us
    ppermute x4, waiting for transfers between devices, shifted(): return lax.ppermute(value, ALL, pairs)  8.01 us
    dot_general x2, matrix products, on_device(): jnp.einsum('itd,ite->de', part, logit_grad, preferred_element_type=F32)  4.45 us
    ppermute x2, starting transfers between devices, swapped(): lax.ppermute(rows[1:], 'c', [(0, 1), (1, 0)])  3.85 us
    dot_general x1, matrix products, on_device(): jnp.einsum('ite,de->itd', logit_grad, slot_proj, preferred_element_type=F32)  3.63 us
  transfers between devices with their start and end apart: 10, of which 8 were waited for; matrix products, arithmetic and copies ran while one was open for 6% of the time, Pallas kernels for 0%

profile of v2, /device:TPU:24, one launch (start us, length us, event | category | flops | bytes accessed | tf_op | source)
XLA Modules:
  0.0 176.1 jit_solution(16098948506398235455)
XLA Ops:
  0.6 0.0 copy-start
  0.6 0.0 copy-start.1
  0.7 2.0 %fusion.30 = f32[2,256,64]{1,2,0:T(8,128)S(1)} fusion(bf16[2,256,1280]{2,1,0:T(8,128)(2,1)} %param.5, bf16[1280,64]{0,1:T(8,128)(2,1)} %param.6), kind=kOutput, calls=%fused_computation.53 | convolution fusion | flops 83886080 | bytes 1605632 | tf_op jit(solution)/shard_map/itd,de->ite/dot_general | solution.py:58
  2.6 0.7 fusion.92
  3.3 0.8 fusion.93
  4.1 0.0 copy-done.1
  4.1 0.4 convolution_convert_fusion.9
  4.5 0.4 convolution_convert_fusion.8
  4.9 0.2 convolution_convert_fusion.10
  5.1 1.9 %collective-permute-start = (bf16[1,8,1280]{2,1,0:T(8,128)(2,1)S(1)}, bf16[1,8,1280]{2,1,0:T(8,128)(2,1)S(1)}, u32[]{:S(2)}, u32[]{:S(2)}) collective-permute-start(bf16[1,8,1280]{2,1,0:T(8,128)(2,1)S(1)} %get-tuple-element.29), channel_id=1, source_target_pairs={{0,1},{1,0},{2,3},{3,2},{4,5},{5,4},{6,7},{7,6},{8,9},{9,8},{10,11... | collective-permute-start | bytes 61448 | tf_op jit(solution)/shard_map/ppermute | solution.py:36
  7.1 1.2 collective-permute-done
  8.2 20.0 %collective-permute-start.1 = (bf16[16,1280]{1,0:T(8,128)(2,1)S(1)}, bf16[16,1280]{1,0:T(8,128)(2,1)S(1)}, u32[]{:S(2)}, u32[]{:S(2)}) collective-permute-start(bf16[16,1280]{1,0:T(8,128)(2,1)S(1)} %maximum_bitcast_fusion), channel_id=1, source_target_pairs={{0,0},{1,1},{2,2},{3,3},{4,4},{5,5},{6,6},{7,7},{8,8},{9,9},{10,10... | collective-permute-start | bytes 122888 | tf_op jit(solution)/shard_map/ppermute | solution.py:28
  28.2 1.7 collective-permute-done.1
  29.9 0.9 broadcast_in_dim.10
  30.8 10.2 %all-to-all-start = ((bf16[16,16,1280]{2,1,0:T(8,128)(2,1)}), bf16[16,16,1280]{2,1,0:T(8,128)(2,1)S(1)}, u32[]{:S(2)}, u32[]{:S(2)}) async-start(bf16[16,16,1280]{2,1,0:T(8,128)(2,1)} %broadcast_in_dim.10), calls=%async_computation | async-start | bytes 1310720 | tf_op jit(solution)/shard_map/all_to_all | solution.py:50
  40.9 9.5 %all-to-all-done = bf16[16,16,1280]{2,1,0:T(8,128)(2,1)S(1)} async-done(((bf16[16,16,1280]{2,1,0:T(8,128)(2,1)}), bf16[16,16,1280]{2,1,0:T(8,128)(2,1)S(1)}, u32[]{:S(2)}, u32[]{:S(2)}) %all-to-all-start) | async-done | bytes 655392 | tf_op jit(solution)/shard_map/all_to_all | solution.py:50
  50.5 0.4 convolution_convert_fusion.5
  50.9 0.0 copy-start.7
  51.0 0.0 copy-start.5
  51.0 0.7 copy-done.2
  51.6 0.4 fusion.94
  52.0 0.2 copy-done.7
  52.2 0.5 fusion.38
  52.7 0.3 convolution_convert_fusion.6
  53.0 0.3 convolution_convert_fusion.7
  53.3 0.4 convolution_convert_fusion.4
  53.7 14.2 %all_to_all.25 = bf16[16,16,1280]{2,1,0:T(8,128)(2,1)} all-to-all(bf16[16,16,1280]{2,1,0:T(8,128)(2,1)S(1)} %bitcast.80), channel_id=1, replica_groups=mesh['y'=4,'zh'=2,'x'=4,'zq'=4,'zr'=4,'c'=2] {'y','x'}, dimensions={0} | all-to-all | bytes 1310720 | tf_op jit(solution)/shard_map/all_to_all | solution.py:86
  67.9 1.2 reduce_sum.74
  69.1 5.2 %collective-permute-start.2 = (bf16[16,1280]{1,0:T(8,128)(2,1)S(1)}, bf16[16,1280]{1,0:T(8,128)(2,1)S(1)}, u32[]{:S(2)}, u32[]{:S(2)}) collective-permute-start(bf16[16,1280]{1,0:T(8,128)(2,1)S(1)} %reduce_sum.74), channel_id=1, source_target_pairs={{0,0},{1,1},{2,2},{3,3},{4,4},{5,5},{6,6},{7,7},{8,8},{9,9},{10,10... | collective-permute-start | bytes 122888 | tf_op jit(solution)/shard_map/ppermute | solution.py:28
  74.3 14.6 %collective-permute-start.3 = (bf16[16,1280]{1,0:T(8,128)(2,1)S(1)}, bf16[16,1280]{1,0:T(8,128)(2,1)S(1)}, u32[]{:S(2)}, u32[]{:S(2)}) collective-permute-start(bf16[16,1280]{1,0:T(8,128)(2,1)S(1)} %reduce_sum.74), channel_id=1, source_target_pairs={{0,128},{1,129},{2,130},{3,131},{4,132},{5,133},{6,134},{7,135},{8... | collective-permute-start | bytes 122888 | tf_op jit(solution)/shard_map/ppermute | solution.py:28
  88.9 0.0 collective-permute-done.2
  88.9 6.3 %collective-permute-done.3 = bf16[16,1280]{1,0:T(8,128)(2,1)S(1)} collective-permute-done((bf16[16,1280]{1,0:T(8,128)(2,1)S(1)}, bf16[16,1280]{1,0:T(8,128)(2,1)S(1)}, u32[]{:S(2)}, u32[]{:S(2)}) %collective-permute-start.3) | collective-permute-done | bytes 40992 | tf_op jit(solution)/shard_map/ppermute | solution.py:28
  95.3 1.9 %collective-permute-start.4 = (bf16[1,8,1280]{2,1,0:T(8,128)(2,1)S(1)}, bf16[1,8,1280]{2,1,0:T(8,128)(2,1)S(1)}, u32[]{:S(2)}, u32[]{:S(2)}) collective-permute-start(bf16[1,8,1280]{2,1,0:T(8,128)(2,1)S(1)} %get-tuple-element.27), channel_id=1, source_target_pairs={{0,1},{1,0},{2,3},{3,2},{4,5},{5,4},{6,7},{7,6},{8,9},{9,8},{10,11... | collective-permute-start | bytes 61448 | tf_op jit(solution)/shard_map/ppermute | solution.py:36
  97.2 1.2 collective-permute-done.4
  98.4 0.9 broadcast_in_dim.12
  99.3 9.4 %all-to-all-start.2 = ((bf16[16,16,1280]{2,1,0:T(8,128)(2,1)}), bf16[16,16,1280]{2,1,0:T(8,128)(2,1)}, u32[]{:S(2)}, u32[]{:S(2)}) async-start(bf16[16,16,1280]{2,1,0:T(8,128)(2,1)} %broadcast_in_dim.12), calls=%async_computation.2 | async-start | bytes 1310720 | tf_op jit(solution)/shard_map/all_to_all | solution.py:50
  108.7 11.1 %all-to-all-done.2 = bf16[16,16,1280]{2,1,0:T(8,128)(2,1)} async-done(((bf16[16,16,1280]{2,1,0:T(8,128)(2,1)}), bf16[16,16,1280]{2,1,0:T(8,128)(2,1)}, u32[]{:S(2)}, u32[]{:S(2)}) %all-to-all-start.2) | async-done | bytes 655392 | tf_op jit(solution)/shard_map/all_to_all | solution.py:50
  119.8 1.5 convolution_convert_fusion.3
  121.3 0.0 copy-start.3
  121.3 0.5 convolution_bitcast_fusion.3
  121.8 0.0 copy-start.11
  121.8 1.2 convolution_bitcast_fusion.2
  123.0 1.2 fusion.13
  124.2 2.2 %convolution_bitcast_fusion = bf16[640,64]{1,0:T(8,128)(2,1)} fusion(f32[2,256,64]{1,2,0:T(8,128)} %fusion.13, f32[2,256,64]{1,2,0:T(8,128)} %convolution_bitcast_fusion.2, bf16[2,256,1280]{2,1,0:T(8,128)(2,1)S(1)} %copy-done.1, f32[2,256,64]{1,2,0:T(8,128)} %get-tuple-element.31, f32[2,256]{1,0:T(2,128)S(1)} %get-tuple-element.30), kind=kOutput, calls=%fused_computation.17 | convolution fusion | flops 42172992 | bytes 1396736 | tf_op jit(solution)/shard_map/itd,ite->de/dot_general | solution.py:107
  126.4 2.2 %convolution_bitcast_fusion.1 = bf16[640,64]{1,0:T(8,128)(2,1)} fusion(f32[2,256,64]{1,2,0:T(8,128)} %fusion.13, f32[2,256,64]{1,2,0:T(8,128)} %convolution_bitcast_fusion.2, bf16[2,256,1280]{2,1,0:T(8,128)(2,1)S(1)} %copy-done.1, f32[2,256,64]{1,2,0:T(8,128)} %get-tuple-element.31, f32[2,256]{1,0:T(2,128)S(1)} %get-tuple-element.30), kind=kOutput, calls=%fused_computation.18 | convolution fusion | flops 42172992 | bytes 1396736 | tf_op jit(solution)/shard_map/itd,ite->de/dot_general | solution.py:107
  128.7 0.9 fusion.44
  129.6 0.8 broadcast_in_dim.13
  130.4 3.4 %all-to-all-start.3 = ((bf16[8,160,128]{2,1,0:T(8,128)(2,1)}), bf16[8,160,128]{2,1,0:T(8,128)(2,1)S(1)}, u32[]{:S(2)}, u32[]{:S(2)}) async-start(bf16[8,160,128]{2,1,0:T(8,128)(2,1)} %broadcast_in_dim.13), calls=%async_computation.3 | async-start | bytes 655360 | tf_op jit(solution)/shard_map/all_to_all | solution.py:50
  133.8 1.3 convolution_convert_fusion.2
  135.1 1.3 convolution_convert_fusion.1
  136.5 8.4 %all-to-all-done.3 = bf16[8,160,128]{2,1,0:T(8,128)(2,1)S(1)} async-done(((bf16[8,160,128]{2,1,0:T(8,128)(2,1)}), bf16[8,160,128]{2,1,0:T(8,128)(2,1)S(1)}, u32[]{:S(2)}, u32[]{:S(2)}) %all-to-all-start.3) | async-done | bytes 327712 | tf_op jit(solution)/shard_map/all_to_all | solution.py:50
  144.9 0.7 collective-permute-start.5
  145.6 1.6 convolution_convert_fusion
  147.2 0.0 collective-permute-done.5
  147.2 0.9 broadcast_in_dim.14
  148.2 17.6 %all-to-all-start.4 = ((bf16[16,160,128]{2,1,0:T(8,128)(2,1)}), bf16[16,160,128]{2,1,0:T(8,128)(2,1)S(1)}, u32[]{:S(2)}, u32[]{:S(2)}) async-start(bf16[16,160,128]{2,1,0:T(8,128)(2,1)} %broadcast_in_dim.14), calls=%async_computation.4 | async-start | bytes 1310720 | tf_op jit(solution)/shard_map/all_to_all | solution.py:50
  165.8 0.0 copy-start.8
  165.8 2.2 %fusion.45 = f32[2,256,1280]{2,1,0:T(8,128)} fusion(bf16[2,64,1280]{2,1,0:T(8,128)(2,1)S(1)} %bitcast.75, f32[2,64]{1,0:T(2,128)S(1)} %get-tuple-element.32, f32[2,256,64]{1,2,0:T(8,128)S(1)} %fusion.30), kind=kOutput, calls=%fused_computation.75 | convolution fusion | flops 83984768 | bytes 3080704 | tf_op jit(solution)/shard_map/ite,ied->itd/dot_general | solution.py:118
  167.9 3.6 %fusion.4 = bf16[2,256,1280]{2,1,0:T(8,128)(2,1)} fusion(f32[2,256,1280]{2,1,0:T(8,128)} %fusion.45, f32[2,256,64]{1,2,0:T(8,128)S(1)} %copy-done.12, f32[2,256,64]{1,2,0:T(8,128)} %convolution_bitcast_fusion.2, bf16[1280,64]{0,1:T(8,128)(2,1)S(1)} %copy-done.8, f32[2,256,64]{1,2,0:T(8,128)} %get-tuple-element.31, f32[2,256]{1,0:T(2,128)S(1)} %get-tuple-element.30), kind=kOutput, calls=%fused_computation.5 | convolution fusion | flops 85426752 | bytes 4491264 | tf_op jit(solution)/shard_map/ite,de->itd/dot_general | solution.py:119
  171.6 3.4 %all-to-all-done.4 = bf16[16,160,128]{2,1,0:T(8,128)(2,1)S(1)} async-done(((bf16[16,160,128]{2,1,0:T(8,128)(2,1)}), bf16[16,160,128]{2,1,0:T(8,128)(2,1)S(1)}, u32[]{:S(2)}, u32[]{:S(2)}) %all-to-all-start.4) | async-done | bytes 655392 | tf_op jit(solution)/shard_map/all_to_all | solution.py:50
  174.9 0.1 bitcast_reduce_fusion
  175.0 0.1 fusion.91
  175.1 0.1 pad_maximum_fusion
  175.2 0.8 copy.17
  (28 shorter events, 0.3 us)
Async XLA Ops:
  0.6 3.9 %copy-start = (bf16[2,256,1280]{2,1,0:T(8,128)(2,1)S(1)}, bf16[2,256,1280]{2,1,0:T(8,128)(2,1)}, u32[]{:S(2)}) copy-start(bf16[2,256,1280]{2,1,0:T(8,128)(2,1)} %param.9) | copy-start | bytes 3932164
  0.6 3.4 %copy-start.1 = (bf16[2,256,1280]{2,1,0:T(8,128)(2,1)S(1)}, bf16[2,256,1280]{2,1,0:T(8,128)(2,1)}, u32[]{:S(2)}) copy-start(bf16[2,256,1280]{2,1,0:T(8,128)(2,1)} %param.5) | copy-start | bytes 3932164
  5.1 3.1 %collective-permute-start = (bf16[1,8,1280]{2,1,0:T(8,128)(2,1)S(1)}, bf16[1,8,1280]{2,1,0:T(8,128)(2,1)S(1)}, u32[]{:S(2)}, u32[]{:S(2)}) collective-permute-start(bf16[1,8,1280]{2,1,0:T(8,128)(2,1)S(1)} %get-tuple-element.29), channel_id=1, source_target_pairs={{0,1},{1,0},{2,3},{3,2},{4,5},{5,4},{6,7},{7,6},{8,9},{9,8},{10,11... | collective-permute-start | bytes 61448 | tf_op jit(solution)/shard_map/ppermute | solution.py:36
  8.2 21.7 %collective-permute-start.1 = (bf16[16,1280]{1,0:T(8,128)(2,1)S(1)}, bf16[16,1280]{1,0:T(8,128)(2,1)S(1)}, u32[]{:S(2)}, u32[]{:S(2)}) collective-permute-start(bf16[16,1280]{1,0:T(8,128)(2,1)S(1)} %maximum_bitcast_fusion), channel_id=1, source_target_pairs={{0,0},{1,1},{2,2},{3,3},{4,4},{5,5},{6,6},{7,7},{8,8},{9,9},{10,10... | collective-permute-start | bytes 122888 | tf_op jit(solution)/shard_map/ppermute | solution.py:28
  30.8 19.7 %all-to-all-start = ((bf16[16,16,1280]{2,1,0:T(8,128)(2,1)}), bf16[16,16,1280]{2,1,0:T(8,128)(2,1)S(1)}, u32[]{:S(2)}, u32[]{:S(2)}) async-start(bf16[16,16,1280]{2,1,0:T(8,128)(2,1)} %broadcast_in_dim.10), calls=%async_computation | async-start | bytes 1310720 | tf_op jit(solution)/shard_map/all_to_all | solution.py:50
  50.5 1.1 copy-start.2
  50.9 1.3 copy-start.7
  51.0 1.7 copy-start.5
  52.7 0.9 copy-start.9
  69.1 19.9 %collective-permute-start.2 = (bf16[16,1280]{1,0:T(8,128)(2,1)S(1)}, bf16[16,1280]{1,0:T(8,128)(2,1)S(1)}, u32[]{:S(2)}, u32[]{:S(2)}) collective-permute-start(bf16[16,1280]{1,0:T(8,128)(2,1)S(1)} %reduce_sum.74), channel_id=1, source_target_pairs={{0,0},{1,1},{2,2},{3,3},{4,4},{5,5},{6,6},{7,7},{8,8},{9,9},{10,10... | collective-permute-start | bytes 122888 | tf_op jit(solution)/shard_map/ppermute | solution.py:28
  74.3 20.9 %collective-permute-start.3 = (bf16[16,1280]{1,0:T(8,128)(2,1)S(1)}, bf16[16,1280]{1,0:T(8,128)(2,1)S(1)}, u32[]{:S(2)}, u32[]{:S(2)}) collective-permute-start(bf16[16,1280]{1,0:T(8,128)(2,1)S(1)} %reduce_sum.74), channel_id=1, source_target_pairs={{0,128},{1,129},{2,130},{3,131},{4,132},{5,133},{6,134},{7,135},{8... | collective-permute-start | bytes 122888 | tf_op jit(solution)/shard_map/ppermute | solution.py:28
  95.3 3.1 %collective-permute-start.4 = (bf16[1,8,1280]{2,1,0:T(8,128)(2,1)S(1)}, bf16[1,8,1280]{2,1,0:T(8,128)(2,1)S(1)}, u32[]{:S(2)}, u32[]{:S(2)}) collective-permute-start(bf16[1,8,1280]{2,1,0:T(8,128)(2,1)S(1)} %get-tuple-element.27), channel_id=1, source_target_pairs={{0,1},{1,0},{2,3},{3,2},{4,5},{5,4},{6,7},{7,6},{8,9},{9,8},{10,11... | collective-permute-start | bytes 61448 | tf_op jit(solution)/shard_map/ppermute | solution.py:36
  99.3 20.5 %all-to-all-start.2 = ((bf16[16,16,1280]{2,1,0:T(8,128)(2,1)}), bf16[16,16,1280]{2,1,0:T(8,128)(2,1)}, u32[]{:S(2)}, u32[]{:S(2)}) async-start(bf16[16,16,1280]{2,1,0:T(8,128)(2,1)} %broadcast_in_dim.12), calls=%async_computation.2 | async-start | bytes 1310720 | tf_op jit(solution)/shard_map/all_to_all | solution.py:50
  121.3 1.7 copy-start.3
  121.8 1.2 copy-start.11
  128.7 5.2 %copy-start.6 = (bf16[128,1280]{1,0:T(8,128)(2,1)S(1)}, bf16[128,1280]{1,0:T(8,128)(2,1)}, u32[]{:S(2)}) copy-start(bf16[128,1280]{1,0:T(8,128)(2,1)} %copy-done.5) | copy-start | bytes 983044
  128.7 5.2 %copy-start.10 = (bf16[2,64,160]{2,1,0:T(8,128)(2,1)S(1)}, bf16[2,64,160]{2,1,0:T(8,128)(2,1)}, u32[]{:S(2)}) copy-start(bf16[2,64,160]{2,1,0:T(8,128)(2,1)} %copy-done.9) | copy-start | bytes 122884
  130.4 14.5 %all-to-all-start.3 = ((bf16[8,160,128]{2,1,0:T(8,128)(2,1)}), bf16[8,160,128]{2,1,0:T(8,128)(2,1)S(1)}, u32[]{:S(2)}, u32[]{:S(2)}) async-start(bf16[8,160,128]{2,1,0:T(8,128)(2,1)} %broadcast_in_dim.13), calls=%async_computation.3 | async-start | bytes 655360 | tf_op jit(solution)/shard_map/all_to_all | solution.py:50
  144.9 2.3 %collective-permute-start.5 = (bf16[160,128]{1,0:T(8,128)(2,1)S(1)}, bf16[160,128]{1,0:T(8,128)(2,1)S(1)}, u32[]{:S(2)}, u32[]{:S(2)}) collective-permute-start(bf16[160,128]{1,0:T(8,128)(2,1)S(1)} %reduce_sum.77), channel_id=1, source_target_pairs={{0,0},{1,1},{2,2},{3,3},{4,4},{5,5},{6,6},{7,7},{8,8},{9,9},{10,10... | collective-permute-start | bytes 122888 | tf_op jit(solution)/shard_map/ppermute | solution.py:28
  147.2 18.5 %copy-start.4 = (bf16[128,1280]{1,0:T(8,128)(2,1)S(1)}, bf16[128,1280]{1,0:T(8,128)(2,1)}, u32[]{:S(2)}) copy-start(bf16[128,1280]{1,0:T(8,128)(2,1)} %copy-done.3) | copy-start | bytes 983044
  148.2 26.8 %all-to-all-start.4 = ((bf16[16,160,128]{2,1,0:T(8,128)(2,1)}), bf16[16,160,128]{2,1,0:T(8,128)(2,1)S(1)}, u32[]{:S(2)}, u32[]{:S(2)}) async-start(bf16[16,160,128]{2,1,0:T(8,128)(2,1)} %broadcast_in_dim.14), calls=%async_computation.4 | async-start | bytes 1310720 | tf_op jit(solution)/shard_map/all_to_all | solution.py:50
  165.8 2.2 %copy-start.8 = (bf16[1280,64]{0,1:T(8,128)(2,1)S(1)}, bf16[1280,64]{0,1:T(8,128)(2,1)}, u32[]{:S(2)}) copy-start(bf16[1280,64]{0,1:T(8,128)(2,1)} %param.6) | copy-start | bytes 491524
  165.8 2.2 %copy-start.12 = (f32[2,256,64]{1,2,0:T(8,128)S(1)}, f32[2,256,64]{1,2,0:T(8,128)}, u32[]{:S(2)}) copy-start(f32[2,256,64]{1,2,0:T(8,128)} %fusion.13) | copy-start | bytes 393220

commit v3 on v2

v3 whole, which is shorter than its diff:
```python
import jax
import jax.numpy as jnp
import numpy as np
from jax import lax
from jax.sharding import Mesh, PartitionSpec as P

ALL = ("y", "zh", "x", "zq", "zr", "c")
PLANE = ("y", "x")
EXP = ("zq", "zr", "c")
REP = ("y", "zh", "x")
BF = jnp.bfloat16
F32 = jnp.float32


def signed(r):
    return r if r <= 8 else r - 16


def shifted(value, shift):
    pairs = []
    for y in range(4):
        for x in range(4):
            for z in range(32):
                for c in range(2):
                    to = (z + shift(y, x, c)) % 32
                    source = (((y * 2 + z // 16) * 4 + x) * 16 + z % 16) * 2 + c
                    target = (((y * 2 + to // 16) * 4 + x) * 16 + to % 16) * 2 + c
                    pairs.append((source, target))
    return lax.ppermute(value, ALL, pairs)


def out_shift(y, x, c):
    return signed(4 * y + x) * (1 - 2 * c)


def swapped(rows):
    return jnp.concatenate([rows[:1], lax.ppermute(rows[1:], "c", [(0, 1), (1, 0)])])


def smooth(values):
    return jax.nn.gelu(values, approximate=True)


def chooser(index, size):
    return (index[:, None] == jnp.arange(size)[None, :]).astype(BF)


def chosen(index, size):
    return jnp.asarray((index[:, None] == np.arange(size)[None, :]).astype(BF))


def picked(choose, rows):
    return jnp.dot(choose, rows, preferred_element_type=F32).astype(BF)


def added(rows, groups, inner):
    to, source = np.arange(groups * inner), np.arange(rows.shape[0])
    span = rows.shape[0] // groups
    same = (source[None, :] // span == to[:, None] // inner) & (source[None, :] % inner == to[:, None] % inner)
    return jnp.dot(jnp.asarray(same.astype(BF)), rows, preferred_element_type=F32).astype(BF)


def tied(*values):
    return lax.optimization_barrier(values)


def gathered(value, axes, size):
    out = jnp.broadcast_to(value[None], (size,) + value.shape)
    return lax.all_to_all(out, axes, 0, 0, tiled=True)


def on_device(tokens, slot_proj, in_weight, out_weight, out_grad):
    width = tokens.shape[2]
    column = lax.axis_index("y") * 4 + lax.axis_index("x")
    core = lax.axis_index("c")
    z_lo = lax.axis_index("zq") * 4 + lax.axis_index("zr")
    row = jnp.arange(16)
    to_core = core ^ (row // 8)
    target = (z_lo + (1 - 2 * to_core) * column) % 16
    outgoing = chooser((row // 4) % 2 * 128 + row % 2 * 64 + 4 * target + 2 * to_core + (row // 2) % 2, 256)
    static, row = np.arange(256), jnp.arange(256)
    by_expert = chosen((static // 2) % 32 * 8 + static // 64 * 2 + static % 2, 256)
    by_column = chosen((static // 2) % 4 * 64 + static // 16 * 4 + (static // 8) % 2 * 2 + static % 2, 256)
    expert = row % 64
    core_of = (expert // 2) % 2
    source = ((1 - 2 * core_of) * (expert // 4 - z_lo)) % 16
    by_image = chooser(
        source * 16 + (core_of ^ core) * 8 + row // 128 * 4 + expert % 2 * 2 + (row // 64) % 2, 256
    )

    logits = jnp.einsum("itd,de->ite", tokens, slot_proj, preferred_element_type=F32)
    dispatch = jax.nn.softmax(logits, axis=1)
    combine = jax.nn.softmax(logits, axis=2)
    dispatch_b = dispatch.astype(BF)
    combine_b = combine.astype(BF)
    slot_rows = jnp.einsum("ite,itd->ied", dispatch_b, tokens, preferred_element_type=F32).astype(BF)
    expert_grad = jnp.einsum("ite,itd->ied", combine_b, out_grad, preferred_element_type=F32).astype(BF)
    both = jnp.concatenate([slot_rows.reshape(128, width), expert_grad.reshape(128, width)])
    held = swapped(picked(outgoing, both).reshape(2, 8, width))
    sent = shifted(held.reshape(16, width), out_shift)
    sent, by_image, first = tied(sent, by_image, lax.axis_index("y") * 16)
    got = gathered(sent, PLANE, 16).reshape(256, width)
    kinds = picked(by_expert, got).reshape(2, 2, 64, width)
    got_slots, got_grads = kinds[0], kinds[1]
    pre_act = jnp.einsum("erd,edf->erf", got_slots, in_weight, preferred_element_type=F32)
    activated, pullback = jax.vjp(smooth, pre_act)
    hidden = activated.astype(BF)
    out_part = jnp.einsum("erf,efd->erd", hidden, out_weight, preferred_element_type=F32).astype(BF)
    hidden_grad = jnp.einsum("erd,efd->erf", got_grads, out_weight, preferred_element_type=F32)
    pre_grad = pullback(hidden_grad)[0].astype(BF)
    slot_part = jnp.einsum("erf,edf->erd", pre_grad, in_weight, preferred_element_type=F32).astype(BF)
    parts = jnp.concatenate([out_part.reshape(128, width), slot_part.reshape(128, width)])
    scattered = lax.all_to_all(picked(by_column, parts).reshape(16, 16, width), PLANE, 0, 0, tiled=True)
    summed = added(scattered.reshape(256, width), 1, 16)
    summed, hidden, pre_grad, got_slots, got_grads = tied(summed, hidden, pre_grad, got_slots, got_grads)
    near = shifted(summed, lambda y, x, c: -out_shift(y, x, c))
    far = shifted(summed, lambda y, x, c: 16 - out_shift(y, x, c))
    out_weight_grad = jnp.einsum("erf,erd->efd", hidden, got_grads, preferred_element_type=F32).astype(BF)
    in_weight_grad = jnp.einsum("erd,erf->edf", got_slots, pre_grad, preferred_element_type=F32).astype(BF)
    near, far, out_weight_grad, in_weight_grad = tied(near, far, out_weight_grad, in_weight_grad)
    home = (near.astype(F32) + far.astype(F32)).astype(BF)
    back = gathered(swapped(home.reshape(2, 8, width)).reshape(16, width), PLANE, 16).reshape(256, width)
    results = picked(by_image, back).reshape(2, 2, 64, width)
    expert_out, slot_grad = results[0], results[1]
    combine_grad = jnp.einsum("itd,ied->ite", out_grad, expert_out, preferred_element_type=F32)
    dispatch_grad = jnp.einsum("itd,ied->ite", tokens, slot_grad, preferred_element_type=F32)
    from_dispatch = dispatch * (dispatch_grad - jnp.sum(dispatch * dispatch_grad, axis=1, keepdims=True))
    from_combine = combine * (combine_grad - jnp.sum(combine * combine_grad, axis=2, keepdims=True))
    logit_grad = (from_dispatch + from_combine).astype(BF)
    own = lax.dynamic_slice(logit_grad, (0, 0, first), (2, 256, 16), allow_negative_indices=False)
    mine = jnp.einsum("ite,itd->ed", own, tokens, preferred_element_type=F32).astype(BF)
    mine = added(gathered(mine, ("zr", "c"), 8).reshape(128, width), 1, 16)
    mine, logit_grad, expert_out, slot_grad = tied(mine, logit_grad, expert_out, slot_grad)
    mine = shifted(mine, lambda y, x, c: 4 * (0, 1, 2, -1)[x])
    mixed = jnp.einsum("ite,ied->itd", combine_b, expert_out, preferred_element_type=F32).astype(BF)
    weights = jnp.concatenate([dispatch_b, logit_grad], axis=2)
    vectors = jnp.concatenate([slot_grad, jnp.broadcast_to(slot_proj.T, (2, 64, width))], axis=1)
    token_grad = jnp.einsum("itk,ikd->itd", weights, vectors, preferred_element_type=F32).astype(BF)
    mine, mixed, token_grad = tied(mine, mixed, token_grad)
    shares = gathered(mine, PLANE, 16).reshape(256, width)
    proj_grad = added(shares, 4, 16).T
    return (mixed, token_grad, proj_grad, in_weight_grad, out_weight_grad)


def solution(mesh):
    fine = Mesh(mesh.devices.reshape(4, 2, 4, 4, 4, 2), ALL)
    images, first, second = P(EXP, None, None), P(EXP, None, REP), P(EXP, REP, None)
    return jax.shard_map(
        on_device,
        mesh=fine,
        in_specs=(images, P(), first, second, images),
        out_specs=(images, images, P(), first, second),
        check_vma=False,
    )
```

time: 178 us -> 166 us (0.933)
  blocking collectives: 14.2 us -> 92.5 us
  starting transfers between devices: 84.9 us -> 43.9 us
  waiting for transfers between devices: 42.7 us -> 6.07 us
  matrix products: 22.7 us -> 15.1 us
  other arithmetic: 5.06 us -> 2.46 us
  local copies, waits for them, and re-layouts: 5.43 us -> 3.04 us
    all_to_all x1 -> x5, blocking collectives: 14.2 us -> 92.5 us  [the longest x4 78.4 us: gathered(): return lax.all_to_all(out, axes, 0, 0, tiled=True)]
    all_to_all x4 -> x0, starting transfers between devices: 40.6 us -> none  [gathered(): return lax.all_to_all(out, axes, 0, 0, tiled=True)]
    all_to_all x4 -> x0, waiting for transfers between devices: 32.4 us -> none  [gathered(): return lax.all_to_all(out, axes, 0, 0, tiled=True)]
    dot_general x4 -> x5, matrix products: 10.3 us -> 3.15 us  [the longest x1 1.61 us: on_device(): jnp.einsum('itk,ikd->itd', weights, vectors, preferred_element_type=F32)]
    ppermute x4, waiting for transfers between devices: 8.01 us -> 3.79 us  [shifted(): return lax.ppermute(value, ALL, pairs)]
    broadcast_in_dim x4, local copies, waits for them, and re-layouts: 3.46 us -> 0.16 us  [gathered(): out = jnp.broadcast_to(value[None], (size,) + value.shape)]
  transfers between devices with their start and end apart: 10 -> 6, of which waited for: 8 -> 4; matrix products, arithmetic and copies ran while one was open for 6% -> 4% of each run, Pallas kernels for 0% -> 0%
where the time goes in v3:
time: 166 us; the launch traced here: 164 us
  blocking collectives  92.5 us (56%)
  starting transfers between devices  43.9 us (26%)
  matrix products  15.1 us (9%)
  waiting for transfers between devices  6.07 us (4%)
  local copies, waits for them, and re-layouts  3.04 us (2%)
  other arithmetic  2.46 us (1%)
    all_to_all x4, blocking collectives, gathered(): return lax.all_to_all(out, axes, 0, 0, tiled=True)  78.4 us
    ppermute x4, starting transfers between devices, shifted(): return lax.ppermute(value, ALL, pairs)  39.9 us
    all_to_all x1, blocking collectives, on_device(): lax.all_to_all(picked(by_column, parts).reshape(16, 16, width), PLANE, 0,...  14 us
    ppermute x2, starting transfers between devices, swapped(): lax.ppermute(rows[1:], 'c', [(0, 1), (1, 0)])  3.98 us
    ppermute x4, waiting for transfers between devices, shifted(): return lax.ppermute(value, ALL, pairs)  3.79 us
  transfers between devices with their start and end apart: 6, of which 4 were waited for; matrix products, arithmetic and copies ran while one was open for 4% of the time, Pallas kernels for 0%

profile of v3, /device:TPU:24, one launch (start us, length us, event | category | flops | bytes accessed | tf_op | source)
XLA Modules:
  0.0 164.0 jit_solution(15336967995677223186)
XLA Ops:
  0.6 0.0 copy-start
  0.6 1.3 copy-done
  2.0 1.4 fusion.26
  3.4 0.0 copy-start.1
  3.4 0.4 fusion.75
  3.8 0.7 fusion.74
  4.5 0.1 fusion.71
  4.6 1.1 convolution_convert_fusion.9
  5.7 0.0 copy-done.1
  5.7 0.3 convolution_convert_fusion.8
  6.1 1.2 convolution_convert_fusion.13
  7.3 2.1 %collective-permute-start = (bf16[1,8,1280]{2,1,0:T(8,128)(2,1)S(1)}, bf16[1,8,1280]{2,1,0:T(8,128)(2,1)S(1)}, u32[]{:S(2)}, u32[]{:S(2)}) collective-permute-start(bf16[1,8,1280]{2,1,0:T(8,128)(2,1)S(1)} %get-tuple-element.52), channel_id=1, source_target_pairs={{0,1},{1,0},{2,3},{3,2},{4,5},{5,4},{6,7},{7,6},{8,9},{9,8},{10,11... | collective-permute-start | bytes 61448 | tf_op jit(solution)/shard_map/ppermute | solution.py:37
  9.4 1.1 collective-permute-done
  10.5 20.0 %collective-permute-start.1 = (bf16[16,1280]{1,0:T(8,128)(2,1)S(1)}, bf16[16,1280]{1,0:T(8,128)(2,1)S(1)}, u32[]{:S(2)}, u32[]{:S(2)}) collective-permute-start(bf16[16,1280]{1,0:T(8,128)(2,1)S(1)} %maximum_bitcast_fusion), channel_id=1, source_target_pairs={{0,0},{1,1},{2,2},{3,3},{4,4},{5,5},{6,6},{7,7},{8,8},{9,9},{10,10... | collective-permute-start | bytes 122888 | tf_op jit(solution)/shard_map/ppermute | solution.py:29
  30.5 0.8 fusion.25
  31.3 0.9 collective-permute-done.1
  32.2 19.5 %all_to_all.25 = bf16[16,16,1280]{2,1,0:T(8,128)(2,1)S(1)} all-to-all(bf16[16,16,1280]{2,1,0:T(8,128)(2,1)S(1)} %broadcast_in_dim.12), channel_id=1, replica_groups=mesh['y'=4,'zh'=2,'x'=4,'zq'=4,'zr'=4,'c'=2] {'y','x'}, dimensions={0} | all-to-all | bytes 1310720 | tf_op jit(solution)/shard_map/all_to_all | solution.py:69
  51.7 0.3 fusion.5
  52.1 0.0 copy-start.3
  52.1 0.7 copy-done.2
  52.9 0.4 fusion.76
  53.3 0.0 copy-done.3
  53.3 0.5 fusion.34
  53.8 0.0 copy-start.11
  53.8 0.3 convolution_convert_fusion.6
  54.0 0.0 copy-start.10
  54.1 0.3 convolution_convert_fusion.7
  54.3 0.3 copy-done.11
  54.6 0.3 fusion.77
  54.9 0.0 copy-start.13
  55.0 0.3 fusion.4
  55.3 14.0 %all_to_all.26 = bf16[16,16,1280]{2,1,0:T(8,128)(2,1)S(1)} all-to-all(bf16[16,16,1280]{2,1,0:T(8,128)(2,1)S(1)} %bitcast.92), channel_id=1, replica_groups=mesh['y'=4,'zh'=2,'x'=4,'zq'=4,'zr'=4,'c'=2] {'y','x'}, dimensions={0} | all-to-all | bytes 1310720 | tf_op jit(solution)/shard_map/all_to_all | solution.py:113
  69.3 0.0 copy-done.13
  69.3 0.2 fusion.7
  69.5 15.0 %collective-permute-start.3 = (bf16[16,1280]{1,0:T(8,128)(2,1)S(1)}, bf16[16,1280]{1,0:T(8,128)(2,1)S(1)}, u32[]{:S(2)}, u32[]{:S(2)}) collective-permute-start(bf16[16,1280]{1,0:T(8,128)(2,1)S(1)} %fusion.7), channel_id=1, source_target_pairs={{0,128},{1,129},{2,130},{3,131},{4,132},{5,133},{6,134},{7,135},{8... | collective-permute-start | bytes 122888 | tf_op jit(solution)/shard_map/ppermute | solution.py:29
  84.5 4.3 %collective-permute-start.2 = (bf16[16,1280]{1,0:T(8,128)(2,1)S(1)}, bf16[16,1280]{1,0:T(8,128)(2,1)S(1)}, u32[]{:S(2)}, u32[]{:S(2)}) collective-permute-start(bf16[16,1280]{1,0:T(8,128)(2,1)S(1)} %fusion.7), channel_id=1, source_target_pairs={{0,0},{1,1},{2,2},{3,3},{4,4},{5,5},{6,6},{7,7},{8,8},{9,9},{10,10... | collective-permute-start | bytes 122888 | tf_op jit(solution)/shard_map/ppermute | solution.py:29
  88.8 1.3 convolution_convert_fusion.3
  90.1 1.3 convolution_convert_fusion.2
  91.4 0.0 collective-permute-done.3
  91.4 2.9 %collective-permute-done.2 = bf16[16,1280]{1,0:T(8,128)(2,1)S(1)} collective-permute-done((bf16[16,1280]{1,0:T(8,128)(2,1)S(1)}, bf16[16,1280]{1,0:T(8,128)(2,1)S(1)}, u32[]{:S(2)}, u32[]{:S(2)}) %collective-permute-start.2) | collective-permute-done | bytes 40992 | tf_op jit(solution)/shard_map/ppermute | solution.py:29
  94.3 1.9 %collective-permute-start.4 = (bf16[1,8,1280]{2,1,0:T(8,128)(2,1)S(1)}, bf16[1,8,1280]{2,1,0:T(8,128)(2,1)S(1)}, u32[]{:S(2)}, u32[]{:S(2)}) collective-permute-start(bf16[1,8,1280]{2,1,0:T(8,128)(2,1)S(1)} %get-tuple-element.50), channel_id=1, source_target_pairs={{0,1},{1,0},{2,3},{3,2},{4,5},{5,4},{6,7},{7,6},{8,9},{9,8},{10,11... | collective-permute-start | bytes 61448 | tf_op jit(solution)/shard_map/ppermute | solution.py:37
  96.3 1.2 collective-permute-done.4
  97.5 18.2 %all_to_all.27 = bf16[16,16,1280]{2,1,0:T(8,128)(2,1)S(1)} all-to-all(bf16[16,16,1280]{2,1,0:T(8,128)(2,1)S(1)} %broadcast_in_dim.14), channel_id=1, replica_groups=mesh['y'=4,'zh'=2,'x'=4,'zq'=4,'zr'=4,'c'=2] {'y','x'}, dimensions={0} | all-to-all | bytes 1310720 | tf_op jit(solution)/shard_map/all_to_all | solution.py:69
  115.7 0.0 copy-done.7
  115.7 0.3 convolution_convert_fusion.5
  116.0 0.0 copy-start.6
  116.1 0.5 convolution_bitcast_fusion.2
  116.6 0.3 copy-done.6
  117.0 0.4 fusion.17
  117.3 0.5 convolution_bitcast_fusion.1
  117.9 0.1 fusion.18
  117.9 0.0 copy-start.14
  117.9 0.3 fusion.6
  118.3 0.0 copy-start.4
  118.3 13.7 %all_to_all.28 = bf16[8,16,1280]{2,1,0:T(8,128)(2,1)S(1)} all-to-all(bf16[8,16,1280]{2,1,0:T(8,128)(2,1)S(1)} %broadcast_in_dim.15), channel_id=1, replica_groups=mesh['y'=4,'zh'=2,'x'=4,'zq'=4,'zr'=4,'c'=2] {'zr','c'}, dimensions={0} | all-to-all | bytes 655360 | tf_op jit(solution)/shard_map/all_to_all | solution.py:69
  131.9 0.0 copy-done.14
  131.9 0.2 fusion.8
  132.1 0.7 collective-permute-start.5
  132.8 1.6 convolution_convert_fusion.1
  134.4 0.0 copy-done.4
  134.4 1.6 convolution_convert_fusion
  136.0 0.0 collective-permute-done.5
  136.1 27.1 %all_to_all.29 = bf16[16,16,1280]{2,1,0:T(8,128)(2,1)S(1)} all-to-all(bf16[16,16,1280]{2,1,0:T(8,128)(2,1)S(1)} %broadcast_in_dim.17), channel_id=1, replica_groups=mesh['y'=4,'zh'=2,'x'=4,'zq'=4,'zr'=4,'c'=2] {'y','x'}, dimensions={0} | all-to-all | bytes 1310720 | tf_op jit(solution)/shard_map/all_to_all | solution.py:69
  163.1 0.9 convolution_convert_fusion.10
  (25 shorter events, 0.4 us)
Async XLA Ops:
  0.6 1.3 copy-start
  3.4 2.3 %copy-start.1 = (bf16[2,256,1280]{2,1,0:T(8,128)(2,1)S(1)}, bf16[2,256,1280]{2,1,0:T(8,128)(2,1)}, u32[]{:S(2)}) copy-start(bf16[2,256,1280]{2,1,0:T(8,128)(2,1)} %param.14) | copy-start | bytes 3932164
  3.8 2.3 %copy-start.5 = (f32[2,256,64]{1,2,0:T(8,128)}, f32[2,256,64]{1,2,0:T(8,128)S(1)}, u32[]{:S(2)}) copy-start(f32[2,256,64]{1,2,0:T(8,128)S(1)} %get-tuple-element.56) | copy-start | bytes 393220
  7.3 44.5 %copy-start.9 = (bf16[256,256]{1,0:T(8,128)(2,1)S(1)}, bf16[256,256]{1,0:T(8,128)(2,1)}, u32[]{:S(2)}) copy-start(bf16[256,256]{1,0:T(8,128)(2,1)} %constant.209.clone) | copy-start | bytes 393220
  7.3 3.2 %collective-permute-start = (bf16[1,8,1280]{2,1,0:T(8,128)(2,1)S(1)}, bf16[1,8,1280]{2,1,0:T(8,128)(2,1)S(1)}, u32[]{:S(2)}, u32[]{:S(2)}) collective-permute-start(bf16[1,8,1280]{2,1,0:T(8,128)(2,1)S(1)} %get-tuple-element.52), channel_id=1, source_target_pairs={{0,1},{1,0},{2,3},{3,2},{4,5},{5,4},{6,7},{7,6},{8,9},{9,8},{10,11... | collective-permute-start | bytes 61448 | tf_op jit(solution)/shard_map/ppermute | solution.py:37
  10.5 21.7 %collective-permute-start.1 = (bf16[16,1280]{1,0:T(8,128)(2,1)S(1)}, bf16[16,1280]{1,0:T(8,128)(2,1)S(1)}, u32[]{:S(2)}, u32[]{:S(2)}) collective-permute-start(bf16[16,1280]{1,0:T(8,128)(2,1)S(1)} %maximum_bitcast_fusion), channel_id=1, source_target_pairs={{0,0},{1,1},{2,2},{3,3},{4,4},{5,5},{6,6},{7,7},{8,8},{9,9},{10,10... | collective-permute-start | bytes 122888 | tf_op jit(solution)/shard_map/ppermute | solution.py:29
  51.7 1.1 copy-start.2
  52.1 1.2 copy-start.3
  53.8 0.8 copy-start.11
  54.0 0.9 copy-start.10
  54.9 14.4 %copy-start.13 = (bf16[16,256]{1,0:T(8,128)(2,1)S(1)}, bf16[16,256]{1,0:T(8,128)(2,1)}, u32[]{:S(2)}) copy-start(bf16[16,256]{1,0:T(8,128)(2,1)} %constant.211.clone) | copy-start | bytes 24580
  69.5 21.9 %collective-permute-start.3 = (bf16[16,1280]{1,0:T(8,128)(2,1)S(1)}, bf16[16,1280]{1,0:T(8,128)(2,1)S(1)}, u32[]{:S(2)}, u32[]{:S(2)}) collective-permute-start(bf16[16,1280]{1,0:T(8,128)(2,1)S(1)} %fusion.7), channel_id=1, source_target_pairs={{0,128},{1,129},{2,130},{3,131},{4,132},{5,133},{6,134},{7,135},{8... | collective-permute-start | bytes 122888 | tf_op jit(solution)/shard_map/ppermute | solution.py:29
  84.5 9.8 %collective-permute-start.2 = (bf16[16,1280]{1,0:T(8,128)(2,1)S(1)}, bf16[16,1280]{1,0:T(8,128)(2,1)S(1)}, u32[]{:S(2)}, u32[]{:S(2)}) collective-permute-start(bf16[16,1280]{1,0:T(8,128)(2,1)S(1)} %fusion.7), channel_id=1, source_target_pairs={{0,0},{1,1},{2,2},{3,3},{4,4},{5,5},{6,6},{7,7},{8,8},{9,9},{10,10... | collective-permute-start | bytes 122888 | tf_op jit(solution)/shard_map/ppermute | solution.py:29
  91.4 24.3 %copy-start.7 = (bf16[256,256]{1,0:T(8,128)(2,1)S(1)}, bf16[256,256]{1,0:T(8,128)(2,1)}, u32[]{:S(2)}) copy-start(bf16[256,256]{1,0:T(8,128)(2,1)} %fusion.25) | copy-start | bytes 393220
  94.3 3.1 %collective-permute-start.4 = (bf16[1,8,1280]{2,1,0:T(8,128)(2,1)S(1)}, bf16[1,8,1280]{2,1,0:T(8,128)(2,1)S(1)}, u32[]{:S(2)}, u32[]{:S(2)}) collective-permute-start(bf16[1,8,1280]{2,1,0:T(8,128)(2,1)S(1)} %get-tuple-element.50), channel_id=1, source_target_pairs={{0,1},{1,0},{2,3},{3,2},{4,5},{5,4},{6,7},{7,6},{8,9},{9,8},{10,11... | collective-permute-start | bytes 61448 | tf_op jit(solution)/shard_map/ppermute | solution.py:37
  116.0 0.9 copy-start.6
  117.0 0.9 copy-start.8
  117.9 14.0 %copy-start.14 = (bf16[16,128]{1,0:T(8,128)(2,1)S(1)}, bf16[16,128]{1,0:T(8,128)(2,1)}, u32[]{:S(2)}) copy-start(bf16[16,128]{1,0:T(8,128)(2,1)} %constant.212.clone) | copy-start | bytes 12292
  118.3 16.1 %copy-start.4 = (bf16[1280,64]{0,1:T(8,128)(2,1)S(1)}, bf16[1280,64]{0,1:T(8,128)(2,1)}, u32[]{:S(2)}) copy-start(bf16[1280,64]{0,1:T(8,128)(2,1)} %param.11) | copy-start | bytes 491524
  132.1 3.9 %collective-permute-start.5 = (bf16[16,1280]{1,0:T(8,128)(2,1)S(1)}, bf16[16,1280]{1,0:T(8,128)(2,1)S(1)}, u32[]{:S(2)}, u32[]{:S(2)}) collective-permute-start(bf16[16,1280]{1,0:T(8,128)(2,1)S(1)} %fusion.8), channel_id=1, source_target_pairs={{0,0},{1,1},{2,2},{3,3},{4,4},{5,5},{6,6},{7,7},{8,8},{9,9},{10,10... | collective-permute-start | bytes 122888 | tf_op jit(solution)/shard_map/ppermute | solution.py:29
  136.0 27.1 %copy-start.12 = (bf16[64,256]{1,0:T(8,128)(2,1)S(1)}, bf16[64,256]{1,0:T(8,128)(2,1)}, u32[]{:S(2)}) copy-start(bf16[64,256]{1,0:T(8,128)(2,1)} %constant.213.clone) | copy-start | bytes 98308

commit v4 on v3

--- a/solution.py
+++ b/solution.py
@@ -2,6 +2,8 @@
 import jax.numpy as jnp
 import numpy as np
 from jax import lax
+from jax.experimental import pallas as pl
+from jax.experimental.pallas import tpu as pltpu
 from jax.sharding import Mesh, PartitionSpec as P
 
 ALL = ("y", "zh", "x", "zq", "zr", "c")
@@ -69,15 +71,58 @@
     return lax.all_to_all(out, axes, 0, 0, tiled=True)
 
 
+def front_body(place_ref, tokens_ref, cotangent_ref, proj_ref, sent_ref, dispatch_ref, combine_ref, rows_ref):
+    image = pl.program_id(0)
+    tokens = tokens_ref[0]
+    logits = lax.dot_general(proj_ref[...], tokens, (((1,), (1,)), ((), ())), preferred_element_type=F32)
+    raised = jnp.exp(logits - jnp.max(logits, axis=1, keepdims=True))
+    dispatch = raised / jnp.sum(raised, axis=1, keepdims=True)
+    raised = jnp.exp(logits - jnp.max(logits, axis=0, keepdims=True))
+    combine = raised / jnp.sum(raised, axis=0, keepdims=True)
+    dispatch_ref[0] = dispatch
+    combine_ref[0] = combine
+    first = pl.multiple_of(image * 64, 64)
+    rows_ref[pl.ds(first, 64), :] = jnp.dot(dispatch.astype(BF), tokens, preferred_element_type=F32).astype(BF)
+    rows_ref[pl.ds(first + 128, 64), :] = jnp.dot(
+        combine.astype(BF), cotangent_ref[0], preferred_element_type=F32
+    ).astype(BF)
+
+    @pl.when(image == 1)
+    def _():
+        z_lo, column, core = place_ref[0], place_ref[1], place_ref[2]
+        row = lax.broadcasted_iota(jnp.int32, (16, 256), 0)
+        near = (z_lo + (1 - 2 * core) * column) & 15
+        cross = (z_lo - (1 - 2 * core) * column) & 15
+        block = jnp.where(row < 8, 4 * near + 2 * core, 4 * cross + 2 * (1 - core))
+        wanted = ((row >> 2) & 1) * 128 + (row & 1) * 64 + block + ((row >> 1) & 1)
+        choose = (wanted == lax.broadcasted_iota(jnp.int32, (16, 256), 1)).astype(F32).astype(BF)
+        sent_ref[...] = jnp.dot(choose, rows_ref[...], preferred_element_type=F32).astype(BF)
+
+
+def front(place, tokens, cotangent, proj):
+    width = tokens.shape[2]
+    image = pl.BlockSpec((1, 256, width), lambda i: (i, 0, 0))
+    scores = pl.BlockSpec((1, 64, 256), lambda i: (i, 0, 0))
+    return pl.pallas_call(
+        front_body,
+        grid=(2,),
+        in_specs=[pl.BlockSpec(memory_space=pltpu.SMEM), image, image, pl.BlockSpec((64, width), lambda i: (0, 0))],
+        out_specs=[pl.BlockSpec((16, width), lambda i: (0, 0)), scores, scores],
+        out_shape=[
+            jax.ShapeDtypeStruct((16, width), BF),
+            jax.ShapeDtypeStruct((2, 64, 256), F32),
+            jax.ShapeDtypeStruct((2, 64, 256), F32),
+        ],
+        scratch_shapes=[pltpu.VMEM((256, width), BF)],
+        compiler_params=pltpu.CompilerParams(vmem_limit_bytes=56 * 2**20),
+    )(place, tokens, cotangent, proj)
+
+
 def on_device(tokens, slot_proj, in_weight, out_weight, out_grad):
     width = tokens.shape[2]
     column = lax.axis_index("y") * 4 + lax.axis_index("x")
     core = lax.axis_index("c")
     z_lo = lax.axis_index("zq") * 4 + lax.axis_index("zr")
-    row = jnp.arange(16)
-    to_core = core ^ (row // 8)
-    target = (z_lo + (1 - 2 * to_core) * column) % 16
-    outgoing = chooser((row // 4) % 2 * 128 + row % 2 * 64 + 4 * target + 2 * to_core + (row // 2) % 2, 256)
     static, row = np.arange(256), jnp.arange(256)
     by_expert = chosen((static // 2) % 32 * 8 + static // 64 * 2 + static % 2, 256)
     by_column = chosen((static // 2) % 4 * 64 + static // 16 * 4 + (static // 8) % 2 * 2 + static % 2, 256)
@@ -85,20 +130,18 @@
     core_of = (expert // 2) % 2
     source = ((1 - 2 * core_of) * (expert // 4 - z_lo)) % 16
     by_image = chooser(
-        source * 16 + (core_of ^ core) * 8 + row // 128 * 4 + expert % 2 * 2 + (row // 64) % 2, 256
+        source * 16 + core_of * 8 + row // 128 * 4 + expert % 2 * 2 + (row // 64) % 2, 256
     )
 
-    logits = jnp.einsum("itd,de->ite", tokens, slot_proj, preferred_element_type=F32)
-    dispatch = jax.nn.softmax(logits, axis=1)
-    combine = jax.nn.softmax(logits, axis=2)
-    dispatch_b = dispatch.astype(BF)
-    combine_b = combine.astype(BF)
-    slot_rows = jnp.einsum("ite,itd->ied", dispatch_b, tokens, preferred_element_type=F32).astype(BF)
-    expert_grad = jnp.einsum("ite,itd->ied", combine_b, out_grad, preferred_element_type=F32).astype(BF)
-    both = jnp.concatenate([slot_rows.reshape(128, width), expert_grad.reshape(128, width)])
-    held = swapped(picked(outgoing, both).reshape(2, 8, width))
+    place = jnp.stack([z_lo, column, core]).astype(jnp.int32)
+    outgoing, dispatch, combine = front(place, tokens, out_grad, slot_proj.T)
+    dispatch, combine = jnp.swapaxes(dispatch, 1, 2), jnp.swapaxes(combine, 1, 2)
+    dispatch_b, combine_b = dispatch.astype(BF), combine.astype(BF)
+    held = swapped(outgoing.reshape(2, 8, width))
     sent = shifted(held.reshape(16, width), out_shift)
-    sent, by_image, first = tied(sent, by_image, lax.axis_index("y") * 16)
+    sent, by_image, first, dispatch_b, combine_b, leading = tied(
+        sent, by_image, lax.axis_index("y") * 16, dispatch_b, combine_b, core == 0
+    )
     got = gathered(sent, PLANE, 16).reshape(256, width)
     kinds = picked(by_expert, got).reshape(2, 2, 64, width)
     got_slots, got_grads = kinds[0], kinds[1]
@@ -119,7 +162,9 @@
     in_weight_grad = jnp.einsum("erd,erf->edf", got_slots, pre_grad, preferred_element_type=F32).astype(BF)
     near, far, out_weight_grad, in_weight_grad = tied(near, far, out_weight_grad, in_weight_grad)
     home = (near.astype(F32) + far.astype(F32)).astype(BF)
-    back = gathered(swapped(home.reshape(2, 8, width)).reshape(16, width), PLANE, 16).reshape(256, width)
+    mine = home.reshape(2, 8, width)
+    mine = jnp.broadcast_to(jnp.where(leading, mine, mine[::-1])[None], (16, 2, 8, width))
+    back = lax.all_to_all(mine.reshape(32, 8, width), PLANE + ("c",), 0, 0, tiled=True).reshape(256, width)
     results = picked(by_image, back).reshape(2, 2, 64, width)
     expert_out, slot_grad = results[0], results[1]
     combine_grad = jnp.einsum("itd,ied->ite", out_grad, expert_out, preferred_element_type=F32)
@@ -129,14 +174,14 @@
     logit_grad = (from_dispatch + from_combine).astype(BF)
     own = lax.dynamic_slice(logit_grad, (0, 0, first), (2, 256, 16), allow_negative_indices=False)
     mine = jnp.einsum("ite,itd->ed", own, tokens, preferred_element_type=F32).astype(BF)
+    mixed = jnp.einsum("ite,ied->itd", combine_b, expert_out, preferred_element_type=F32).astype(BF)
     mine = added(gathered(mine, ("zr", "c"), 8).reshape(128, width), 1, 16)
-    mine, logit_grad, expert_out, slot_grad = tied(mine, logit_grad, expert_out, slot_grad)
+    mine, mixed, logit_grad, slot_grad = tied(mine, mixed, logit_grad, slot_grad)
     mine = shifted(mine, lambda y, x, c: 4 * (0, 1, 2, -1)[x])
-    mixed = jnp.einsum("ite,ied->itd", combine_b, expert_out, preferred_element_type=F32).astype(BF)
     weights = jnp.concatenate([dispatch_b, logit_grad], axis=2)
     vectors = jnp.concatenate([slot_grad, jnp.broadcast_to(slot_proj.T, (2, 64, width))], axis=1)
     token_grad = jnp.einsum("itk,ikd->itd", weights, vectors, preferred_element_type=F32).astype(BF)
-    mine, mixed, token_grad = tied(mine, mixed, token_grad)
+    mine, token_grad = tied(mine, token_grad)
     shares = gathered(mine, PLANE, 16).reshape(256, width)
     proj_grad = added(shares, 4, 16).T
     return (mixed, token_grad, proj_grad, in_weight_grad, out_weight_grad)

time: 166 us -> 163 us (0.982)
  blocking collectives: 92.5 us -> 78.9 us
  waiting for transfers between devices: 6.07 us -> 14 us
  Pallas kernels: 0 us -> 4.44 us
  matrix products: 15.1 us -> 11.1 us
  starting transfers between devices: 43.9 us -> 45.8 us
    all_to_all x4 -> x2, blocking collectives: 78.4 us -> 46.9 us  [gathered(): return lax.all_to_all(out, axes, 0, 0, tiled=True)]
    all_to_all x0 -> x1, blocking collectives: none -> 17.9 us  [on_device(): lax.all_to_all(mine.reshape(32, 8, width), PLANE + ('c',), 0, 0, tiled=True)]
    all_to_all x0 -> x1, waiting for transfers between devices: none -> 9.46 us  [gathered(): return lax.all_to_all(out, axes, 0, 0, tiled=True)]
    pallas_call x0 -> x1, Pallas kernels: none -> 4.44 us  [front(): pl.pallas_call(front_body, grid=(2,), in_specs=[pl.BlockSpec(memory_space...]
    all_to_all x0 -> x1, starting transfers between devices: none -> 3.56 us  [gathered(): return lax.all_to_all(out, axes, 0, 0, tiled=True)]
    dot_general x3 -> x0, matrix products: 2.85 us -> none  [the longest x1 1.42 us: on_device(): jnp.einsum('itd,de->ite', tokens, slot_proj, preferred_element_type=F32)]
    ppermute x2 -> x1, waiting for transfers between devices: 2.28 us -> 0.09 us  [swapped(): lax.ppermute(rows[1:], 'c', [(0, 1), (1, 0)])]
    ppermute x2 -> x1, starting transfers between devices: 3.98 us -> 1.91 us  [swapped(): lax.ppermute(rows[1:], 'c', [(0, 1), (1, 0)])]
where the time goes in v4:
time: 163 us; the launch traced here: 161 us
  blocking collectives  78.9 us (48%)
  starting transfers between devices  45.8 us (28%)
  waiting for transfers between devices  14 us (9%)
  matrix products  11.1 us (7%)
  Pallas kernels  4.44 us (3%)
  local copies, waits for them, and re-layouts  3.88 us (2%)
  other arithmetic  2.03 us (1%)
    all_to_all x2, blocking collectives, gathered(): return lax.all_to_all(out, axes, 0, 0, tiled=True)  46.9 us
    ppermute x4, starting transfers between devices, shifted(): return lax.ppermute(value, ALL, pairs)  40.3 us
    all_to_all x1, blocking collectives, on_device(): lax.all_to_all(mine.reshape(32, 8, width), PLANE + ('c',), 0, 0, tiled=True)  17.9 us
    all_to_all x1, blocking collectives, on_device(): lax.all_to_all(picked(by_column, parts).reshape(16, 16, width), PLANE, 0,...  14.1 us
    all_to_all x1, waiting for transfers between devices, gathered(): return lax.all_to_all(out, axes, 0, 0, tiled=True)  9.46 us
    ppermute x4, waiting for transfers between devices, shifted(): return lax.ppermute(value, ALL, pairs)  4.44 us
    pallas_call x1, Pallas kernels, front(): pl.pallas_call(front_body, grid=(2,), in_specs=[pl.BlockSpec(memory_space...  4.44 us
    all_to_all x1, starting transfers between devices, gathered(): return lax.all_to_all(out, axes, 0, 0, tiled=True)  3.56 us
  transfers between devices with their start and end apart: 6, of which 4 were waited for; matrix products, arithmetic and copies ran while one was open for 4% of the time, Pallas kernels for 0%

profile of v4, /device:TPU:24, one launch (start us, length us, event | category | flops | bytes accessed | tf_op | source)
XLA Modules:
  0.0 161.1 jit_solution(14098557359587307671)
XLA Ops:
  0.6 0.0 copy-start
  0.7 0.6 pad_add_fusion.place_ref
  1.2 4.4 %shard_map.137 = (bf16[16,1280]{1,0:T(8,128)(2,1)}, f32[2,64,256]{2,1,0:T(8,128)}, f32[2,64,256]{2,1,0:T(8,128)}) custom-call(s32[3]{0:T(128)} %pad_add_fusion.place_ref, bf16[2,256,1280]{2,1,0:T(8,128)(2,1)} %tokens_ref.1, bf16[2,256,1280]{2,1,0:T(8,128)(2,1)} %cotangent_ref.1, bf16[64,1280]{1,0:T(8,128)(2,1)} %bitcast.105), custom_call_target="tpu_custom_call" | custom-call | tf_op jit(solution)/shard_map/pallas_call | solution.py:106
  5.7 0.7 slice_bitcast_fusion.1
  6.4 1.9 %collective-permute-start = (bf16[1,8,1280]{2,1,0:T(8,128)(2,1)S(1)}, bf16[1,8,1280]{2,1,0:T(8,128)(2,1)S(1)}, u32[]{:S(2)}, u32[]{:S(2)}) collective-permute-start(bf16[1,8,1280]{2,1,0:T(8,128)(2,1)S(1)} %get-tuple-element.60), channel_id=1, source_target_pairs={{0,1},{1,0},{2,3},{3,2},{4,5},{5,4},{6,7},{7,6},{8,9},{9,8},{10,11... | collective-permute-start | bytes 61448 | tf_op jit(solution)/shard_map/ppermute | solution.py:39
  8.3 0.0 copy-start.7
  8.4 1.0 bitcast_convert_fusion
  9.4 0.1 collective-permute-done
  9.5 20.0 %collective-permute-start.1 = (bf16[16,1280]{1,0:T(8,128)(2,1)S(1)}, bf16[16,1280]{1,0:T(8,128)(2,1)S(1)}, u32[]{:S(2)}, u32[]{:S(2)}) collective-permute-start(bf16[16,1280]{1,0:T(8,128)(2,1)S(1)} %maximum_bitcast_fusion), channel_id=1, source_target_pairs={{0,0},{1,1},{2,2},{3,3},{4,4},{5,5},{6,6},{7,7},{8,8},{9,9},{10,10... | collective-permute-start | bytes 122888 | tf_op jit(solution)/shard_map/ppermute | solution.py:31
  29.5 0.1 fusion.17
  29.6 1.5 collective-permute-done.1
  31.2 19.8 %all_to_all.25 = bf16[16,16,1280]{2,1,0:T(8,128)(2,1)S(1)} all-to-all(bf16[16,16,1280]{2,1,0:T(8,128)(2,1)S(1)} %broadcast_in_dim.10), channel_id=1, replica_groups=mesh['y'=4,'zh'=2,'x'=4,'zq'=4,'zr'=4,'c'=2] {'y','x'}, dimensions={0} | all-to-all | bytes 1310720 | tf_op jit(solution)/shard_map/all_to_all | solution.py:71
  51.0 0.0 copy-done.7
  51.0 0.0 copy-start.3
  51.0 0.3 fusion.3
  51.4 0.7 copy-done.3
  52.2 0.4 fusion.47
  52.5 0.0 copy-done
  52.6 0.5 fusion.24
  53.0 0.0 copy-start.9
  53.0 0.3 convolution_convert_fusion.6
  53.3 0.0 copy-start.8
  53.3 0.3 convolution_convert_fusion.7
  53.6 0.3 copy-done.9
  53.9 0.3 fusion.48
  54.2 0.0 copy-done.8
  54.2 0.0 copy-start.11
  54.2 0.3 fusion.2
  54.5 14.1 %all_to_all.26 = bf16[16,16,1280]{2,1,0:T(8,128)(2,1)S(1)} all-to-all(bf16[16,16,1280]{2,1,0:T(8,128)(2,1)S(1)} %bitcast.95), channel_id=1, replica_groups=mesh['y'=4,'zh'=2,'x'=4,'zq'=4,'zr'=4,'c'=2] {'y','x'}, dimensions={0} | all-to-all | bytes 1310720 | tf_op jit(solution)/shard_map/all_to_all | solution.py:156
  68.6 0.0 copy-done.11
  68.7 0.2 fusion.5
  68.8 15.4 %collective-permute-start.3 = (bf16[16,1280]{1,0:T(8,128)(2,1)S(1)}, bf16[16,1280]{1,0:T(8,128)(2,1)S(1)}, u32[]{:S(2)}, u32[]{:S(2)}) collective-permute-start(bf16[16,1280]{1,0:T(8,128)(2,1)S(1)} %fusion.5), channel_id=1, source_target_pairs={{0,128},{1,129},{2,130},{3,131},{4,132},{5,133},{6,134},{7,135},{8... | collective-permute-start | bytes 122888 | tf_op jit(solution)/shard_map/ppermute | solution.py:31
  84.2 4.3 %collective-permute-start.2 = (bf16[16,1280]{1,0:T(8,128)(2,1)S(1)}, bf16[16,1280]{1,0:T(8,128)(2,1)S(1)}, u32[]{:S(2)}, u32[]{:S(2)}) collective-permute-start(bf16[16,1280]{1,0:T(8,128)(2,1)S(1)} %fusion.5), channel_id=1, source_target_pairs={{0,0},{1,1},{2,2},{3,3},{4,4},{5,5},{6,6},{7,7},{8,8},{9,9},{10,10... | collective-permute-start | bytes 122888 | tf_op jit(solution)/shard_map/ppermute | solution.py:31
  88.5 1.3 convolution_convert_fusion.3
  89.8 1.3 convolution_convert_fusion.2
  91.1 0.0 collective-permute-done.3
  91.1 2.9 %collective-permute-done.2 = bf16[16,1280]{1,0:T(8,128)(2,1)S(1)} collective-permute-done((bf16[16,1280]{1,0:T(8,128)(2,1)S(1)}, bf16[16,1280]{1,0:T(8,128)(2,1)S(1)}, u32[]{:S(2)}, u32[]{:S(2)}) %collective-permute-start.2) | collective-permute-done | bytes 40992 | tf_op jit(solution)/shard_map/ppermute | solution.py:31
  94.1 17.9 %all_to_all.27 = bf16[32,8,1280]{2,1,0:T(8,128)(2,1)S(1)} all-to-all(bf16[32,8,1280]{2,1,0:T(8,128)(2,1)S(1)} %bitcast.99), channel_id=1, replica_groups=mesh['y'=4,'zh'=2,'x'=4,'zq'=4,'zr'=4,'c'=2] {'y','x','c'}, dimensions={0} | all-to-all | bytes 1310720 | tf_op jit(solution)/shard_map/all_to_all | solution.py:167
  112.1 0.0 copy-start.1
  112.1 0.3 convolution_convert_fusion.5
  112.4 0.0 copy-start.6
  112.5 0.0 copy-start.2
  112.5 0.9 copy-done.1
  113.4 0.5 convolution_bitcast_fusion.2
  113.9 0.0 copy-done.6
  113.9 0.0 copy-start.5
  113.9 0.2 fusion.11
  114.1 0.0 copy-done.2
  114.2 0.5 convolution_bitcast_fusion.1
  114.7 0.2 copy-done.5
  114.9 0.3 fusion.4
  115.1 0.8 broadcast_in_dim.12
  115.9 3.6 %all-to-all-start.3 = ((bf16[8,16,1280]{2,1,0:T(8,128)(2,1)}), bf16[8,16,1280]{2,1,0:T(8,128)(2,1)S(1)}, u32[]{:S(2)}, u32[]{:S(2)}) async-start(bf16[8,16,1280]{2,1,0:T(8,128)(2,1)} %broadcast_in_dim.12), calls=%async_computation.3 | async-start | bytes 655360 | tf_op jit(solution)/shard_map/all_to_all | solution.py:71
  119.5 1.6 convolution_convert_fusion.1
  121.1 9.5 %all-to-all-done.3 = bf16[8,16,1280]{2,1,0:T(8,128)(2,1)S(1)} async-done(((bf16[8,16,1280]{2,1,0:T(8,128)(2,1)}), bf16[8,16,1280]{2,1,0:T(8,128)(2,1)S(1)}, u32[]{:S(2)}, u32[]{:S(2)}) %all-to-all-start.3) | async-done | bytes 327712 | tf_op jit(solution)/shard_map/all_to_all | solution.py:71
  130.5 0.0 copy-done.12
  130.5 0.2 fusion.6
  130.7 0.7 collective-permute-start.4
  131.4 0.0 copy-done.4
  131.4 1.6 convolution_convert_fusion
  133.0 0.0 collective-permute-done.4
  133.1 27.1 %all_to_all.28 = bf16[16,16,1280]{2,1,0:T(8,128)(2,1)S(1)} all-to-all(bf16[16,16,1280]{2,1,0:T(8,128)(2,1)S(1)} %broadcast_in_dim.14), channel_id=1, replica_groups=mesh['y'=4,'zh'=2,'x'=4,'zq'=4,'zr'=4,'c'=2] {'y','x'}, dimensions={0} | all-to-all | bytes 1310720 | tf_op jit(solution)/shard_map/all_to_all | solution.py:71
  160.2 0.0 copy-done.10
  160.2 0.9 convolution_convert_fusion.8
  (14 shorter events, 0.4 us)
Async XLA Ops:
  0.6 51.9 %copy-start = (bf16[2,1280,160]{1,2,0:T(8,128)(2,1)S(1)}, bf16[2,1280,160]{1,2,0:T(8,128)(2,1)}, u32[]{:S(2)}) copy-start(bf16[2,1280,160]{1,2,0:T(8,128)(2,1)} %param.12) | copy-start | bytes 2457604
  6.4 3.1 %collective-permute-start = (bf16[1,8,1280]{2,1,0:T(8,128)(2,1)S(1)}, bf16[1,8,1280]{2,1,0:T(8,128)(2,1)S(1)}, u32[]{:S(2)}, u32[]{:S(2)}) collective-permute-start(bf16[1,8,1280]{2,1,0:T(8,128)(2,1)S(1)} %get-tuple-element.60), channel_id=1, source_target_pairs={{0,1},{1,0},{2,3},{3,2},{4,5},{5,4},{6,7},{7,6},{8,9},{9,8},{10,11... | collective-permute-start | bytes 61448 | tf_op jit(solution)/shard_map/ppermute | solution.py:39
  8.3 42.7 %copy-start.7 = (bf16[256,256]{1,0:T(8,128)(2,1)S(1)}, bf16[256,256]{1,0:T(8,128)(2,1)}, u32[]{:S(2)}) copy-start(bf16[256,256]{1,0:T(8,128)(2,1)} %constant.144.clone) | copy-start | bytes 393220
  9.5 21.7 %collective-permute-start.1 = (bf16[16,1280]{1,0:T(8,128)(2,1)S(1)}, bf16[16,1280]{1,0:T(8,128)(2,1)S(1)}, u32[]{:S(2)}, u32[]{:S(2)}) collective-permute-start(bf16[16,1280]{1,0:T(8,128)(2,1)S(1)} %maximum_bitcast_fusion), channel_id=1, source_target_pairs={{0,0},{1,1},{2,2},{3,3},{4,4},{5,5},{6,6},{7,7},{8,8},{9,9},{10,10... | collective-permute-start | bytes 122888 | tf_op jit(solution)/shard_map/ppermute | solution.py:31
  51.0 1.1 copy-start.3
  53.0 0.8 copy-start.9
  53.3 0.9 copy-start.8
  54.2 14.4 %copy-start.11 = (bf16[16,256]{1,0:T(8,128)(2,1)S(1)}, bf16[16,256]{1,0:T(8,128)(2,1)}, u32[]{:S(2)}) copy-start(bf16[16,256]{1,0:T(8,128)(2,1)} %constant.146.clone) | copy-start | bytes 24580
  68.8 22.3 %collective-permute-start.3 = (bf16[16,1280]{1,0:T(8,128)(2,1)S(1)}, bf16[16,1280]{1,0:T(8,128)(2,1)S(1)}, u32[]{:S(2)}, u32[]{:S(2)}) collective-permute-start(bf16[16,1280]{1,0:T(8,128)(2,1)S(1)} %fusion.5), channel_id=1, source_target_pairs={{0,128},{1,129},{2,130},{3,131},{4,132},{5,133},{6,134},{7,135},{8... | collective-permute-start | bytes 122888 | tf_op jit(solution)/shard_map/ppermute | solution.py:31
  84.2 9.8 %collective-permute-start.2 = (bf16[16,1280]{1,0:T(8,128)(2,1)S(1)}, bf16[16,1280]{1,0:T(8,128)(2,1)S(1)}, u32[]{:S(2)}, u32[]{:S(2)}) collective-permute-start(bf16[16,1280]{1,0:T(8,128)(2,1)S(1)} %fusion.5), channel_id=1, source_target_pairs={{0,0},{1,1},{2,2},{3,3},{4,4},{5,5},{6,6},{7,7},{8,8},{9,9},{10,10... | collective-permute-start | bytes 122888 | tf_op jit(solution)/shard_map/ppermute | solution.py:31
  112.1 1.3 copy-start.1
  112.4 1.5 copy-start.6
  112.5 1.7 %copy-start.2 = (bf16[2,256,1280]{2,1,0:T(8,128)(2,1)S(1)}, bf16[2,256,1280]{2,1,0:T(8,128)(2,1)}, u32[]{:S(2)}) copy-start(bf16[2,256,1280]{2,1,0:T(8,128)(2,1)} %cotangent_ref.1) | copy-start | bytes 3932164
  113.9 0.9 copy-start.5
  115.1 15.4 %copy-start.12 = (bf16[16,128]{1,0:T(8,128)(2,1)S(1)}, bf16[16,128]{1,0:T(8,128)(2,1)}, u32[]{:S(2)}) copy-start(bf16[16,128]{1,0:T(8,128)(2,1)} %constant.147.clone) | copy-start | bytes 12292
  115.9 15.5 %copy-start.4 = (bf16[1280,64]{0,1:T(8,128)(2,1)S(1)}, bf16[1280,64]{0,1:T(8,128)(2,1)}, u32[]{:S(2)}) copy-start(bf16[1280,64]{0,1:T(8,128)(2,1)} %param.11) | copy-start | bytes 491524
  115.9 14.6 %all-to-all-start.3 = ((bf16[8,16,1280]{2,1,0:T(8,128)(2,1)}), bf16[8,16,1280]{2,1,0:T(8,128)(2,1)S(1)}, u32[]{:S(2)}, u32[]{:S(2)}) async-start(bf16[8,16,1280]{2,1,0:T(8,128)(2,1)} %broadcast_in_dim.12), calls=%async_computation.3 | async-start | bytes 655360 | tf_op jit(solution)/shard_map/all_to_all | solution.py:71
  130.7 2.3 %collective-permute-start.4 = (bf16[16,1280]{1,0:T(8,128)(2,1)S(1)}, bf16[16,1280]{1,0:T(8,128)(2,1)S(1)}, u32[]{:S(2)}, u32[]{:S(2)}) collective-permute-start(bf16[16,1280]{1,0:T(8,128)(2,1)S(1)} %fusion.6), channel_id=1, source_target_pairs={{0,0},{1,1},{2,2},{3,3},{4,4},{5,5},{6,6},{7,7},{8,8},{9,9},{10,10... | collective-permute-start | bytes 122888 | tf_op jit(solution)/shard_map/ppermute | solution.py:31
  133.0 27.1 %copy-start.10 = (bf16[64,256]{1,0:T(8,128)(2,1)S(1)}, bf16[64,256]{1,0:T(8,128)(2,1)}, u32[]{:S(2)}) copy-start(bf16[64,256]{1,0:T(8,128)(2,1)} %constant.148.clone) | copy-start | bytes 98308

commit v5 on v4

v5 whole, which is shorter than its diff:
```python
import jax
import jax.numpy as jnp
import numpy as np
from jax import lax
from jax.experimental import pallas as pl
from jax.experimental.pallas import tpu as pltpu
from jax.sharding import Mesh, PartitionSpec as P

ALL = ("y", "zh", "x", "zq", "zr", "c")
PLANE = ("y", "x")
EXP = ("zq", "zr", "c")
REP = ("y", "zh", "x")
BF = jnp.bfloat16
F32 = jnp.float32


def signed(r):
    return r if r <= 8 else r - 16


def shifted(value, shift):
    pairs = []
    for y in range(4):
        for x in range(4):
            for z in range(32):
                for c in range(2):
                    to = (z + shift(y, x, c)) % 32
                    source = (((y * 2 + z // 16) * 4 + x) * 16 + z % 16) * 2 + c
                    target = (((y * 2 + to // 16) * 4 + x) * 16 + to % 16) * 2 + c
                    pairs.append((source, target))
    return lax.ppermute(value, ALL, pairs)


def out_shift(y, x, c):
    return signed(4 * y + x) * (1 - 2 * c)


def spread(rows):
    out = jnp.broadcast_to(rows[None], (16,) + rows.shape).reshape((32,) + rows.shape[1:])
    return lax.all_to_all(out, PLANE + ("c",), 0, 0, tiled=True)


def chooser(index, size):
    return (index[:, None] == jnp.arange(size)[None, :]).astype(BF)


def picked(choose, rows):
    return jnp.dot(choose, rows, preferred_element_type=F32).astype(BF)


def added(rows, groups, inner):
    to, source = np.arange(groups * inner), np.arange(rows.shape[0])
    span = rows.shape[0] // groups
    same = (source[None, :] // span == to[:, None] // inner) & (source[None, :] % inner == to[:, None] % inner)
    return jnp.dot(jnp.asarray(same.astype(BF)), rows, preferred_element_type=F32).astype(BF)


def tied(*values):
    return lax.optimization_barrier(values)


def gathered(value, axes, size):
    out = jnp.broadcast_to(value[None], (size,) + value.shape)
    return lax.all_to_all(out, axes, 0, 0, tiled=True)


def front_body(place_ref, tokens_ref, cotangent_ref, proj_ref, sent_ref, dispatch_ref, combine_ref, rows_ref):
    for image in range(2):
        tokens = tokens_ref[image]
        logits = lax.dot_general(proj_ref[...], tokens, (((1,), (1,)), ((), ())), preferred_element_type=F32)
        raised = jnp.exp(logits - jnp.max(logits, axis=1, keepdims=True))
        dispatch = raised / jnp.sum(raised, axis=1, keepdims=True)
        raised = jnp.exp(logits - jnp.max(logits, axis=0, keepdims=True))
        combine = raised / jnp.sum(raised, axis=0, keepdims=True)
        dispatch_ref[image] = dispatch
        combine_ref[image] = combine
        rows_ref[64 * image : 64 * image + 64, :] = jnp.dot(
            dispatch.astype(BF), tokens, preferred_element_type=F32
        ).astype(BF)
        rows_ref[64 * image + 128 : 64 * image + 192, :] = jnp.dot(
            combine.astype(BF), cotangent_ref[image], preferred_element_type=F32
        ).astype(BF)
    z_lo, column, core = place_ref[0], place_ref[1], place_ref[2]
    row = lax.broadcasted_iota(jnp.int32, (16, 256), 0)
    target = (z_lo + (1 - 2 * core) * column) & 15
    wanted = ((row >> 2) & 1) * 128 + (row & 1) * 64 + 4 * target + (row >> 3) * 2 + ((row >> 1) & 1)
    choose = (wanted == lax.broadcasted_iota(jnp.int32, (16, 256), 1)).astype(F32).astype(BF)
    sent_ref[...] = jnp.dot(choose, rows_ref[...], preferred_element_type=F32).astype(BF)


def front(place, tokens, cotangent, proj):
    width = tokens.shape[2]
    vmem = pl.BlockSpec(memory_space=pltpu.VMEM)
    return pl.pallas_call(
        front_body,
        in_specs=[pl.BlockSpec(memory_space=pltpu.SMEM), vmem, vmem, vmem],
        out_specs=[vmem, vmem, vmem],
        out_shape=[
            jax.ShapeDtypeStruct((16, width), BF),
            jax.ShapeDtypeStruct((2, 64, 256), F32),
            jax.ShapeDtypeStruct((2, 64, 256), F32),
        ],
        scratch_shapes=[pltpu.VMEM((256, width), BF)],
        compiler_params=pltpu.CompilerParams(vmem_limit_bytes=56 * 2**20),
    )(place, tokens, cotangent, proj)


def experts_body(place_ref, got_ref, first_ref, second_ref, out_ref, rows_ref, hidden_ref, grad_ref, parts_ref):
    which = pl.program_id(0)
    row = lax.broadcasted_iota(jnp.int32, (128, 256), 0)
    wanted = ((row >> 1) & 31) * 8 + (row >> 6) * 4 + which * 2 + (row & 1)
    choose = (wanted == lax.broadcasted_iota(jnp.int32, (128, 256), 1)).astype(F32).astype(BF)
    rows = jnp.dot(choose, got_ref[...], preferred_element_type=F32).astype(BF)
    rows_ref[0] = rows
    slots, cotangents = rows[:64], rows[64:]
    first, second = first_ref[0], second_ref[0]
    turned = (((1,), (1,)), ((), ()))
    v = lax.dot_general(slots, first, turned, preferred_element_type=F32)
    hidden_grad = lax.dot_general(cotangents, second, turned, preferred_element_type=F32)
    root = 0.7978845608028654
    square = v * v
    t = jnp.tanh(root * v * (1.0 + 0.044715 * square))
    hidden = (0.5 * v * (1.0 + t)).astype(BF)
    slope = 0.5 * (1.0 + t) + 0.5 * v * (1.0 - t * t) * (root * (1.0 + 3.0 * 0.044715 * square))
    pre_grad = (hidden_grad * slope).astype(BF)
    hidden_ref[0] = hidden
    grad_ref[0] = pre_grad
    start = pl.multiple_of(which * 128, 128)
    parts_ref[pl.ds(start, 64), :] = jnp.dot(hidden, second, preferred_element_type=F32).astype(BF)
    parts_ref[pl.ds(start + 64, 64), :] = jnp.dot(pre_grad, first, preferred_element_type=F32).astype(BF)

    @pl.when(which == 1)
    def _():
        core = place_ref[2]
        row = lax.broadcasted_iota(jnp.int32, (256, 256), 0)
        other = (row >> 3) & 1
        to = row >> 4
        source = jnp.where(other == 1, (16 - to) & 15, to)
        image_core = jnp.where(other == 1, 1 - core, core)
        wanted = ((row >> 1) & 1) * 128 + ((row >> 2) & 1) * 64 + source * 4 + image_core * 2 + (row & 1)
        choose = (wanted == lax.broadcasted_iota(jnp.int32, (256, 256), 1)).astype(F32).astype(BF)
        out_ref[...] = jnp.dot(choose, parts_ref[...], preferred_element_type=F32).astype(BF)


def experts(place, got, first, second):
    width = got.shape[1]
    units = first.shape[1]
    whole = pl.BlockSpec((256, width), lambda i: (0, 0))
    weight = pl.BlockSpec((1, units, width), lambda i: (i, 0, 0))
    act = pl.BlockSpec((1, 64, units), lambda i: (i, 0, 0))
    return pl.pallas_call(
        experts_body,
        grid=(2,),
        in_specs=[pl.BlockSpec(memory_space=pltpu.SMEM), whole, weight, weight],
        out_specs=[whole, pl.BlockSpec((1, 128, width), lambda i: (i, 0, 0)), act, act],
        out_shape=[
            jax.ShapeDtypeStruct((256, width), BF),
            jax.ShapeDtypeStruct((2, 128, width), BF),
            jax.ShapeDtypeStruct((2, 64, units), BF),
            jax.ShapeDtypeStruct((2, 64, units), BF),
        ],
        scratch_shapes=[pltpu.VMEM((256, width), BF)],
        compiler_params=pltpu.CompilerParams(vmem_limit_bytes=24 * 2**20),
    )(place, got, first, second)


def on_device(tokens, slot_proj, in_weight, out_weight, out_grad):
    width = tokens.shape[2]
    column = lax.axis_index("y") * 4 + lax.axis_index("x")
    core = lax.axis_index("c")
    z_lo = lax.axis_index("zq") * 4 + lax.axis_index("zr")
    row = jnp.arange(256)
    expert = row % 64
    core_of = (expert // 2) % 2
    source = ((1 - 2 * core_of) * (expert // 4 - z_lo)) % 16
    by_image = chooser(
        source * 16 + core_of * 8 + row // 128 * 4 + expert % 2 * 2 + (row // 64) % 2, 256
    )

    place = jnp.stack([z_lo, column, core]).astype(jnp.int32)
    outgoing, dispatch, combine = front(place, tokens, out_grad, slot_proj.T)
    dispatch, combine = jnp.swapaxes(dispatch, 1, 2), jnp.swapaxes(combine, 1, 2)
    dispatch_b, combine_b = dispatch.astype(BF), combine.astype(BF)
    sent = shifted(outgoing, out_shift)
    sent, by_image, first, dispatch_b, combine_b, leading = tied(
        sent, by_image, lax.axis_index("y") * 16, dispatch_b, combine_b, core == 0
    )
    got = spread(sent.reshape(2, 8, width)).reshape(256, width)
    parts, rows, hidden, pre_grad = experts(place, got, jnp.swapaxes(in_weight, 1, 2), out_weight)
    scattered = lax.all_to_all(parts.reshape(16, 16, width), PLANE, 0, 0, tiled=True)
    summed = added(scattered.reshape(256, width), 1, 16)
    near = shifted(summed, lambda y, x, c: -out_shift(y, x, c))
    far = shifted(summed, lambda y, x, c: 16 - out_shift(y, x, c))
    home = (near.astype(F32) + far.astype(F32)).astype(BF)
    mine = home.reshape(2, 8, width)
    back = spread(jnp.where(leading, mine, mine[::-1])).reshape(256, width)
    results = picked(by_image, back).reshape(2, 2, 64, width)
    expert_out, slot_grad = results[0], results[1]
    combine_grad = jnp.einsum("itd,ied->ite", out_grad, expert_out, preferred_element_type=F32)
    dispatch_grad = jnp.einsum("itd,ied->ite", tokens, slot_grad, preferred_element_type=F32)
    from_dispatch = dispatch * (dispatch_grad - jnp.sum(dispatch * dispatch_grad, axis=1, keepdims=True))
    from_combine = combine * (combine_grad - jnp.sum(combine * combine_grad, axis=2, keepdims=True))
    logit_grad = (from_dispatch + from_combine).astype(BF)
    own = lax.dynamic_slice(logit_grad, (0, 0, first), (2, 256, 16), allow_negative_indices=False)
    mine = jnp.einsum("ite,itd->ed", own, tokens, preferred_element_type=F32).astype(BF)
    mixed = jnp.einsum("ite,ied->itd", combine_b, expert_out, preferred_element_type=F32).astype(BF)
    mine = added(gathered(mine, ("zr", "c"), 8).reshape(128, width), 1, 16)
    mine, mixed = tied(mine, mixed)
    mine = shifted(mine, lambda y, x, c: 4 * (0, 1, 2, -1)[x] * (1 - 2 * c))
    mine, logit_grad, slot_grad, rows, hidden, pre_grad = tied(mine, logit_grad, slot_grad, rows, hidden, pre_grad)
    shares = gathered(mine, PLANE, 16).reshape(256, width)
    slots, cotangents = rows[:, :64], rows[:, 64:]
    out_weight_grad = jnp.einsum("erf,erd->efd", hidden, cotangents, preferred_element_type=F32).astype(BF)
    in_weight_grad = jnp.einsum("erd,erf->edf", slots, pre_grad, preferred_element_type=F32).astype(BF)
    weights = jnp.concatenate([dispatch_b, logit_grad], axis=2)
    vectors = jnp.concatenate([slot_grad, jnp.broadcast_to(slot_proj.T, (2, 64, width))], axis=1)
    token_grad = jnp.einsum("itk,ikd->itd", weights, vectors, preferred_element_type=F32).astype(BF)
    proj_grad = added(shares, 4, 16).T
    return (mixed, token_grad, proj_grad, in_weight_grad, out_weight_grad)


def solution(mesh):
    fine = Mesh(mesh.devices.reshape(4, 2, 4, 4, 4, 2), ALL)
    images, first, second = P(EXP, None, None), P(EXP, None, REP), P(EXP, REP, None)
    return jax.shard_map(
        on_device,
        mesh=fine,
        in_specs=(images, P(), first, second, images),
        out_specs=(images, images, P(), first, second),
        check_vma=False,
    )
```

time: 163 us -> 163 us (level)
  blocking collectives: 78.9 us -> 57.4 us
  starting transfers between devices: 45.8 us -> 61.4 us
  waiting for transfers between devices: 14 us -> 21.1 us
  matrix products: 11.1 us -> 8.73 us
  Pallas kernels: 4.44 us -> 6.41 us
    all_to_all x4 -> x3, blocking collectives: 78.9 us -> 57.4 us  [the longest x2 40.8 us: spread(): return lax.all_to_all(out, PLANE + ('c',), 0, 0, tiled=True)]
    all_to_all x1 -> x2, starting transfers between devices: 3.56 us -> 23 us  [gathered(): return lax.all_to_all(out, axes, 0, 0, tiled=True)]
    all_to_all x1 -> x2, waiting for transfers between devices: 9.46 us -> 14.3 us  [gathered(): return lax.all_to_all(out, axes, 0, 0, tiled=True)]
    ppermute x4, waiting for transfers between devices: 4.44 us -> 6.82 us  [shifted(): return lax.ppermute(value, ALL, pairs)]
    pallas_call x1 -> x2, Pallas kernels: 4.44 us -> 6.41 us  [the longest x1 3.93 us: front(): pl.pallas_call(front_body, in_specs=[pl.BlockSpec(memory_space=pltpu.SMEM...]
    ppermute x1 -> x0, starting transfers between devices: 1.91 us -> none  [swapped(): lax.ppermute(rows[1:], 'c', [(0, 1), (1, 0)])]
    ppermute x4, starting transfers between devices: 40.3 us -> 38.5 us  [shifted(): return lax.ppermute(value, ALL, pairs)]
    dot_general x6 -> x2, matrix products: 3.99 us -> 2.61 us  [the longest x1 1.31 us: on_device(): jnp.einsum('erd,erf->edf', slots, pre_grad, preferred_element_type=F32)]
  transfers between devices with their start and end apart: 6 -> 6, of which waited for: 4 -> 5; matrix products, arithmetic and copies ran while one was open for 4% -> 4% of each run, Pallas kernels for 0% -> 0%
where the time goes in v5:
time: 163 us; the launch traced here: 161 us
  starting transfers between devices  61.4 us (38%)
  blocking collectives  57.4 us (35%)
  waiting for transfers between devices  21.1 us (13%)
  matrix products  8.73 us (5%)
  Pallas kernels  6.41 us (4%)
  local copies, waits for them, and re-layouts  2.88 us (2%)
  other arithmetic  1.96 us (1%)
    all_to_all x2, blocking collectives, spread(): return lax.all_to_all(out, PLANE + ('c',), 0, 0, tiled=True)  40.8 us
    ppermute x4, starting transfers between devices, shifted(): return lax.ppermute(value, ALL, pairs)  38.5 us
    all_to_all x2, starting transfers between devices, gathered(): return lax.all_to_all(out, axes, 0, 0, tiled=True)  23 us
    all_to_all x1, blocking collectives, on_device(): lax.all_to_all(parts.reshape(16, 16, width), PLANE, 0, 0, tiled=True)  16.6 us
    all_to_all x2, waiting for transfers between devices, gathered(): return lax.all_to_all(out, axes, 0, 0, tiled=True)  14.3 us
    ppermute x4, waiting for transfers between devices, shifted(): return lax.ppermute(value, ALL, pairs)  6.82 us
    pallas_call x1, Pallas kernels, front(): pl.pallas_call(front_body, in_specs=[pl.BlockSpec(memory_space=pltpu.SMEM...  3.93 us
  transfers between devices with their start and end apart: 6, of which 5 were waited for; matrix products, arithmetic and copies ran while one was open for 4% of the time, Pallas kernels for 0%

profile of v5, /device:TPU:24, one launch (start us, length us, event | category | flops | bytes accessed | tf_op | source)
XLA Modules:
  0.0 160.8 jit_solution(2640135609502848690)
XLA Ops:
  0.6 0.6 pad_add_fusion.place_ref
  1.2 3.9 %shard_map.119 = (bf16[16,1280]{1,0:T(8,128)(2,1)}, f32[2,64,256]{2,1,0:T(8,128)}, f32[2,64,256]{2,1,0:T(8,128)}) custom-call(s32[3]{0:T(128)} %pad_add_fusion.place_ref, bf16[2,256,1280]{2,1,0:T(8,128)(2,1)} %tokens_ref.1, bf16[2,256,1280]{2,1,0:T(8,128)(2,1)} %cotangent_ref.1, bf16[64,1280]{1,0:T(8,128)(2,1)} %bitcast.74), custom_call_target="tpu_custom_call" | custom-call | tf_op jit(solution)/shard_map/pallas_call | solution.py:94
  5.1 0.0 copy-start
  5.1 0.0 copy-start.1
  5.1 0.0 copy-start.2
  5.1 20.1 %collective-permute-start = (bf16[16,1280]{1,0:T(8,128)(2,1)}, bf16[16,1280]{1,0:T(8,128)(2,1)S(1)}, u32[]{:S(2)}, u32[]{:S(2)}) collective-permute-start(bf16[16,1280]{1,0:T(8,128)(2,1)} %get-tuple-element.27), channel_id=1, source_target_pairs={{0,0},{1,1},{2,2},{3,3},{4,4},{5,5},{6,6},{7,7},{8,8},{9,9},{10,10... | collective-permute-start | bytes 122888 | tf_op jit(solution)/shard_map/ppermute | solution.py:31
  25.3 1.0 bitcast_convert_fusion
  26.3 0.1 fusion.17
  26.4 0.8 collective-permute-done
  27.3 21.0 %all_to_all.25 = bf16[32,8,1280]{2,1,0:T(8,128)(2,1)S(1)} all-to-all(bf16[32,8,1280]{2,1,0:T(8,128)(2,1)S(1)} %bitcast.71), channel_id=1, replica_groups=mesh['y'=4,'zh'=2,'x'=4,'zq'=4,'zr'=4,'c'=2] {'y','x','c'}, dimensions={0} | all-to-all | bytes 1310720 | tf_op jit(solution)/shard_map/all_to_all | solution.py:40
  48.3 0.0 copy-done
  48.3 0.0 copy-done.1
  48.3 0.0 copy-done.2
  48.3 0.0 copy-start.9
  48.3 2.5 %shard_map.120 = (bf16[256,1280]{1,0:T(8,128)(2,1)S(1)}, bf16[2,128,1280]{2,1,0:T(8,128)(2,1)S(1)}, bf16[2,64,160]{2,1,0:T(8,128)(2,1)S(1)}, bf16[2,64,160]{2,1,0:T(8,128)(2,1)S(1)}) custom-call(s32[3]{0:T(128)S(1)} %copy-done.2, bf16[256,1280]{1,0:T(8,128)(2,1)S(1)} %bitcast.62, bf16[2,160,1280]{2,1,0:T(8,128)(2,1)S(1)} %bitcast.63, ...), custom_call_target="tpu_custom_call" | custom-call | tf_op jit(solution)/shard_map/pallas_call | solution.py:151
  50.8 16.6 %all_to_all.26 = bf16[16,16,1280]{2,1,0:T(8,128)(2,1)S(1)} all-to-all(bf16[16,16,1280]{2,1,0:T(8,128)(2,1)S(1)} %bitcast.64), channel_id=1, replica_groups=mesh['y'=4,'zh'=2,'x'=4,'zq'=4,'zr'=4,'c'=2] {'y','x'}, dimensions={0} | all-to-all | bytes 1310720 | tf_op jit(solution)/shard_map/all_to_all | solution.py:190
  67.5 0.0 copy-done.9
  67.5 0.2 fusion.3
  67.7 13.4 %collective-permute-start.2 = (bf16[16,1280]{1,0:T(8,128)(2,1)S(1)}, bf16[16,1280]{1,0:T(8,128)(2,1)S(1)}, u32[]{:S(2)}, u32[]{:S(2)}) collective-permute-start(bf16[16,1280]{1,0:T(8,128)(2,1)S(1)} %fusion.3), channel_id=1, source_target_pairs={{0,128},{1,129},{2,130},{3,131},{4,132},{5,133},{6,134},{7,135},{8... | collective-permute-start | bytes 122888 | tf_op jit(solution)/shard_map/ppermute | solution.py:31
  81.1 4.3 %collective-permute-start.1 = (bf16[16,1280]{1,0:T(8,128)(2,1)S(1)}, bf16[16,1280]{1,0:T(8,128)(2,1)S(1)}, u32[]{:S(2)}, u32[]{:S(2)}) collective-permute-start(bf16[16,1280]{1,0:T(8,128)(2,1)S(1)} %fusion.3), channel_id=1, source_target_pairs={{0,0},{1,1},{2,2},{3,3},{4,4},{5,5},{6,6},{7,7},{8,8},{9,9},{10,10... | collective-permute-start | bytes 122888 | tf_op jit(solution)/shard_map/ppermute | solution.py:31
  85.4 2.2 %collective-permute-done.2 = bf16[16,1280]{1,0:T(8,128)(2,1)S(1)} collective-permute-done((bf16[16,1280]{1,0:T(8,128)(2,1)S(1)}, bf16[16,1280]{1,0:T(8,128)(2,1)S(1)}, u32[]{:S(2)}, u32[]{:S(2)}) %collective-permute-start.2) | collective-permute-done | bytes 40992 | tf_op jit(solution)/shard_map/ppermute | solution.py:31
  87.6 3.8 %collective-permute-done.1 = bf16[16,1280]{1,0:T(8,128)(2,1)S(1)} collective-permute-done((bf16[16,1280]{1,0:T(8,128)(2,1)S(1)}, bf16[16,1280]{1,0:T(8,128)(2,1)S(1)}, u32[]{:S(2)}, u32[]{:S(2)}) %collective-permute-start.1) | collective-permute-done | bytes 40992 | tf_op jit(solution)/shard_map/ppermute | solution.py:31
  91.4 19.7 %all_to_all.27 = bf16[32,8,1280]{2,1,0:T(8,128)(2,1)S(1)} all-to-all(bf16[32,8,1280]{2,1,0:T(8,128)(2,1)S(1)} %bitcast.72), channel_id=1, replica_groups=mesh['y'=4,'zh'=2,'x'=4,'zq'=4,'zr'=4,'c'=2] {'y','x','c'}, dimensions={0} | all-to-all | bytes 1310720 | tf_op jit(solution)/shard_map/all_to_all | solution.py:40
  111.2 0.0 copy-start.3
  111.2 0.3 convolution_convert_fusion.4
  111.5 0.0 copy-start.7
  111.6 0.0 copy-start.4
  111.6 0.9 copy-done.3
  112.5 0.5 convolution_bitcast_fusion.2
  113.0 0.0 copy-done.7
  113.0 0.0 copy-start.6
  113.0 0.2 fusion.9
  113.2 0.0 copy-done.4
  113.2 0.5 convolution_bitcast_fusion.1
  113.8 0.2 copy-done.6
  114.0 0.3 fusion.2
  114.2 0.0 copy-start.10
  114.2 0.8 broadcast_in_dim.15
  115.0 3.4 %all-to-all-start.3 = ((bf16[8,16,1280]{2,1,0:T(8,128)(2,1)}), bf16[8,16,1280]{2,1,0:T(8,128)(2,1)S(1)}, u32[]{:S(2)}, u32[]{:S(2)}) async-start(bf16[8,16,1280]{2,1,0:T(8,128)(2,1)} %broadcast_in_dim.15), calls=%async_computation.3 | async-start | bytes 655360 | tf_op jit(solution)/shard_map/all_to_all | solution.py:64
  118.4 1.6 convolution_convert_fusion.1
  120.0 0.0 copy-start.5
  120.0 9.5 %all-to-all-done.3 = bf16[8,16,1280]{2,1,0:T(8,128)(2,1)S(1)} async-done(((bf16[8,16,1280]{2,1,0:T(8,128)(2,1)}), bf16[8,16,1280]{2,1,0:T(8,128)(2,1)S(1)}, u32[]{:S(2)}, u32[]{:S(2)}) %all-to-all-start.3) | async-done | bytes 327712 | tf_op jit(solution)/shard_map/all_to_all | solution.py:64
  129.5 0.0 copy-done.10
  129.5 0.2 fusion.4
  129.7 0.7 collective-permute-start.3
  130.3 0.0 collective-permute-done.3
  130.3 0.9 broadcast_in_dim.17
  131.2 19.5 %all-to-all-start.4 = ((bf16[16,16,1280]{2,1,0:T(8,128)(2,1)}), bf16[16,16,1280]{2,1,0:T(8,128)(2,1)S(1)}, u32[]{:S(2)}, u32[]{:S(2)}) async-start(bf16[16,16,1280]{2,1,0:T(8,128)(2,1)} %broadcast_in_dim.17), calls=%async_computation.4 | async-start | bytes 1310720 | tf_op jit(solution)/shard_map/all_to_all | solution.py:64
  150.8 0.0 copy-done.5
  150.8 1.6 convolution_convert_fusion
  152.4 0.0 copy-start.8
  152.4 1.3 convolution_convert_fusion.3
  153.7 1.3 convolution_convert_fusion.2
  155.0 4.8 %all-to-all-done.4 = bf16[16,16,1280]{2,1,0:T(8,128)(2,1)S(1)} async-done(((bf16[16,16,1280]{2,1,0:T(8,128)(2,1)}), bf16[16,16,1280]{2,1,0:T(8,128)(2,1)S(1)}, u32[]{:S(2)}, u32[]{:S(2)}) %all-to-all-start.4) | async-done | bytes 655392 | tf_op jit(solution)/shard_map/all_to_all | solution.py:64
  159.8 0.0 copy-done.8
  159.8 0.9 convolution_convert_fusion.5
  (8 shorter events, 0.3 us)
Async XLA Ops:
  5.1 43.2 %copy-start = (bf16[2,1280,160]{1,2,0:T(8,128)(2,1)S(1)}, bf16[2,1280,160]{1,2,0:T(8,128)(2,1)}, u32[]{:S(2)}) copy-start(bf16[2,1280,160]{1,2,0:T(8,128)(2,1)} %param.10) | copy-start | bytes 2457604
  5.1 43.2 %copy-start.1 = (bf16[2,160,1280]{2,1,0:T(8,128)(2,1)S(1)}, bf16[2,160,1280]{2,1,0:T(8,128)(2,1)}, u32[]{:S(2)}) copy-start(bf16[2,160,1280]{2,1,0:T(8,128)(2,1)} %second_ref.1) | copy-start | bytes 2457604
  5.1 43.2 %copy-start.2 = (s32[3]{0:T(128)S(1)}, s32[3]{0:T(128)}, u32[]{:S(2)}) copy-start(s32[3]{0:T(128)} %pad_add_fusion.place_ref) | copy-start | bytes 40
  5.1 22.1 %collective-permute-start = (bf16[16,1280]{1,0:T(8,128)(2,1)}, bf16[16,1280]{1,0:T(8,128)(2,1)S(1)}, u32[]{:S(2)}, u32[]{:S(2)}) collective-permute-start(bf16[16,1280]{1,0:T(8,128)(2,1)} %get-tuple-element.27), channel_id=1, source_target_pairs={{0,0},{1,1},{2,2},{3,3},{4,4},{5,5},{6,6},{7,7},{8,8},{9,9},{10,10... | collective-permute-start | bytes 122888 | tf_op jit(solution)/shard_map/ppermute | solution.py:31
  48.3 19.1 %copy-start.9 = (bf16[16,256]{1,0:T(8,128)(2,1)S(1)}, bf16[16,256]{1,0:T(8,128)(2,1)}, u32[]{:S(2)}) copy-start(bf16[16,256]{1,0:T(8,128)(2,1)} %constant.128.clone) | copy-start | bytes 24580
  67.7 19.9 %collective-permute-start.2 = (bf16[16,1280]{1,0:T(8,128)(2,1)S(1)}, bf16[16,1280]{1,0:T(8,128)(2,1)S(1)}, u32[]{:S(2)}, u32[]{:S(2)}) collective-permute-start(bf16[16,1280]{1,0:T(8,128)(2,1)S(1)} %fusion.3), channel_id=1, source_target_pairs={{0,128},{1,129},{2,130},{3,131},{4,132},{5,133},{6,134},{7,135},{8... | collective-permute-start | bytes 122888 | tf_op jit(solution)/shard_map/ppermute | solution.py:31
  81.1 10.3 %collective-permute-start.1 = (bf16[16,1280]{1,0:T(8,128)(2,1)S(1)}, bf16[16,1280]{1,0:T(8,128)(2,1)S(1)}, u32[]{:S(2)}, u32[]{:S(2)}) collective-permute-start(bf16[16,1280]{1,0:T(8,128)(2,1)S(1)} %fusion.3), channel_id=1, source_target_pairs={{0,0},{1,1},{2,2},{3,3},{4,4},{5,5},{6,6},{7,7},{8,8},{9,9},{10,10... | collective-permute-start | bytes 122888 | tf_op jit(solution)/shard_map/ppermute | solution.py:31
  111.2 1.3 copy-start.3
  111.5 1.5 copy-start.7
  111.6 1.7 %copy-start.4 = (bf16[2,256,1280]{2,1,0:T(8,128)(2,1)S(1)}, bf16[2,256,1280]{2,1,0:T(8,128)(2,1)}, u32[]{:S(2)}) copy-start(bf16[2,256,1280]{2,1,0:T(8,128)(2,1)} %cotangent_ref.1) | copy-start | bytes 3932164
  113.0 0.9 copy-start.6
  114.2 15.3 %copy-start.10 = (bf16[16,128]{1,0:T(8,128)(2,1)S(1)}, bf16[16,128]{1,0:T(8,128)(2,1)}, u32[]{:S(2)}) copy-start(bf16[16,128]{1,0:T(8,128)(2,1)} %constant.129.clone) | copy-start | bytes 12292
  115.0 14.5 %all-to-all-start.3 = ((bf16[8,16,1280]{2,1,0:T(8,128)(2,1)}), bf16[8,16,1280]{2,1,0:T(8,128)(2,1)S(1)}, u32[]{:S(2)}, u32[]{:S(2)}) async-start(bf16[8,16,1280]{2,1,0:T(8,128)(2,1)} %broadcast_in_dim.15), calls=%async_computation.3 | async-start | bytes 655360 | tf_op jit(solution)/shard_map/all_to_all | solution.py:64
  120.0 30.7 %copy-start.5 = (bf16[1280,64]{0,1:T(8,128)(2,1)S(1)}, bf16[1280,64]{0,1:T(8,128)(2,1)}, u32[]{:S(2)}) copy-start(bf16[1280,64]{0,1:T(8,128)(2,1)} %param.9) | copy-start | bytes 491524
  129.7 0.7 collective-permute-start.3
  131.2 28.6 %all-to-all-start.4 = ((bf16[16,16,1280]{2,1,0:T(8,128)(2,1)}), bf16[16,16,1280]{2,1,0:T(8,128)(2,1)S(1)}, u32[]{:S(2)}, u32[]{:S(2)}) async-start(bf16[16,16,1280]{2,1,0:T(8,128)(2,1)} %broadcast_in_dim.17), calls=%async_computation.4 | async-start | bytes 1310720 | tf_op jit(solution)/shard_map/all_to_all | solution.py:64
  152.4 7.5 %copy-start.8 = (bf16[64,256]{1,0:T(8,128)(2,1)S(1)}, bf16[64,256]{1,0:T(8,128)(2,1)}, u32[]{:S(2)}) copy-start(bf16[64,256]{1,0:T(8,128)(2,1)} %constant.130.clone) | copy-start | bytes 98308

commit v6 on v5

--- a/solution.py
+++ b/solution.py
@@ -24,15 +24,19 @@
         for x in range(4):
             for z in range(32):
                 for c in range(2):
-                    to = (z + shift(y, x, c)) % 32
+                    to = (z + shift(y, x, z, c)) % 32
                     source = (((y * 2 + z // 16) * 4 + x) * 16 + z % 16) * 2 + c
                     target = (((y * 2 + to // 16) * 4 + x) * 16 + to % 16) * 2 + c
                     pairs.append((source, target))
     return lax.ppermute(value, ALL, pairs)
 
 
-def out_shift(y, x, c):
+def out_shift(y, x, z, c):
     return signed(4 * y + x) * (1 - 2 * c)
+
+
+def group_shift(y, x, z, c):
+    return (0, 4 - 8 * c, 6 if z % 4 >= 2 else -6, 8 * c - 4)[x]
 
 
 def spread(rows):
@@ -189,8 +193,8 @@
     parts, rows, hidden, pre_grad = experts(place, got, jnp.swapaxes(in_weight, 1, 2), out_weight)
     scattered = lax.all_to_all(parts.reshape(16, 16, width), PLANE, 0, 0, tiled=True)
     summed = added(scattered.reshape(256, width), 1, 16)
-    near = shifted(summed, lambda y, x, c: -out_shift(y, x, c))
-    far = shifted(summed, lambda y, x, c: 16 - out_shift(y, x, c))
+    near = shifted(summed, lambda y, x, z, c: -out_shift(y, x, z, c))
+    far = shifted(summed, lambda y, x, z, c: 16 - out_shift(y, x, z, c))
     home = (near.astype(F32) + far.astype(F32)).astype(BF)
     mine = home.reshape(2, 8, width)
     back = spread(jnp.where(leading, mine, mine[::-1])).reshape(256, width)
@@ -204,9 +208,11 @@
     own = lax.dynamic_slice(logit_grad, (0, 0, first), (2, 256, 16), allow_negative_indices=False)
     mine = jnp.einsum("ite,itd->ed", own, tokens, preferred_element_type=F32).astype(BF)
     mixed = jnp.einsum("ite,ied->itd", combine_b, expert_out, preferred_element_type=F32).astype(BF)
-    mine = added(gathered(mine, ("zr", "c"), 8).reshape(128, width), 1, 16)
+    other = lax.ppermute(mine, "c", [(0, 1), (1, 0)])
+    mine = (mine.astype(F32) + other.astype(F32)).astype(BF)
+    mine = added(gathered(mine, "zr", 4).reshape(64, width), 1, 16)
     mine, mixed = tied(mine, mixed)
-    mine = shifted(mine, lambda y, x, c: 4 * (0, 1, 2, -1)[x] * (1 - 2 * c))
+    mine = shifted(mine, group_shift)
     mine, logit_grad, slot_grad, rows, hidden, pre_grad = tied(mine, logit_grad, slot_grad, rows, hidden, pre_grad)
     shares = gathered(mine, PLANE, 16).reshape(256, width)
     slots, cotangents = rows[:, :64], rows[:, 64:]

time: 163 us -> 161 us (0.988)
  waiting for transfers between devices: 21.1 us -> 17.5 us
    all_to_all x2, waiting for transfers between devices: 14.3 us -> 9.6 us  [gathered(): return lax.all_to_all(out, axes, 0, 0, tiled=True)]
    ppermute x0 -> x1, starting transfers between devices: none -> 2.11 us  [on_device(): other = lax.ppermute(mine, 'c', [(0, 1), (1, 0)])]
    all_to_all x2, starting transfers between devices: 23 us -> 21.2 us  [gathered(): return lax.all_to_all(out, axes, 0, 0, tiled=True)]
  transfers between devices with their start and end apart: 6 -> 7, of which waited for: 5 -> 6; matrix products, arithmetic and copies ran while one was open for 4% -> 4% of each run, Pallas kernels for 0% -> 0%
where the time goes in v6:
time: 161 us; the launch traced here: 158 us
  starting transfers between devices  61.7 us (38%)
  blocking collectives  57.4 us (36%)
  waiting for transfers between devices  17.5 us (11%)
  matrix products  8.7 us (5%)
  Pallas kernels  6.41 us (4%)
  local copies, waits for them, and re-layouts  2.8 us (2%)
  other arithmetic  2.08 us (1%)
    all_to_all x2, blocking collectives, spread(): return lax.all_to_all(out, PLANE + ('c',), 0, 0, tiled=True)  40.8 us
    ppermute x4, starting transfers between devices, shifted(): return lax.ppermute(value, ALL, pairs)  38.5 us
    all_to_all x2, starting transfers between devices, gathered(): return lax.all_to_all(out, axes, 0, 0, tiled=True)  21.2 us
    all_to_all x1, blocking collectives, on_device(): lax.all_to_all(parts.reshape(16, 16, width), PLANE, 0, 0, tiled=True)  16.6 us
    all_to_all x2, waiting for transfers between devices, gathered(): return lax.all_to_all(out, axes, 0, 0, tiled=True)  9.6 us
    ppermute x4, waiting for transfers between devices, shifted(): return lax.ppermute(value, ALL, pairs)  6.81 us
    pallas_call x1, Pallas kernels, front(): pl.pallas_call(front_body, in_specs=[pl.BlockSpec(memory_space=pltpu.SMEM...  3.93 us
  transfers between devices with their start and end apart: 7, of which 6 were waited for; matrix products, arithmetic and copies ran while one was open for 4% of the time, Pallas kernels for 0%

profile of v6, /device:TPU:24, one launch (start us, length us, event | category | flops | bytes accessed | tf_op | source)
XLA Modules:
  0.0 157.5 jit_solution(15232287008855581310)
XLA Ops:
  0.6 0.7 pad_add_fusion.place_ref
  1.3 3.9 %shard_map.119 = (bf16[16,1280]{1,0:T(8,128)(2,1)}, f32[2,64,256]{2,1,0:T(8,128)}, f32[2,64,256]{2,1,0:T(8,128)}) custom-call(s32[3]{0:T(128)} %pad_add_fusion.place_ref, bf16[2,256,1280]{2,1,0:T(8,128)(2,1)} %tokens_ref.1, bf16[2,256,1280]{2,1,0:T(8,128)(2,1)} %cotangent_ref.1, bf16[64,1280]{1,0:T(8,128)(2,1)} %bitcast.73), custom_call_target="tpu_custom_call" | custom-call | tf_op jit(solution)/shard_map/pallas_call | solution.py:98
  5.2 0.0 copy-start
  5.2 0.0 copy-start.1
  5.2 0.0 copy-start.2
  5.2 20.1 %collective-permute-start = (bf16[16,1280]{1,0:T(8,128)(2,1)}, bf16[16,1280]{1,0:T(8,128)(2,1)S(1)}, u32[]{:S(2)}, u32[]{:S(2)}) collective-permute-start(bf16[16,1280]{1,0:T(8,128)(2,1)} %get-tuple-element.27), channel_id=1, source_target_pairs={{0,0},{1,1},{2,2},{3,3},{4,4},{5,5},{6,6},{7,7},{8,8},{9,9},{10,10... | collective-permute-start | bytes 122888 | tf_op jit(solution)/shard_map/ppermute | solution.py:31
  25.4 1.0 bitcast_convert_fusion
  26.4 0.1 fusion.17
  26.5 0.8 collective-permute-done
  27.4 21.0 %all_to_all.25 = bf16[32,8,1280]{2,1,0:T(8,128)(2,1)S(1)} all-to-all(bf16[32,8,1280]{2,1,0:T(8,128)(2,1)S(1)} %bitcast.71), channel_id=1, replica_groups=mesh['y'=4,'zh'=2,'x'=4,'zq'=4,'zr'=4,'c'=2] {'y','x','c'}, dimensions={0} | all-to-all | bytes 1310720 | tf_op jit(solution)/shard_map/all_to_all | solution.py:44
  48.4 0.0 copy-done
  48.4 0.0 copy-done.1
  48.4 0.0 copy-done.2
  48.4 0.0 copy-start.9
  48.5 2.5 %shard_map.120 = (bf16[256,1280]{1,0:T(8,128)(2,1)S(1)}, bf16[2,128,1280]{2,1,0:T(8,128)(2,1)S(1)}, bf16[2,64,160]{2,1,0:T(8,128)(2,1)S(1)}, bf16[2,64,160]{2,1,0:T(8,128)(2,1)S(1)}) custom-call(s32[3]{0:T(128)S(1)} %copy-done.2, bf16[256,1280]{1,0:T(8,128)(2,1)S(1)} %bitcast.62, bf16[2,160,1280]{2,1,0:T(8,128)(2,1)S(1)} %bitcast.63, ...), custom_call_target="tpu_custom_call" | custom-call | tf_op jit(solution)/shard_map/pallas_call | solution.py:155
  50.9 16.6 %all_to_all.26 = bf16[16,16,1280]{2,1,0:T(8,128)(2,1)S(1)} all-to-all(bf16[16,16,1280]{2,1,0:T(8,128)(2,1)S(1)} %bitcast.64), channel_id=1, replica_groups=mesh['y'=4,'zh'=2,'x'=4,'zq'=4,'zr'=4,'c'=2] {'y','x'}, dimensions={0} | all-to-all | bytes 1310720 | tf_op jit(solution)/shard_map/all_to_all | solution.py:194
  67.6 0.0 copy-done.9
  67.6 0.2 fusion.3
  67.8 13.4 %collective-permute-start.2 = (bf16[16,1280]{1,0:T(8,128)(2,1)S(1)}, bf16[16,1280]{1,0:T(8,128)(2,1)S(1)}, u32[]{:S(2)}, u32[]{:S(2)}) collective-permute-start(bf16[16,1280]{1,0:T(8,128)(2,1)S(1)} %fusion.3), channel_id=1, source_target_pairs={{0,128},{1,129},{2,130},{3,131},{4,132},{5,133},{6,134},{7,135},{8... | collective-permute-start | bytes 122888 | tf_op jit(solution)/shard_map/ppermute | solution.py:31
  81.2 4.3 %collective-permute-start.1 = (bf16[16,1280]{1,0:T(8,128)(2,1)S(1)}, bf16[16,1280]{1,0:T(8,128)(2,1)S(1)}, u32[]{:S(2)}, u32[]{:S(2)}) collective-permute-start(bf16[16,1280]{1,0:T(8,128)(2,1)S(1)} %fusion.3), channel_id=1, source_target_pairs={{0,0},{1,1},{2,2},{3,3},{4,4},{5,5},{6,6},{7,7},{8,8},{9,9},{10,10... | collective-permute-start | bytes 122888 | tf_op jit(solution)/shard_map/ppermute | solution.py:31
  85.5 2.2 %collective-permute-done.2 = bf16[16,1280]{1,0:T(8,128)(2,1)S(1)} collective-permute-done((bf16[16,1280]{1,0:T(8,128)(2,1)S(1)}, bf16[16,1280]{1,0:T(8,128)(2,1)S(1)}, u32[]{:S(2)}, u32[]{:S(2)}) %collective-permute-start.2) | collective-permute-done | bytes 40992 | tf_op jit(solution)/shard_map/ppermute | solution.py:31
  87.7 3.8 %collective-permute-done.1 = bf16[16,1280]{1,0:T(8,128)(2,1)S(1)} collective-permute-done((bf16[16,1280]{1,0:T(8,128)(2,1)S(1)}, bf16[16,1280]{1,0:T(8,128)(2,1)S(1)}, u32[]{:S(2)}, u32[]{:S(2)}) %collective-permute-start.1) | collective-permute-done | bytes 40992 | tf_op jit(solution)/shard_map/ppermute | solution.py:31
  91.5 19.8 %all_to_all.27 = bf16[32,8,1280]{2,1,0:T(8,128)(2,1)S(1)} all-to-all(bf16[32,8,1280]{2,1,0:T(8,128)(2,1)S(1)} %bitcast.72), channel_id=1, replica_groups=mesh['y'=4,'zh'=2,'x'=4,'zq'=4,'zr'=4,'c'=2] {'y','x','c'}, dimensions={0} | all-to-all | bytes 1310720 | tf_op jit(solution)/shard_map/all_to_all | solution.py:44
  111.3 0.0 copy-start.3
  111.3 0.3 convolution_convert_fusion.4
  111.6 0.0 copy-start.7
  111.7 0.0 copy-start.4
  111.7 0.9 copy-done.3
  112.6 0.5 convolution_bitcast_fusion.2
  113.1 0.0 copy-done.7
  113.1 0.0 copy-start.6
  113.1 0.2 fusion.9
  113.3 0.0 copy-done.4
  113.4 0.5 convolution_bitcast_fusion.1
  113.9 0.2 copy-done.6
  114.1 0.3 fusion.2
  114.3 0.0 copy-start.10
  114.3 2.1 %collective-permute-start.3 = (bf16[16,1280]{1,0:T(8,128)(2,1)S(1)}, bf16[16,1280]{1,0:T(8,128)(2,1)S(1)}, u32[]{:S(2)}, u32[]{:S(2)}) collective-permute-start(bf16[16,1280]{1,0:T(8,128)(2,1)S(1)} %fusion.2), channel_id=1, source_target_pairs={{0,1},{1,0},{2,3},{3,2},{4,5},{5,4},{6,7},{7,6},{8,9},{9,8},{10,11... | collective-permute-start | bytes 122888 | tf_op jit(solution)/shard_map/ppermute | solution.py:211
  116.5 1.1 collective-permute-done.3
  117.6 0.7 broadcast_in_dim.15
  118.3 3.3 %all-to-all-start.3 = ((bf16[4,16,1280]{2,1,0:T(8,128)(2,1)}), bf16[4,16,1280]{2,1,0:T(8,128)(2,1)S(1)}, u32[]{:S(2)}, u32[]{:S(2)}) async-start(bf16[4,16,1280]{2,1,0:T(8,128)(2,1)} %broadcast_in_dim.15), calls=%async_computation.3 | async-start | bytes 327680 | tf_op jit(solution)/shard_map/all_to_all | solution.py:68
  121.6 1.6 %convolution_convert_fusion.1 = bf16[2,256,1280]{2,1,0:T(8,128)(2,1)} fusion(bf16[2,256,64]{1,2,0:T(8,128)(2,1)S(1)} %get-tuple-element.34, bf16[2,64,1280]{2,1,0:T(8,128)(2,1)S(1)} %bitcast.66), kind=kOutput, calls=%fused_computation.3 | convolution fusion | flops 84541440 | bytes 1703936 | tf_op jit(solution)/shard_map/ite,ied->itd/dot_general | solution.py:210
  123.2 0.0 copy-start.5
  123.2 5.3 %all-to-all-done.3 = bf16[4,16,1280]{2,1,0:T(8,128)(2,1)S(1)} async-done(((bf16[4,16,1280]{2,1,0:T(8,128)(2,1)}), bf16[4,16,1280]{2,1,0:T(8,128)(2,1)S(1)}, u32[]{:S(2)}, u32[]{:S(2)}) %all-to-all-start.3) | async-done | bytes 163872 | tf_op jit(solution)/shard_map/all_to_all | solution.py:68
  128.5 0.0 copy-done.10
  128.5 0.1 fusion.4
  128.7 0.7 collective-permute-start.4
  129.4 0.0 collective-permute-done.4
  129.4 0.9 broadcast_in_dim.17
  130.2 17.8 %all-to-all-start.4 = ((bf16[16,16,1280]{2,1,0:T(8,128)(2,1)}), bf16[16,16,1280]{2,1,0:T(8,128)(2,1)S(1)}, u32[]{:S(2)}, u32[]{:S(2)}) async-start(bf16[16,16,1280]{2,1,0:T(8,128)(2,1)} %broadcast_in_dim.17), calls=%async_computation.4 | async-start | bytes 1310720 | tf_op jit(solution)/shard_map/all_to_all | solution.py:68
  148.1 0.0 copy-done.5
  148.1 1.6 %convolution_convert_fusion = bf16[2,256,1280]{2,1,0:T(8,128)(2,1)} fusion(bf16[2,64,1280]{2,1,0:T(8,128)(2,1)S(1)} %broadcast_in_dim.16, bf16[2,64,1280]{2,1,0:T(8,128)(2,1)S(1)} %bitcast.68, bf16[2,256,64]{1,2,0:T(8,128)(2,1)S(1)} %fusion.10, bf16[2,256,64]{1,2,0:T(8,128)(2,1)S(1)} %get-tuple-element.36), kind=kOutput, calls=%fused_computation.2 | convolution fusion | flops 170000384 | bytes 2097152 | tf_op jit(solution)/shard_map/itk,ikd->itd/dot_general | solution.py:223
  149.7 0.0 copy-start.8
  149.7 1.3 convolution_convert_fusion.3
  151.0 1.3 convolution_convert_fusion.2
  152.3 4.3 %all-to-all-done.4 = bf16[16,16,1280]{2,1,0:T(8,128)(2,1)S(1)} async-done(((bf16[16,16,1280]{2,1,0:T(8,128)(2,1)}), bf16[16,16,1280]{2,1,0:T(8,128)(2,1)S(1)}, u32[]{:S(2)}, u32[]{:S(2)}) %all-to-all-start.4) | async-done | bytes 655392 | tf_op jit(solution)/shard_map/all_to_all | solution.py:68
  156.6 0.0 copy-done.8
  156.6 0.9 convolution_convert_fusion.5
  (9 shorter events, 0.3 us)
Async XLA Ops:
  5.2 43.2 %copy-start = (bf16[2,1280,160]{1,2,0:T(8,128)(2,1)S(1)}, bf16[2,1280,160]{1,2,0:T(8,128)(2,1)}, u32[]{:S(2)}) copy-start(bf16[2,1280,160]{1,2,0:T(8,128)(2,1)} %param.10) | copy-start | bytes 2457604
  5.2 43.2 %copy-start.1 = (bf16[2,160,1280]{2,1,0:T(8,128)(2,1)S(1)}, bf16[2,160,1280]{2,1,0:T(8,128)(2,1)}, u32[]{:S(2)}) copy-start(bf16[2,160,1280]{2,1,0:T(8,128)(2,1)} %second_ref.1) | copy-start | bytes 2457604
  5.2 43.2 %copy-start.2 = (s32[3]{0:T(128)S(1)}, s32[3]{0:T(128)}, u32[]{:S(2)}) copy-start(s32[3]{0:T(128)} %pad_add_fusion.place_ref) | copy-start | bytes 40
  5.2 22.1 %collective-permute-start = (bf16[16,1280]{1,0:T(8,128)(2,1)}, bf16[16,1280]{1,0:T(8,128)(2,1)S(1)}, u32[]{:S(2)}, u32[]{:S(2)}) collective-permute-start(bf16[16,1280]{1,0:T(8,128)(2,1)} %get-tuple-element.27), channel_id=1, source_target_pairs={{0,0},{1,1},{2,2},{3,3},{4,4},{5,5},{6,6},{7,7},{8,8},{9,9},{10,10... | collective-permute-start | bytes 122888 | tf_op jit(solution)/shard_map/ppermute | solution.py:31
  48.4 19.1 %copy-start.9 = (bf16[16,256]{1,0:T(8,128)(2,1)S(1)}, bf16[16,256]{1,0:T(8,128)(2,1)}, u32[]{:S(2)}) copy-start(bf16[16,256]{1,0:T(8,128)(2,1)} %constant.128.clone) | copy-start | bytes 24580
  67.8 19.9 %collective-permute-start.2 = (bf16[16,1280]{1,0:T(8,128)(2,1)S(1)}, bf16[16,1280]{1,0:T(8,128)(2,1)S(1)}, u32[]{:S(2)}, u32[]{:S(2)}) collective-permute-start(bf16[16,1280]{1,0:T(8,128)(2,1)S(1)} %fusion.3), channel_id=1, source_target_pairs={{0,128},{1,129},{2,130},{3,131},{4,132},{5,133},{6,134},{7,135},{8... | collective-permute-start | bytes 122888 | tf_op jit(solution)/shard_map/ppermute | solution.py:31
  81.2 10.3 %collective-permute-start.1 = (bf16[16,1280]{1,0:T(8,128)(2,1)S(1)}, bf16[16,1280]{1,0:T(8,128)(2,1)S(1)}, u32[]{:S(2)}, u32[]{:S(2)}) collective-permute-start(bf16[16,1280]{1,0:T(8,128)(2,1)S(1)} %fusion.3), channel_id=1, source_target_pairs={{0,0},{1,1},{2,2},{3,3},{4,4},{5,5},{6,6},{7,7},{8,8},{9,9},{10,10... | collective-permute-start | bytes 122888 | tf_op jit(solution)/shard_map/ppermute | solution.py:31
  111.3 1.3 copy-start.3
  111.6 1.5 copy-start.7
  111.7 1.7 %copy-start.4 = (bf16[2,256,1280]{2,1,0:T(8,128)(2,1)S(1)}, bf16[2,256,1280]{2,1,0:T(8,128)(2,1)}, u32[]{:S(2)}) copy-start(bf16[2,256,1280]{2,1,0:T(8,128)(2,1)} %cotangent_ref.1) | copy-start | bytes 3932164
  113.1 0.9 copy-start.6
  114.3 14.2 %copy-start.10 = (bf16[16,64]{1,0:T(8,128)(2,1)S(1)}, bf16[16,64]{1,0:T(8,128)(2,1)}, u32[]{:S(2)}) copy-start(bf16[16,64]{1,0:T(8,128)(2,1)} %constant.129.clone) | copy-start | bytes 6148
  114.3 3.2 %collective-permute-start.3 = (bf16[16,1280]{1,0:T(8,128)(2,1)S(1)}, bf16[16,1280]{1,0:T(8,128)(2,1)S(1)}, u32[]{:S(2)}, u32[]{:S(2)}) collective-permute-start(bf16[16,1280]{1,0:T(8,128)(2,1)S(1)} %fusion.2), channel_id=1, source_target_pairs={{0,1},{1,0},{2,3},{3,2},{4,5},{5,4},{6,7},{7,6},{8,9},{9,8},{10,11... | collective-permute-start | bytes 122888 | tf_op jit(solution)/shard_map/ppermute | solution.py:211
  118.3 10.3 %all-to-all-start.3 = ((bf16[4,16,1280]{2,1,0:T(8,128)(2,1)}), bf16[4,16,1280]{2,1,0:T(8,128)(2,1)S(1)}, u32[]{:S(2)}, u32[]{:S(2)}) async-start(bf16[4,16,1280]{2,1,0:T(8,128)(2,1)} %broadcast_in_dim.15), calls=%async_computation.3 | async-start | bytes 327680 | tf_op jit(solution)/shard_map/all_to_all | solution.py:68
  123.2 24.8 %copy-start.5 = (bf16[1280,64]{0,1:T(8,128)(2,1)S(1)}, bf16[1280,64]{0,1:T(8,128)(2,1)}, u32[]{:S(2)}) copy-start(bf16[1280,64]{0,1:T(8,128)(2,1)} %param.9) | copy-start | bytes 491524
  128.7 0.7 collective-permute-start.4
  130.2 26.4 %all-to-all-start.4 = ((bf16[16,16,1280]{2,1,0:T(8,128)(2,1)}), bf16[16,16,1280]{2,1,0:T(8,128)(2,1)S(1)}, u32[]{:S(2)}, u32[]{:S(2)}) async-start(bf16[16,16,1280]{2,1,0:T(8,128)(2,1)} %broadcast_in_dim.17), calls=%async_computation.4 | async-start | bytes 1310720 | tf_op jit(solution)/shard_map/all_to_all | solution.py:68
  149.7 6.9 %copy-start.8 = (bf16[64,256]{1,0:T(8,128)(2,1)S(1)}, bf16[64,256]{1,0:T(8,128)(2,1)}, u32[]{:S(2)}) copy-start(bf16[64,256]{1,0:T(8,128)(2,1)} %constant.130.clone) | copy-start | bytes 98308

commit v7 on v6

--- a/solution.py
+++ b/solution.py
@@ -86,8 +86,10 @@
         ).astype(BF)
     z_lo, column, core = place_ref[0], place_ref[1], place_ref[2]
     row = lax.broadcasted_iota(jnp.int32, (16, 256), 0)
-    target = (z_lo + (1 - 2 * core) * column) & 15
-    wanted = ((row >> 2) & 1) * 128 + (row & 1) * 64 + 4 * target + (row >> 3) * 2 + ((row >> 1) & 1)
+    near = (z_lo + (1 - 2 * core) * column) & 15
+    cross = (z_lo - (1 - 2 * core) * column) & 15
+    block = jnp.where(row < 8, 4 * near + 2 * core, 4 * cross + 2 * (1 - core))
+    wanted = ((row >> 2) & 1) * 128 + (row & 1) * 64 + block + ((row >> 1) & 1)
     choose = (wanted == lax.broadcasted_iota(jnp.int32, (16, 256), 1)).astype(F32).astype(BF)
     sent_ref[...] = jnp.dot(choose, rows_ref[...], preferred_element_type=F32).astype(BF)
 
@@ -109,7 +111,7 @@
     )(place, tokens, cotangent, proj)
 
 
-def experts_body(place_ref, got_ref, first_ref, second_ref, out_ref, rows_ref, hidden_ref, grad_ref, parts_ref):
+def experts_body(got_ref, first_ref, second_ref, out_ref, rows_ref, hidden_ref, grad_ref, parts_ref):
     which = pl.program_id(0)
     row = lax.broadcasted_iota(jnp.int32, (128, 256), 0)
     wanted = ((row >> 1) & 31) * 8 + (row >> 6) * 4 + which * 2 + (row & 1)
@@ -135,18 +137,13 @@
 
     @pl.when(which == 1)
     def _():
-        core = place_ref[2]
         row = lax.broadcasted_iota(jnp.int32, (256, 256), 0)
-        other = (row >> 3) & 1
-        to = row >> 4
-        source = jnp.where(other == 1, (16 - to) & 15, to)
-        image_core = jnp.where(other == 1, 1 - core, core)
-        wanted = ((row >> 1) & 1) * 128 + ((row >> 2) & 1) * 64 + source * 4 + image_core * 2 + (row & 1)
+        wanted = ((row >> 1) & 1) * 128 + ((row >> 2) & 1) * 64 + (row >> 3) * 2 + (row & 1)
         choose = (wanted == lax.broadcasted_iota(jnp.int32, (256, 256), 1)).astype(F32).astype(BF)
         out_ref[...] = jnp.dot(choose, parts_ref[...], preferred_element_type=F32).astype(BF)
 
 
-def experts(place, got, first, second):
+def experts(got, first, second):
     width = got.shape[1]
     units = first.shape[1]
     whole = pl.BlockSpec((256, width), lambda i: (0, 0))
@@ -155,7 +152,7 @@
     return pl.pallas_call(
         experts_body,
         grid=(2,),
-        in_specs=[pl.BlockSpec(memory_space=pltpu.SMEM), whole, weight, weight],
+        in_specs=[whole, weight, weight],
         out_specs=[whole, pl.BlockSpec((1, 128, width), lambda i: (i, 0, 0)), act, act],
         out_shape=[
             jax.ShapeDtypeStruct((256, width), BF),
@@ -165,7 +162,7 @@
         ],
         scratch_shapes=[pltpu.VMEM((256, width), BF)],
         compiler_params=pltpu.CompilerParams(vmem_limit_bytes=24 * 2**20),
-    )(place, got, first, second)
+    )(got, first, second)
 
 
 def on_device(tokens, slot_proj, in_weight, out_weight, out_grad):
@@ -185,12 +182,13 @@
     outgoing, dispatch, combine = front(place, tokens, out_grad, slot_proj.T)
     dispatch, combine = jnp.swapaxes(dispatch, 1, 2), jnp.swapaxes(combine, 1, 2)
     dispatch_b, combine_b = dispatch.astype(BF), combine.astype(BF)
-    sent = shifted(outgoing, out_shift)
+    crossed = lax.ppermute(outgoing, "c", [(0, 1), (1, 0)])
+    sent = shifted(jnp.concatenate([outgoing[:8], crossed[8:]]), out_shift)
     sent, by_image, first, dispatch_b, combine_b, leading = tied(
         sent, by_image, lax.axis_index("y") * 16, dispatch_b, combine_b, core == 0
     )
-    got = spread(sent.reshape(2, 8, width)).reshape(256, width)
-    parts, rows, hidden, pre_grad = experts(place, got, jnp.swapaxes(in_weight, 1, 2), out_weight)
+    got = gathered(sent, PLANE, 16).reshape(256, width)
+    parts, rows, hidden, pre_grad = experts(got, jnp.swapaxes(in_weight, 1, 2), out_weight)
     scattered = lax.all_to_all(parts.reshape(16, 16, width), PLANE, 0, 0, tiled=True)
     summed = added(scattered.reshape(256, width), 1, 16)
     near = shifted(summed, lambda y, x, z, c: -out_shift(y, x, z, c))

time: 161 us -> 159 us (0.988)
  blocking collectives: 57.4 us -> 51.6 us
  starting transfers between devices: 61.7 us -> 65.9 us
    all_to_all x2 -> x1, blocking collectives: 40.8 us -> 17.6 us  [spread(): return lax.all_to_all(out, PLANE + ('c',), 0, 0, tiled=True)]
    all_to_all x0 -> x1, blocking collectives: none -> 19.9 us  [gathered(): return lax.all_to_all(out, axes, 0, 0, tiled=True)]
    all_to_all x1, blocking collectives: 16.6 us -> 14.1 us  [on_device(): lax.all_to_all(parts.reshape(16, 16, width), PLANE, 0, 0, tiled=True)]
    ppermute x4, starting transfers between devices: 38.5 us -> 40.8 us  [shifted(): return lax.ppermute(value, ALL, pairs)]
    ppermute x0 -> x1, starting transfers between devices: none -> 1.91 us  [on_device(): crossed = lax.ppermute(outgoing, 'c', [(0, 1), (1, 0)])]
  transfers between devices with their start and end apart: 7 -> 8, of which waited for: 6 -> 5; matrix products, arithmetic and copies ran while one was open for 4% -> 5% of each run, Pallas kernels for 0% -> 0%
where the time goes in v7:
time: 159 us; the launch traced here: 156 us
  starting transfers between devices  65.9 us (41%)
  blocking collectives  51.6 us (32%)
  waiting for transfers between devices  17.8 us (11%)
  matrix products  8.69 us (5%)
  Pallas kernels  5.81 us (4%)
  local copies, waits for them, and re-layouts  3.53 us (2%)
  other arithmetic  2.21 us (1%)
    ppermute x4, starting transfers between devices, shifted(): return lax.ppermute(value, ALL, pairs)  40.8 us
    all_to_all x2, starting transfers between devices, gathered(): return lax.all_to_all(out, axes, 0, 0, tiled=True)  21.1 us
    all_to_all x1, blocking collectives, gathered(): return lax.all_to_all(out, axes, 0, 0, tiled=True)  19.9 us
    all_to_all x1, blocking collectives, spread(): return lax.all_to_all(out, PLANE + ('c',), 0, 0, tiled=True)  17.6 us
    all_to_all x1, blocking collectives, on_device(): lax.all_to_all(parts.reshape(16, 16, width), PLANE, 0, 0, tiled=True)  14.1 us
    all_to_all x2, waiting for transfers between devices, gathered(): return lax.all_to_all(out, axes, 0, 0, tiled=True)  9.66 us
    ppermute x4, waiting for transfers between devices, shifted(): return lax.ppermute(value, ALL, pairs)  7.03 us
    pallas_call x1, Pallas kernels, front(): pl.pallas_call(front_body, in_specs=[pl.BlockSpec(memory_space=pltpu.SMEM...  3.93 us
  transfers between devices with their start and end apart: 8, of which 5 were waited for; matrix products, arithmetic and copies ran while one was open for 5% of the time, Pallas kernels for 0%

profile of v7, /device:TPU:24, one launch (start us, length us, event | category | flops | bytes accessed | tf_op | source)
XLA Modules:
  0.0 156.4 jit_solution(17317964390749864219)
XLA Ops:
  0.6 0.7 pad_add_fusion.place_ref
  1.3 3.9 %shard_map.119 = (bf16[16,1280]{1,0:T(8,128)(2,1)}, f32[2,64,256]{2,1,0:T(8,128)}, f32[2,64,256]{2,1,0:T(8,128)}) custom-call(s32[3]{0:T(128)} %pad_add_fusion.place_ref, bf16[2,256,1280]{2,1,0:T(8,128)(2,1)} %tokens_ref.1, bf16[2,256,1280]{2,1,0:T(8,128)(2,1)} %cotangent_ref.1, bf16[64,1280]{1,0:T(8,128)(2,1)} %bitcast.70), custom_call_target="tpu_custom_call" | custom-call | tf_op jit(solution)/shard_map/pallas_call | solution.py:100
  5.2 1.9 %collective-permute-start = (bf16[16,1280]{1,0:T(8,128)(2,1)}, bf16[16,1280]{1,0:T(8,128)(2,1)S(1)}, u32[]{:S(2)}, u32[]{:S(2)}) collective-permute-start(bf16[16,1280]{1,0:T(8,128)(2,1)} %get-tuple-element.27), channel_id=1, source_target_pairs={{0,1},{1,0},{2,3},{3,2},{4,5},{5,4},{6,7},{7,6},{8,9},{9,8},{10,11... | collective-permute-start | bytes 122888 | tf_op jit(solution)/shard_map/ppermute | solution.py:185
  7.2 0.0 copy-start
  7.2 0.0 copy-start.1
  7.2 1.1 bitcast_convert_fusion
  8.3 0.7 slice.20
  9.0 0.0 collective-permute-done
  9.1 20.0 %collective-permute-start.1 = (bf16[16,1280]{1,0:T(8,128)(2,1)S(1)}, bf16[16,1280]{1,0:T(8,128)(2,1)S(1)}, u32[]{:S(2)}, u32[]{:S(2)}) collective-permute-start(bf16[16,1280]{1,0:T(8,128)(2,1)S(1)} %pad_maximum_fusion), channel_id=1, source_target_pairs={{0,0},{1,1},{2,2},{3,3},{4,4},{5,5},{6,6},{7,7},{8,8},{9,9},{10,10... | collective-permute-start | bytes 122888 | tf_op jit(solution)/shard_map/ppermute | solution.py:31
  29.1 0.1 fusion.17
  29.2 1.5 collective-permute-done.1
  30.8 19.9 %all_to_all.25 = bf16[16,16,1280]{2,1,0:T(8,128)(2,1)S(1)} all-to-all(bf16[16,16,1280]{2,1,0:T(8,128)(2,1)S(1)} %broadcast_in_dim.10), channel_id=1, replica_groups=mesh['y'=4,'zh'=2,'x'=4,'zq'=4,'zr'=4,'c'=2] {'y','x'}, dimensions={0} | all-to-all | bytes 1310720 | tf_op jit(solution)/shard_map/all_to_all | solution.py:68
  50.6 0.0 copy-done
  50.6 0.0 copy-done.1
  50.6 0.0 copy-start.8
  50.6 1.9 %shard_map.120 = (bf16[256,1280]{1,0:T(8,128)(2,1)S(1)}, bf16[2,128,1280]{2,1,0:T(8,128)(2,1)S(1)}, bf16[2,64,160]{2,1,0:T(8,128)(2,1)S(1)}, bf16[2,64,160]{2,1,0:T(8,128)(2,1)S(1)}) custom-call(bf16[256,1280]{1,0:T(8,128)(2,1)S(1)} %bitcast.60, bf16[2,160,1280]{2,1,0:T(8,128)(2,1)S(1)} %bitcast.61, bf16[2,160,1280]{2,1,0:T(8,128)(2,1)S(1)} %copy-done.1), custom_call_target="tpu_custom_call" | custom-call | tf_op jit(solution)/shard_map/pallas_call | solution.py:152
  52.5 14.1 %all_to_all.26 = bf16[16,16,1280]{2,1,0:T(8,128)(2,1)S(1)} all-to-all(bf16[16,16,1280]{2,1,0:T(8,128)(2,1)S(1)} %bitcast.62), channel_id=1, replica_groups=mesh['y'=4,'zh'=2,'x'=4,'zq'=4,'zr'=4,'c'=2] {'y','x'}, dimensions={0} | all-to-all | bytes 1310720 | tf_op jit(solution)/shard_map/all_to_all | solution.py:192
  66.6 0.0 copy-done.8
  66.6 0.2 fusion.3
  66.8 15.8 %collective-permute-start.3 = (bf16[16,1280]{1,0:T(8,128)(2,1)S(1)}, bf16[16,1280]{1,0:T(8,128)(2,1)S(1)}, u32[]{:S(2)}, u32[]{:S(2)}) collective-permute-start(bf16[16,1280]{1,0:T(8,128)(2,1)S(1)} %fusion.3), channel_id=1, source_target_pairs={{0,128},{1,129},{2,130},{3,131},{4,132},{5,133},{6,134},{7,135},{8... | collective-permute-start | bytes 122888 | tf_op jit(solution)/shard_map/ppermute | solution.py:31
  82.7 4.3 %collective-permute-start.2 = (bf16[16,1280]{1,0:T(8,128)(2,1)S(1)}, bf16[16,1280]{1,0:T(8,128)(2,1)S(1)}, u32[]{:S(2)}, u32[]{:S(2)}) collective-permute-start(bf16[16,1280]{1,0:T(8,128)(2,1)S(1)} %fusion.3), channel_id=1, source_target_pairs={{0,0},{1,1},{2,2},{3,3},{4,4},{5,5},{6,6},{7,7},{8,8},{9,9},{10,10... | collective-permute-start | bytes 122888 | tf_op jit(solution)/shard_map/ppermute | solution.py:31
  87.0 0.0 collective-permute-done.3
  87.0 5.5 %collective-permute-done.2 = bf16[16,1280]{1,0:T(8,128)(2,1)S(1)} collective-permute-done((bf16[16,1280]{1,0:T(8,128)(2,1)S(1)}, bf16[16,1280]{1,0:T(8,128)(2,1)S(1)}, u32[]{:S(2)}, u32[]{:S(2)}) %collective-permute-start.2) | collective-permute-done | bytes 40992 | tf_op jit(solution)/shard_map/ppermute | solution.py:31
  92.6 17.6 %all_to_all.27 = bf16[32,8,1280]{2,1,0:T(8,128)(2,1)S(1)} all-to-all(bf16[32,8,1280]{2,1,0:T(8,128)(2,1)S(1)} %bitcast.69), channel_id=1, replica_groups=mesh['y'=4,'zh'=2,'x'=4,'zq'=4,'zr'=4,'c'=2] {'y','x','c'}, dimensions={0} | all-to-all | bytes 1310720 | tf_op jit(solution)/shard_map/all_to_all | solution.py:44
  110.2 0.0 copy-start.2
  110.2 0.3 convolution_convert_fusion.4
  110.6 0.0 copy-start.6
  110.6 0.0 copy-start.3
  110.6 0.9 copy-done.2
  111.5 0.5 convolution_bitcast_fusion.2
  112.0 0.0 copy-done.6
  112.1 0.0 copy-start.5
  112.1 0.2 fusion.9
  112.3 0.0 copy-done.3
  112.3 0.5 convolution_bitcast_fusion.1
  112.8 0.2 copy-done.5
  113.0 0.3 fusion.2
  113.3 0.0 copy-start.9
  113.3 2.1 %collective-permute-start.4 = (bf16[16,1280]{1,0:T(8,128)(2,1)S(1)}, bf16[16,1280]{1,0:T(8,128)(2,1)S(1)}, u32[]{:S(2)}, u32[]{:S(2)}) collective-permute-start(bf16[16,1280]{1,0:T(8,128)(2,1)S(1)} %fusion.2), channel_id=1, source_target_pairs={{0,1},{1,0},{2,3},{3,2},{4,5},{5,4},{6,7},{7,6},{8,9},{9,8},{10,11... | collective-permute-start | bytes 122888 | tf_op jit(solution)/shard_map/ppermute | solution.py:209
  115.4 1.1 collective-permute-done.4
  116.5 0.7 broadcast_in_dim.12
  117.2 3.3 %all-to-all-start.3 = ((bf16[4,16,1280]{2,1,0:T(8,128)(2,1)}), bf16[4,16,1280]{2,1,0:T(8,128)(2,1)S(1)}, u32[]{:S(2)}, u32[]{:S(2)}) async-start(bf16[4,16,1280]{2,1,0:T(8,128)(2,1)} %broadcast_in_dim.12), calls=%async_computation.3 | async-start | bytes 327680 | tf_op jit(solution)/shard_map/all_to_all | solution.py:68
  120.6 1.6 %convolution_convert_fusion.1 = bf16[2,256,1280]{2,1,0:T(8,128)(2,1)} fusion(bf16[2,256,64]{1,2,0:T(8,128)(2,1)S(1)} %get-tuple-element.34, bf16[2,64,1280]{2,1,0:T(8,128)(2,1)S(1)} %bitcast.64), kind=kOutput, calls=%fused_computation.3 | convolution fusion | flops 84541440 | bytes 1703936 | tf_op jit(solution)/shard_map/ite,ied->itd/dot_general | solution.py:208
  122.2 0.0 copy-start.4
  122.2 5.3 %all-to-all-done.3 = bf16[4,16,1280]{2,1,0:T(8,128)(2,1)S(1)} async-done(((bf16[4,16,1280]{2,1,0:T(8,128)(2,1)}), bf16[4,16,1280]{2,1,0:T(8,128)(2,1)S(1)}, u32[]{:S(2)}, u32[]{:S(2)}) %all-to-all-start.3) | async-done | bytes 163872 | tf_op jit(solution)/shard_map/all_to_all | solution.py:68
  127.5 0.0 copy-done.9
  127.5 0.1 fusion.4
  127.6 0.7 collective-permute-start.5
  128.3 0.0 collective-permute-done.5
  128.3 0.9 broadcast_in_dim.14
  129.2 17.7 %all-to-all-start.4 = ((bf16[16,16,1280]{2,1,0:T(8,128)(2,1)}), bf16[16,16,1280]{2,1,0:T(8,128)(2,1)S(1)}, u32[]{:S(2)}, u32[]{:S(2)}) async-start(bf16[16,16,1280]{2,1,0:T(8,128)(2,1)} %broadcast_in_dim.14), calls=%async_computation.4 | async-start | bytes 1310720 | tf_op jit(solution)/shard_map/all_to_all | solution.py:68
  146.9 0.0 copy-done.4
  146.9 1.6 %convolution_convert_fusion = bf16[2,256,1280]{2,1,0:T(8,128)(2,1)} fusion(bf16[2,64,1280]{2,1,0:T(8,128)(2,1)S(1)} %broadcast_in_dim.13, bf16[2,64,1280]{2,1,0:T(8,128)(2,1)S(1)} %bitcast.66, bf16[2,256,64]{1,2,0:T(8,128)(2,1)S(1)} %fusion.10, bf16[2,256,64]{1,2,0:T(8,128)(2,1)S(1)} %get-tuple-element.36), kind=kOutput, calls=%fused_computation.2 | convolution fusion | flops 170000384 | bytes 2097152 | tf_op jit(solution)/shard_map/itk,ikd->itd/dot_general | solution.py:221
  148.6 0.0 copy-start.7
  148.6 1.3 convolution_convert_fusion.3
  149.9 1.3 convolution_convert_fusion.2
  151.2 4.4 %all-to-all-done.4 = bf16[16,16,1280]{2,1,0:T(8,128)(2,1)S(1)} async-done(((bf16[16,16,1280]{2,1,0:T(8,128)(2,1)}), bf16[16,16,1280]{2,1,0:T(8,128)(2,1)S(1)}, u32[]{:S(2)}, u32[]{:S(2)}) %all-to-all-start.4) | async-done | bytes 655392 | tf_op jit(solution)/shard_map/all_to_all | solution.py:68
  155.5 0.0 copy-done.7
  155.5 0.9 convolution_convert_fusion.5
  (11 shorter events, 0.3 us)
Async XLA Ops:
  5.2 3.8 %collective-permute-start = (bf16[16,1280]{1,0:T(8,128)(2,1)}, bf16[16,1280]{1,0:T(8,128)(2,1)S(1)}, u32[]{:S(2)}, u32[]{:S(2)}) collective-permute-start(bf16[16,1280]{1,0:T(8,128)(2,1)} %get-tuple-element.27), channel_id=1, source_target_pairs={{0,1},{1,0},{2,3},{3,2},{4,5},{5,4},{6,7},{7,6},{8,9},{9,8},{10,11... | collective-permute-start | bytes 122888 | tf_op jit(solution)/shard_map/ppermute | solution.py:185
  7.2 43.5 %copy-start = (bf16[2,1280,160]{1,2,0:T(8,128)(2,1)S(1)}, bf16[2,1280,160]{1,2,0:T(8,128)(2,1)}, u32[]{:S(2)}) copy-start(bf16[2,1280,160]{1,2,0:T(8,128)(2,1)} %param.10) | copy-start | bytes 2457604
  7.2 43.5 %copy-start.1 = (bf16[2,160,1280]{2,1,0:T(8,128)(2,1)S(1)}, bf16[2,160,1280]{2,1,0:T(8,128)(2,1)}, u32[]{:S(2)}) copy-start(bf16[2,160,1280]{2,1,0:T(8,128)(2,1)} %second_ref.1) | copy-start | bytes 2457604
  9.1 21.7 %collective-permute-start.1 = (bf16[16,1280]{1,0:T(8,128)(2,1)S(1)}, bf16[16,1280]{1,0:T(8,128)(2,1)S(1)}, u32[]{:S(2)}, u32[]{:S(2)}) collective-permute-start(bf16[16,1280]{1,0:T(8,128)(2,1)S(1)} %pad_maximum_fusion), channel_id=1, source_target_pairs={{0,0},{1,1},{2,2},{3,3},{4,4},{5,5},{6,6},{7,7},{8,8},{9,9},{10,10... | collective-permute-start | bytes 122888 | tf_op jit(solution)/shard_map/ppermute | solution.py:31
  50.6 16.0 %copy-start.8 = (bf16[16,256]{1,0:T(8,128)(2,1)S(1)}, bf16[16,256]{1,0:T(8,128)(2,1)}, u32[]{:S(2)}) copy-start(bf16[16,256]{1,0:T(8,128)(2,1)} %constant.128.clone) | copy-start | bytes 24580
  66.8 20.2 %collective-permute-start.3 = (bf16[16,1280]{1,0:T(8,128)(2,1)S(1)}, bf16[16,1280]{1,0:T(8,128)(2,1)S(1)}, u32[]{:S(2)}, u32[]{:S(2)}) collective-permute-start(bf16[16,1280]{1,0:T(8,128)(2,1)S(1)} %fusion.3), channel_id=1, source_target_pairs={{0,128},{1,129},{2,130},{3,131},{4,132},{5,133},{6,134},{7,135},{8... | collective-permute-start | bytes 122888 | tf_op jit(solution)/shard_map/ppermute | solution.py:31
  82.7 9.8 %collective-permute-start.2 = (bf16[16,1280]{1,0:T(8,128)(2,1)S(1)}, bf16[16,1280]{1,0:T(8,128)(2,1)S(1)}, u32[]{:S(2)}, u32[]{:S(2)}) collective-permute-start(bf16[16,1280]{1,0:T(8,128)(2,1)S(1)} %fusion.3), channel_id=1, source_target_pairs={{0,0},{1,1},{2,2},{3,3},{4,4},{5,5},{6,6},{7,7},{8,8},{9,9},{10,10... | collective-permute-start | bytes 122888 | tf_op jit(solution)/shard_map/ppermute | solution.py:31
  110.2 1.3 copy-start.2
  110.6 1.5 copy-start.6
  110.6 1.7 %copy-start.3 = (bf16[2,256,1280]{2,1,0:T(8,128)(2,1)S(1)}, bf16[2,256,1280]{2,1,0:T(8,128)(2,1)}, u32[]{:S(2)}) copy-start(bf16[2,256,1280]{2,1,0:T(8,128)(2,1)} %cotangent_ref.1) | copy-start | bytes 3932164
  112.1 0.9 copy-start.5
  113.3 14.2 %copy-start.9 = (bf16[16,64]{1,0:T(8,128)(2,1)S(1)}, bf16[16,64]{1,0:T(8,128)(2,1)}, u32[]{:S(2)}) copy-start(bf16[16,64]{1,0:T(8,128)(2,1)} %constant.129.clone) | copy-start | bytes 6148
  113.3 3.2 %collective-permute-start.4 = (bf16[16,1280]{1,0:T(8,128)(2,1)S(1)}, bf16[16,1280]{1,0:T(8,128)(2,1)S(1)}, u32[]{:S(2)}, u32[]{:S(2)}) collective-permute-start(bf16[16,1280]{1,0:T(8,128)(2,1)S(1)} %fusion.2), channel_id=1, source_target_pairs={{0,1},{1,0},{2,3},{3,2},{4,5},{5,4},{6,7},{7,6},{8,9},{9,8},{10,11... | collective-permute-start | bytes 122888 | tf_op jit(solution)/shard_map/ppermute | solution.py:209
  117.2 10.3 %all-to-all-start.3 = ((bf16[4,16,1280]{2,1,0:T(8,128)(2,1)}), bf16[4,16,1280]{2,1,0:T(8,128)(2,1)S(1)}, u32[]{:S(2)}, u32[]{:S(2)}) async-start(bf16[4,16,1280]{2,1,0:T(8,128)(2,1)} %broadcast_in_dim.12), calls=%async_computation.3 | async-start | bytes 327680 | tf_op jit(solution)/shard_map/all_to_all | solution.py:68
  122.2 24.7 %copy-start.4 = (bf16[1280,64]{0,1:T(8,128)(2,1)S(1)}, bf16[1280,64]{0,1:T(8,128)(2,1)}, u32[]{:S(2)}) copy-start(bf16[1280,64]{0,1:T(8,128)(2,1)} %param.9) | copy-start | bytes 491524
  127.6 0.7 collective-permute-start.5
  129.2 26.3 %all-to-all-start.4 = ((bf16[16,16,1280]{2,1,0:T(8,128)(2,1)}), bf16[16,16,1280]{2,1,0:T(8,128)(2,1)S(1)}, u32[]{:S(2)}, u32[]{:S(2)}) async-start(bf16[16,16,1280]{2,1,0:T(8,128)(2,1)} %broadcast_in_dim.14), calls=%async_computation.4 | async-start | bytes 1310720 | tf_op jit(solution)/shard_map/all_to_all | solution.py:68
  148.6 7.0 %copy-start.7 = (bf16[64,256]{1,0:T(8,128)(2,1)S(1)}, bf16[64,256]{1,0:T(8,128)(2,1)}, u32[]{:S(2)}) copy-start(bf16[64,256]{1,0:T(8,128)(2,1)} %constant.130.clone) | copy-start | bytes 98308

commit v8 on v7

--- a/solution.py
+++ b/solution.py
@@ -68,7 +68,7 @@
     return lax.all_to_all(out, axes, 0, 0, tiled=True)
 
 
-def front_body(place_ref, tokens_ref, cotangent_ref, proj_ref, sent_ref, dispatch_ref, combine_ref, rows_ref):
+def front_body(z_ref, column_ref, core_ref, tokens_ref, cotangent_ref, proj_ref, sent_ref, dispatch_ref, combine_ref, rows_ref):
     for image in range(2):
         tokens = tokens_ref[image]
         logits = lax.dot_general(proj_ref[...], tokens, (((1,), (1,)), ((), ())), preferred_element_type=F32)
@@ -84,7 +84,7 @@
         rows_ref[64 * image + 128 : 64 * image + 192, :] = jnp.dot(
             combine.astype(BF), cotangent_ref[image], preferred_element_type=F32
         ).astype(BF)
-    z_lo, column, core = place_ref[0], place_ref[1], place_ref[2]
+    z_lo, column, core = z_ref[0], column_ref[0], core_ref[0]
     row = lax.broadcasted_iota(jnp.int32, (16, 256), 0)
     near = (z_lo + (1 - 2 * core) * column) & 15
     cross = (z_lo - (1 - 2 * core) * column) & 15
@@ -94,12 +94,12 @@
     sent_ref[...] = jnp.dot(choose, rows_ref[...], preferred_element_type=F32).astype(BF)
 
 
-def front(place, tokens, cotangent, proj):
+def front(places, tokens, cotangent, proj):
     width = tokens.shape[2]
     vmem = pl.BlockSpec(memory_space=pltpu.VMEM)
     return pl.pallas_call(
         front_body,
-        in_specs=[pl.BlockSpec(memory_space=pltpu.SMEM), vmem, vmem, vmem],
+        in_specs=[pl.BlockSpec(memory_space=pltpu.SMEM)] * 3 + [vmem] * 3,
         out_specs=[vmem, vmem, vmem],
         out_shape=[
             jax.ShapeDtypeStruct((16, width), BF),
@@ -108,7 +108,7 @@
         ],
         scratch_shapes=[pltpu.VMEM((256, width), BF)],
         compiler_params=pltpu.CompilerParams(vmem_limit_bytes=56 * 2**20),
-    )(place, tokens, cotangent, proj)
+    )(*places, tokens, cotangent, proj)
 
 
 def experts_body(got_ref, first_ref, second_ref, out_ref, rows_ref, hidden_ref, grad_ref, parts_ref):
@@ -178,12 +178,13 @@
         source * 16 + core_of * 8 + row // 128 * 4 + expert % 2 * 2 + (row // 64) % 2, 256
     )
 
-    place = jnp.stack([z_lo, column, core]).astype(jnp.int32)
-    outgoing, dispatch, combine = front(place, tokens, out_grad, slot_proj.T)
+    places = [value.astype(jnp.int32).reshape(1) for value in (z_lo, column, core)]
+    outgoing, dispatch, combine = front(places, tokens, out_grad, slot_proj.T)
     dispatch, combine = jnp.swapaxes(dispatch, 1, 2), jnp.swapaxes(combine, 1, 2)
+    crossed = lax.ppermute(outgoing, "c", [(0, 1), (1, 0)])
+    sent, dispatch, combine = tied(jnp.concatenate([outgoing[:8], crossed[8:]]), dispatch, combine)
     dispatch_b, combine_b = dispatch.astype(BF), combine.astype(BF)
-    crossed = lax.ppermute(outgoing, "c", [(0, 1), (1, 0)])
-    sent = shifted(jnp.concatenate([outgoing[:8], crossed[8:]]), out_shift)
+    sent = shifted(sent, out_shift)
     sent, by_image, first, dispatch_b, combine_b, leading = tied(
         sent, by_image, lax.axis_index("y") * 16, dispatch_b, combine_b, core == 0
     )
@@ -205,13 +206,13 @@
     logit_grad = (from_dispatch + from_combine).astype(BF)
     own = lax.dynamic_slice(logit_grad, (0, 0, first), (2, 256, 16), allow_negative_indices=False)
     mine = jnp.einsum("ite,itd->ed", own, tokens, preferred_element_type=F32).astype(BF)
-    mixed = jnp.einsum("ite,ied->itd", combine_b, expert_out, preferred_element_type=F32).astype(BF)
     other = lax.ppermute(mine, "c", [(0, 1), (1, 0)])
     mine = (mine.astype(F32) + other.astype(F32)).astype(BF)
     mine = added(gathered(mine, "zr", 4).reshape(64, width), 1, 16)
-    mine, mixed = tied(mine, mixed)
     mine = shifted(mine, group_shift)
-    mine, logit_grad, slot_grad, rows, hidden, pre_grad = tied(mine, logit_grad, slot_grad, rows, hidden, pre_grad)
+    mine, logit_grad, expert_out, slot_grad, rows, hidden, pre_grad = tied(
+        mine, logit_grad, expert_out, slot_grad, rows, hidden, pre_grad
+    )
     shares = gathered(mine, PLANE, 16).reshape(256, width)
     slots, cotangents = rows[:, :64], rows[:, 64:]
     out_weight_grad = jnp.einsum("erf,erd->efd", hidden, cotangents, preferred_element_type=F32).astype(BF)
@@ -219,6 +220,7 @@
     weights = jnp.concatenate([dispatch_b, logit_grad], axis=2)
     vectors = jnp.concatenate([slot_grad, jnp.broadcast_to(slot_proj.T, (2, 64, width))], axis=1)
     token_grad = jnp.einsum("itk,ikd->itd", weights, vectors, preferred_element_type=F32).astype(BF)
+    mixed = jnp.einsum("ite,ied->itd", combine_b, expert_out, preferred_element_type=F32).astype(BF)
     proj_grad = added(shares, 4, 16).T
     return (mixed, token_grad, proj_grad, in_weight_grad, out_weight_grad)
 

time: 159 us -> 158 us (level)
  blocking collectives: 51.6 us -> 61.1 us
  waiting for transfers between devices: 17.8 us -> 9.98 us
  starting transfers between devices: 65.9 us -> 64.2 us
    all_to_all x1 -> x2, blocking collectives: 19.9 us -> 28.9 us  [gathered(): return lax.all_to_all(out, axes, 0, 0, tiled=True)]
    all_to_all x2 -> x1, waiting for transfers between devices: 9.66 us -> 2.71 us  [gathered(): return lax.all_to_all(out, axes, 0, 0, tiled=True)]
    all_to_all x2 -> x1, starting transfers between devices: 21.1 us -> 20.1 us  [gathered(): return lax.all_to_all(out, axes, 0, 0, tiled=True)]
  transfers between devices with their start and end apart: 8 -> 7, of which waited for: 5 -> 5; matrix products, arithmetic and copies ran while one was open for 5% -> 5% of each run, Pallas kernels for 0% -> 0%
where the time goes in v8:
time: 158 us; the launch traced here: 156 us
  starting transfers between devices  64.2 us (41%)
  blocking collectives  61.1 us (39%)
  waiting for transfers between devices  9.98 us (6%)
  matrix products  8.7 us (6%)
  Pallas kernels  5.8 us (4%)
  local copies, waits for them, and re-layouts  2.87 us (2%)
  other arithmetic  2.26 us (1%)
    ppermute x4, starting transfers between devices, shifted(): return lax.ppermute(value, ALL, pairs)  40.2 us
    all_to_all x2, blocking collectives, gathered(): return lax.all_to_all(out, axes, 0, 0, tiled=True)  28.9 us
    all_to_all x1, starting transfers between devices, gathered(): return lax.all_to_all(out, axes, 0, 0, tiled=True)  20.1 us
    all_to_all x1, blocking collectives, spread(): return lax.all_to_all(out, PLANE + ('c',), 0, 0, tiled=True)  18.3 us
    all_to_all x1, blocking collectives, on_device(): lax.all_to_all(parts.reshape(16, 16, width), PLANE, 0, 0, tiled=True)  13.9 us
    ppermute x4, waiting for transfers between devices, shifted(): return lax.ppermute(value, ALL, pairs)  5.51 us
    pallas_call x1, Pallas kernels, front(): pl.pallas_call(front_body, in_specs=[pl.BlockSpec(memory_space=pltpu.SMEM...  3.92 us
  transfers between devices with their start and end apart: 7, of which 5 were waited for; matrix products, arithmetic and copies ran while one was open for 5% of the time, Pallas kernels for 0%

profile of v8, /device:TPU:24, one launch (start us, length us, event | category | flops | bytes accessed | tf_op | source)
XLA Modules:
  0.0 155.8 jit_solution(10277946494593158831)
XLA Ops:
  0.6 3.9 %shard_map.119 = (bf16[16,1280]{1,0:T(8,128)(2,1)}, f32[2,64,256]{2,1,0:T(8,128)}, f32[2,64,256]{2,1,0:T(8,128)}) custom-call(s32[1]{0:T(128)} %bitcast.z_ref, s32[1]{0:T(128)} %bitcast.1.column_ref, s32[1]{0:T(128)} %bitcast.2.core_ref, bf16[2,256,1280]{2,1,0:T(8,128)(2,1)} %tokens_ref.1, bf16[2,256,1280]{2,1,0:T(8,128)(2,1)} %cotangent_ref.1, ...), custom_call_target="tpu_custom_call" | custom-call | tf_op jit(solution)/shard_map/pallas_call | solution.py:100
  4.6 1.9 %collective-permute-start = (bf16[16,1280]{1,0:T(8,128)(2,1)}, bf16[16,1280]{1,0:T(8,128)(2,1)S(1)}, u32[]{:S(2)}, u32[]{:S(2)}) collective-permute-start(bf16[16,1280]{1,0:T(8,128)(2,1)} %get-tuple-element.28), channel_id=1, source_target_pairs={{0,1},{1,0},{2,3},{3,2},{4,5},{5,4},{6,7},{7,6},{8,9},{9,8},{10,11... | collective-permute-start | bytes 122888 | tf_op jit(solution)/shard_map/ppermute | solution.py:184
  6.5 0.7 slice.20
  7.2 0.6 collective-permute-done
  7.9 0.0 copy-start
  7.9 0.0 copy-start.1
  7.9 20.1 %collective-permute-start.1 = (bf16[16,1280]{1,0:T(8,128)(2,1)S(1)}, bf16[16,1280]{1,0:T(8,128)(2,1)S(1)}, u32[]{:S(2)}, u32[]{:S(2)}) collective-permute-start(bf16[16,1280]{1,0:T(8,128)(2,1)S(1)} %pad_maximum_fusion), channel_id=1, source_target_pairs={{0,0},{1,1},{2,2},{3,3},{4,4},{5,5},{6,6},{7,7},{8,8},{9,9},{10,10... | collective-permute-start | bytes 122888 | tf_op jit(solution)/shard_map/ppermute | solution.py:31
  28.0 0.1 fusion.17
  28.2 0.9 convert_element_type.65
  29.1 0.9 convert_element_type.66
  30.0 0.0 collective-permute-done.1
  30.0 19.2 %all_to_all.25 = bf16[16,16,1280]{2,1,0:T(8,128)(2,1)S(1)} all-to-all(bf16[16,16,1280]{2,1,0:T(8,128)(2,1)S(1)} %broadcast_in_dim.10), channel_id=1, replica_groups=mesh['y'=4,'zh'=2,'x'=4,'zq'=4,'zr'=4,'c'=2] {'y','x'}, dimensions={0} | all-to-all | bytes 1310720 | tf_op jit(solution)/shard_map/all_to_all | solution.py:68
  49.3 0.0 copy-done
  49.3 0.0 copy-done.1
  49.3 0.0 copy-start.8
  49.3 1.9 %shard_map.120 = (bf16[256,1280]{1,0:T(8,128)(2,1)S(1)}, bf16[2,128,1280]{2,1,0:T(8,128)(2,1)S(1)}, bf16[2,64,160]{2,1,0:T(8,128)(2,1)S(1)}, bf16[2,64,160]{2,1,0:T(8,128)(2,1)S(1)}) custom-call(bf16[256,1280]{1,0:T(8,128)(2,1)S(1)} %bitcast.48, bf16[2,160,1280]{2,1,0:T(8,128)(2,1)S(1)} %bitcast.49, bf16[2,160,1280]{2,1,0:T(8,128)(2,1)S(1)} %copy-done.1), custom_call_target="tpu_custom_call" | custom-call | tf_op jit(solution)/shard_map/pallas_call | solution.py:152
  51.2 13.9 %all_to_all.26 = bf16[16,16,1280]{2,1,0:T(8,128)(2,1)S(1)} all-to-all(bf16[16,16,1280]{2,1,0:T(8,128)(2,1)S(1)} %bitcast.50), channel_id=1, replica_groups=mesh['y'=4,'zh'=2,'x'=4,'zq'=4,'zr'=4,'c'=2] {'y','x'}, dimensions={0} | all-to-all | bytes 1310720 | tf_op jit(solution)/shard_map/all_to_all | solution.py:193
  65.1 0.0 copy-done.8
  65.1 0.2 fusion.3
  65.3 15.1 %collective-permute-start.3 = (bf16[16,1280]{1,0:T(8,128)(2,1)S(1)}, bf16[16,1280]{1,0:T(8,128)(2,1)S(1)}, u32[]{:S(2)}, u32[]{:S(2)}) collective-permute-start(bf16[16,1280]{1,0:T(8,128)(2,1)S(1)} %fusion.3), channel_id=1, source_target_pairs={{0,128},{1,129},{2,130},{3,131},{4,132},{5,133},{6,134},{7,135},{8... | collective-permute-start | bytes 122888 | tf_op jit(solution)/shard_map/ppermute | solution.py:31
  80.4 4.3 %collective-permute-start.2 = (bf16[16,1280]{1,0:T(8,128)(2,1)S(1)}, bf16[16,1280]{1,0:T(8,128)(2,1)S(1)}, u32[]{:S(2)}, u32[]{:S(2)}) collective-permute-start(bf16[16,1280]{1,0:T(8,128)(2,1)S(1)} %fusion.3), channel_id=1, source_target_pairs={{0,0},{1,1},{2,2},{3,3},{4,4},{5,5},{6,6},{7,7},{8,8},{9,9},{10,10... | collective-permute-start | bytes 122888 | tf_op jit(solution)/shard_map/ppermute | solution.py:31
  84.7 0.3 collective-permute-done.3
  85.0 5.2 %collective-permute-done.2 = bf16[16,1280]{1,0:T(8,128)(2,1)S(1)} collective-permute-done((bf16[16,1280]{1,0:T(8,128)(2,1)S(1)}, bf16[16,1280]{1,0:T(8,128)(2,1)S(1)}, u32[]{:S(2)}, u32[]{:S(2)}) %collective-permute-start.2) | collective-permute-done | bytes 40992 | tf_op jit(solution)/shard_map/ppermute | solution.py:31
  90.3 18.3 %all_to_all.27 = bf16[32,8,1280]{2,1,0:T(8,128)(2,1)S(1)} all-to-all(bf16[32,8,1280]{2,1,0:T(8,128)(2,1)S(1)} %bitcast.57), channel_id=1, replica_groups=mesh['y'=4,'zh'=2,'x'=4,'zq'=4,'zr'=4,'c'=2] {'y','x','c'}, dimensions={0} | all-to-all | bytes 1310720 | tf_op jit(solution)/shard_map/all_to_all | solution.py:44
  108.6 0.0 copy-start.2
  108.6 0.3 convolution_convert_fusion.4
  108.9 0.0 copy-start.6
  109.0 0.0 copy-start.3
  109.0 0.9 copy-done.2
  109.9 0.5 convolution_bitcast_fusion.2
  110.4 0.0 copy-done.6
  110.4 0.0 copy-start.5
  110.4 0.2 fusion.9
  110.6 0.0 copy-done.3
  110.6 0.5 convolution_bitcast_fusion.1
  111.2 0.2 copy-done.5
  111.3 0.0 copy-start.9
  111.4 0.3 fusion.2
  111.6 2.0 %collective-permute-start.4 = (bf16[16,1280]{1,0:T(8,128)(2,1)S(1)}, bf16[16,1280]{1,0:T(8,128)(2,1)S(1)}, u32[]{:S(2)}, u32[]{:S(2)}) collective-permute-start(bf16[16,1280]{1,0:T(8,128)(2,1)S(1)} %fusion.2), channel_id=1, source_target_pairs={{0,1},{1,0},{2,3},{3,2},{4,5},{5,4},{6,7},{7,6},{8,9},{9,8},{10,11... | collective-permute-start | bytes 122888 | tf_op jit(solution)/shard_map/ppermute | solution.py:209
  113.6 1.1 collective-permute-done.4
  114.8 9.6 %all_to_all.28 = bf16[4,16,1280]{2,1,0:T(8,128)(2,1)S(1)} all-to-all(bf16[4,16,1280]{2,1,0:T(8,128)(2,1)S(1)} %broadcast_in_dim.12), channel_id=1, replica_groups=mesh['y'=4,'zh'=2,'x'=4,'zq'=4,'zr'=4,'c'=2] {'zr'}, dimensions={0} | all-to-all | bytes 327680 | tf_op jit(solution)/shard_map/all_to_all | solution.py:68
  124.4 0.0 copy-done.9
  124.4 0.1 fusion.4
  124.6 0.7 collective-permute-start.5
  125.2 0.0 collective-permute-done.5
  125.3 0.9 broadcast_in_dim.14
  126.1 0.0 copy-start.4
  126.1 20.1 %all-to-all-start.4 = ((bf16[16,16,1280]{2,1,0:T(8,128)(2,1)}), bf16[16,16,1280]{2,1,0:T(8,128)(2,1)S(1)}, u32[]{:S(2)}, u32[]{:S(2)}) async-start(bf16[16,16,1280]{2,1,0:T(8,128)(2,1)} %broadcast_in_dim.14), calls=%async_computation.4 | async-start | bytes 1310720 | tf_op jit(solution)/shard_map/all_to_all | solution.py:68
  146.3 1.3 convolution_convert_fusion.3
  147.6 0.0 copy-done.4
  147.6 1.6 %convolution_convert_fusion = bf16[2,256,1280]{2,1,0:T(8,128)(2,1)} fusion(bf16[2,64,1280]{2,1,0:T(8,128)(2,1)S(1)} %broadcast_in_dim.13, bf16[2,64,1280]{2,1,0:T(8,128)(2,1)S(1)} %bitcast.54, bf16[2,256,64]{1,2,0:T(8,128)(2,1)S(1)} %fusion.10, bf16[2,256,64]{1,2,0:T(8,128)(2,1)S(1)} %convert_element_type.65), kind=kOutput, calls=%fused_computation.2 | convolution fusion | flops 170000384 | bytes 2097152 | tf_op jit(solution)/shard_map/itk,ikd->itd/dot_general | solution.py:222
  149.2 0.0 copy-start.7
  149.2 1.3 convolution_convert_fusion.2
  150.5 1.6 %convolution_convert_fusion.1 = bf16[2,256,1280]{2,1,0:T(8,128)(2,1)} fusion(bf16[2,256,64]{1,2,0:T(8,128)(2,1)S(1)} %convert_element_type.66, bf16[2,64,1280]{2,1,0:T(8,128)(2,1)S(1)} %bitcast.52), kind=kOutput, calls=%fused_computation.3 | convolution fusion | flops 84541440 | bytes 1703936 | tf_op jit(solution)/shard_map/ite,ied->itd/dot_general | solution.py:223
  152.1 2.7 %all-to-all-done.4 = bf16[16,16,1280]{2,1,0:T(8,128)(2,1)S(1)} async-done(((bf16[16,16,1280]{2,1,0:T(8,128)(2,1)}), bf16[16,16,1280]{2,1,0:T(8,128)(2,1)S(1)}, u32[]{:S(2)}, u32[]{:S(2)}) %all-to-all-start.4) | async-done | bytes 655392 | tf_op jit(solution)/shard_map/all_to_all | solution.py:68
  154.8 0.0 copy-done.7
  154.8 0.9 convolution_convert_fusion.5
  (12 shorter events, 0.3 us)
Async XLA Ops:
  4.6 3.3 %collective-permute-start = (bf16[16,1280]{1,0:T(8,128)(2,1)}, bf16[16,1280]{1,0:T(8,128)(2,1)S(1)}, u32[]{:S(2)}, u32[]{:S(2)}) collective-permute-start(bf16[16,1280]{1,0:T(8,128)(2,1)} %get-tuple-element.28), channel_id=1, source_target_pairs={{0,1},{1,0},{2,3},{3,2},{4,5},{5,4},{6,7},{7,6},{8,9},{9,8},{10,11... | collective-permute-start | bytes 122888 | tf_op jit(solution)/shard_map/ppermute | solution.py:184
  7.9 41.4 %copy-start = (bf16[2,1280,160]{1,2,0:T(8,128)(2,1)S(1)}, bf16[2,1280,160]{1,2,0:T(8,128)(2,1)}, u32[]{:S(2)}) copy-start(bf16[2,1280,160]{1,2,0:T(8,128)(2,1)} %param.10) | copy-start | bytes 2457604
  7.9 41.4 %copy-start.1 = (bf16[2,160,1280]{2,1,0:T(8,128)(2,1)S(1)}, bf16[2,160,1280]{2,1,0:T(8,128)(2,1)}, u32[]{:S(2)}) copy-start(bf16[2,160,1280]{2,1,0:T(8,128)(2,1)} %second_ref.1) | copy-start | bytes 2457604
  7.9 22.1 %collective-permute-start.1 = (bf16[16,1280]{1,0:T(8,128)(2,1)S(1)}, bf16[16,1280]{1,0:T(8,128)(2,1)S(1)}, u32[]{:S(2)}, u32[]{:S(2)}) collective-permute-start(bf16[16,1280]{1,0:T(8,128)(2,1)S(1)} %pad_maximum_fusion), channel_id=1, source_target_pairs={{0,0},{1,1},{2,2},{3,3},{4,4},{5,5},{6,6},{7,7},{8,8},{9,9},{10,10... | collective-permute-start | bytes 122888 | tf_op jit(solution)/shard_map/ppermute | solution.py:31
  49.3 15.8 %copy-start.8 = (bf16[16,256]{1,0:T(8,128)(2,1)S(1)}, bf16[16,256]{1,0:T(8,128)(2,1)}, u32[]{:S(2)}) copy-start(bf16[16,256]{1,0:T(8,128)(2,1)} %constant.128.clone) | copy-start | bytes 24580
  65.3 19.7 %collective-permute-start.3 = (bf16[16,1280]{1,0:T(8,128)(2,1)S(1)}, bf16[16,1280]{1,0:T(8,128)(2,1)S(1)}, u32[]{:S(2)}, u32[]{:S(2)}) collective-permute-start(bf16[16,1280]{1,0:T(8,128)(2,1)S(1)} %fusion.3), channel_id=1, source_target_pairs={{0,128},{1,129},{2,130},{3,131},{4,132},{5,133},{6,134},{7,135},{8... | collective-permute-start | bytes 122888 | tf_op jit(solution)/shard_map/ppermute | solution.py:31
  80.4 9.8 %collective-permute-start.2 = (bf16[16,1280]{1,0:T(8,128)(2,1)S(1)}, bf16[16,1280]{1,0:T(8,128)(2,1)S(1)}, u32[]{:S(2)}, u32[]{:S(2)}) collective-permute-start(bf16[16,1280]{1,0:T(8,128)(2,1)S(1)} %fusion.3), channel_id=1, source_target_pairs={{0,0},{1,1},{2,2},{3,3},{4,4},{5,5},{6,6},{7,7},{8,8},{9,9},{10,10... | collective-permute-start | bytes 122888 | tf_op jit(solution)/shard_map/ppermute | solution.py:31
  108.6 1.3 copy-start.2
  108.9 1.5 copy-start.6
  109.0 1.7 %copy-start.3 = (bf16[2,256,1280]{2,1,0:T(8,128)(2,1)S(1)}, bf16[2,256,1280]{2,1,0:T(8,128)(2,1)}, u32[]{:S(2)}) copy-start(bf16[2,256,1280]{2,1,0:T(8,128)(2,1)} %cotangent_ref.1) | copy-start | bytes 3932164
  110.4 0.9 copy-start.5
  111.3 13.1 %copy-start.9 = (bf16[16,64]{1,0:T(8,128)(2,1)S(1)}, bf16[16,64]{1,0:T(8,128)(2,1)}, u32[]{:S(2)}) copy-start(bf16[16,64]{1,0:T(8,128)(2,1)} %constant.129.clone) | copy-start | bytes 6148
  111.6 3.1 %collective-permute-start.4 = (bf16[16,1280]{1,0:T(8,128)(2,1)S(1)}, bf16[16,1280]{1,0:T(8,128)(2,1)S(1)}, u32[]{:S(2)}, u32[]{:S(2)}) collective-permute-start(bf16[16,1280]{1,0:T(8,128)(2,1)S(1)} %fusion.2), channel_id=1, source_target_pairs={{0,1},{1,0},{2,3},{3,2},{4,5},{5,4},{6,7},{7,6},{8,9},{9,8},{10,11... | collective-permute-start | bytes 122888 | tf_op jit(solution)/shard_map/ppermute | solution.py:209
  124.6 0.7 collective-permute-start.5
  126.1 21.4 %copy-start.4 = (bf16[1280,64]{0,1:T(8,128)(2,1)S(1)}, bf16[1280,64]{0,1:T(8,128)(2,1)}, u32[]{:S(2)}) copy-start(bf16[1280,64]{0,1:T(8,128)(2,1)} %param.9) | copy-start | bytes 491524
  126.1 28.7 %all-to-all-start.4 = ((bf16[16,16,1280]{2,1,0:T(8,128)(2,1)}), bf16[16,16,1280]{2,1,0:T(8,128)(2,1)S(1)}, u32[]{:S(2)}, u32[]{:S(2)}) async-start(bf16[16,16,1280]{2,1,0:T(8,128)(2,1)} %broadcast_in_dim.14), calls=%async_computation.4 | async-start | bytes 1310720 | tf_op jit(solution)/shard_map/all_to_all | solution.py:68
  149.2 5.6 %copy-start.7 = (bf16[64,256]{1,0:T(8,128)(2,1)S(1)}, bf16[64,256]{1,0:T(8,128)(2,1)}, u32[]{:S(2)}) copy-start(bf16[64,256]{1,0:T(8,128)(2,1)} %constant.130.clone) | copy-start | bytes 98308

commit v9 on v8

--- a/solution.py
+++ b/solution.py
@@ -68,7 +68,7 @@
     return lax.all_to_all(out, axes, 0, 0, tiled=True)
 
 
-def front_body(z_ref, column_ref, core_ref, tokens_ref, cotangent_ref, proj_ref, sent_ref, dispatch_ref, combine_ref, rows_ref):
+def front_body(z_ref, column_ref, core_ref, tokens_ref, cotangent_ref, proj_ref, kept_ref, crossing_ref, dispatch_ref, combine_ref, rows_ref):
     for image in range(2):
         tokens = tokens_ref[image]
         logits = lax.dot_general(proj_ref[...], tokens, (((1,), (1,)), ((), ())), preferred_element_type=F32)
@@ -91,7 +91,10 @@
     block = jnp.where(row < 8, 4 * near + 2 * core, 4 * cross + 2 * (1 - core))
     wanted = ((row >> 2) & 1) * 128 + (row & 1) * 64 + block + ((row >> 1) & 1)
     choose = (wanted == lax.broadcasted_iota(jnp.int32, (16, 256), 1)).astype(F32).astype(BF)
-    sent_ref[...] = jnp.dot(choose, rows_ref[...], preferred_element_type=F32).astype(BF)
+    chosen = jnp.dot(choose, rows_ref[...], preferred_element_type=F32)
+    own = lax.broadcasted_iota(jnp.int32, chosen.shape, 0) < 8
+    kept_ref[...] = jnp.where(own, chosen, 0.0).astype(BF)
+    crossing_ref[...] = jnp.where(own, 0.0, chosen).astype(BF)
 
 
 def front(places, tokens, cotangent, proj):
@@ -100,8 +103,9 @@
     return pl.pallas_call(
         front_body,
         in_specs=[pl.BlockSpec(memory_space=pltpu.SMEM)] * 3 + [vmem] * 3,
-        out_specs=[vmem, vmem, vmem],
+        out_specs=[vmem, vmem, vmem, vmem],
         out_shape=[
+            jax.ShapeDtypeStruct((16, width), BF),
             jax.ShapeDtypeStruct((16, width), BF),
             jax.ShapeDtypeStruct((2, 64, 256), F32),
             jax.ShapeDtypeStruct((2, 64, 256), F32),
@@ -165,6 +169,24 @@
     )(got, first, second)
 
 
+def staged_body(tokens_ref, cotangent_ref, tokens_out, cotangent_out):
+    tokens_out[...] = tokens_ref[...]
+    cotangent_out[...] = cotangent_ref[...]
+
+
+def staged(tokens, cotangent):
+    image = pl.BlockSpec((1,) + tokens.shape[1:], lambda i: (i, 0, 0))
+    shape = jax.ShapeDtypeStruct(tokens.shape, tokens.dtype)
+    return pl.pallas_call(
+        staged_body,
+        grid=(2,),
+        in_specs=[image, image],
+        out_specs=[image, image],
+        out_shape=[shape, shape],
+        compiler_params=pltpu.CompilerParams(vmem_limit_bytes=24 * 2**20),
+    )(tokens, cotangent)
+
+
 def on_device(tokens, slot_proj, in_weight, out_weight, out_grad):
     width = tokens.shape[2]
     column = lax.axis_index("y") * 4 + lax.axis_index("x")
@@ -179,10 +201,10 @@
     )
 
     places = [value.astype(jnp.int32).reshape(1) for value in (z_lo, column, core)]
-    outgoing, dispatch, combine = front(places, tokens, out_grad, slot_proj.T)
+    kept, crossing, dispatch, combine = front(places, tokens, out_grad, slot_proj.T)
     dispatch, combine = jnp.swapaxes(dispatch, 1, 2), jnp.swapaxes(combine, 1, 2)
-    crossed = lax.ppermute(outgoing, "c", [(0, 1), (1, 0)])
-    sent, dispatch, combine = tied(jnp.concatenate([outgoing[:8], crossed[8:]]), dispatch, combine)
+    crossed = lax.ppermute(crossing, "c", [(0, 1), (1, 0)])
+    sent, dispatch, combine = tied(kept + crossed, dispatch, combine)
     dispatch_b, combine_b = dispatch.astype(BF), combine.astype(BF)
     sent = shifted(sent, out_shift)
     sent, by_image, first, dispatch_b, combine_b, leading = tied(
@@ -192,20 +214,23 @@
     parts, rows, hidden, pre_grad = experts(got, jnp.swapaxes(in_weight, 1, 2), out_weight)
     scattered = lax.all_to_all(parts.reshape(16, 16, width), PLANE, 0, 0, tiled=True)
     summed = added(scattered.reshape(256, width), 1, 16)
+    summed, tokens_in, cotangent_in = tied(summed, tokens, out_grad)
+    tokens_near, cotangent_near = staged(tokens_in, cotangent_in)
     near = shifted(summed, lambda y, x, z, c: -out_shift(y, x, z, c))
     far = shifted(summed, lambda y, x, z, c: 16 - out_shift(y, x, z, c))
     home = (near.astype(F32) + far.astype(F32)).astype(BF)
+    home, tokens_near, cotangent_near = tied(home, tokens_near, cotangent_near)
     mine = home.reshape(2, 8, width)
     back = spread(jnp.where(leading, mine, mine[::-1])).reshape(256, width)
     results = picked(by_image, back).reshape(2, 2, 64, width)
     expert_out, slot_grad = results[0], results[1]
-    combine_grad = jnp.einsum("itd,ied->ite", out_grad, expert_out, preferred_element_type=F32)
-    dispatch_grad = jnp.einsum("itd,ied->ite", tokens, slot_grad, preferred_element_type=F32)
+    combine_grad = jnp.einsum("itd,ied->ite", cotangent_near, expert_out, preferred_element_type=F32)
+    dispatch_grad = jnp.einsum("itd,ied->ite", tokens_near, slot_grad, preferred_element_type=F32)
     from_dispatch = dispatch * (dispatch_grad - jnp.sum(dispatch * dispatch_grad, axis=1, keepdims=True))
     from_combine = combine * (combine_grad - jnp.sum(combine * combine_grad, axis=2, keepdims=True))
     logit_grad = (from_dispatch + from_combine).astype(BF)
     own = lax.dynamic_slice(logit_grad, (0, 0, first), (2, 256, 16), allow_negative_indices=False)
-    mine = jnp.einsum("ite,itd->ed", own, tokens, preferred_element_type=F32).astype(BF)
+    mine = jnp.einsum("ite,itd->ed", own, tokens_near, preferred_element_type=F32).astype(BF)
     other = lax.ppermute(mine, "c", [(0, 1), (1, 0)])
     mine = (mine.astype(F32) + other.astype(F32)).astype(BF)
     mine = added(gathered(mine, "zr", 4).reshape(64, width), 1, 16)

time: 158 us -> 161 us (1.019)
  matrix products: 8.7 us -> 11.9 us
  starting transfers between devices: 64.2 us -> 61.4 us
  other arithmetic: 2.26 us -> 4.17 us
    sub x0 -> x2, matrix products: none -> 4.23 us  [the longest x1 2.12 us: on_device(): dispatch_grad - jnp.sum(dispatch * dispatch_grad, axis=1, keepdims=True)]
    all_to_all x1, starting transfers between devices: 20.1 us -> 17.9 us  [gathered(): return lax.all_to_all(out, axes, 0, 0, tiled=True)]
  transfers between devices with their start and end apart: 7 -> 7, of which waited for: 5 -> 5; matrix products, arithmetic and copies ran while one was open for 5% -> 6% of each run, Pallas kernels for 0% -> 0%
where the time goes in v9:
time: 161 us; the launch traced here: 159 us
  starting transfers between devices  61.4 us (38%)
  blocking collectives  61.2 us (38%)
  matrix products  11.9 us (7%)
  waiting for transfers between devices  11.1 us (7%)
  Pallas kernels  6.08 us (4%)
  other arithmetic  4.17 us (3%)
  local copies, waits for them, and re-layouts  1.93 us (1%)
    ppermute x4, starting transfers between devices, shifted(): return lax.ppermute(value, ALL, pairs)  39.7 us
    all_to_all x2, blocking collectives, gathered(): return lax.all_to_all(out, axes, 0, 0, tiled=True)  28.8 us
    all_to_all x1, blocking collectives, spread(): return lax.all_to_all(out, PLANE + ('c',), 0, 0, tiled=True)  18.3 us
    all_to_all x1, starting transfers between devices, gathered(): return lax.all_to_all(out, axes, 0, 0, tiled=True)  17.9 us
    all_to_all x1, blocking collectives, on_device(): lax.all_to_all(parts.reshape(16, 16, width), PLANE, 0, 0, tiled=True)  14.1 us
    ppermute x4, waiting for transfers between devices, shifted(): return lax.ppermute(value, ALL, pairs)  5.27 us
    pallas_call x1, Pallas kernels, front(): pl.pallas_call(front_body, in_specs=[pl.BlockSpec(memory_space=pltpu.SMEM...  3.99 us
    all_to_all x1, waiting for transfers between devices, gathered(): return lax.all_to_all(out, axes, 0, 0, tiled=True)  3.29 us
  transfers between devices with their start and end apart: 7, of which 5 were waited for; matrix products, arithmetic and copies ran while one was open for 6% of the time, Pallas kernels for 0%

profile of v9, /device:TPU:24, one launch (start us, length us, event | category | flops | bytes accessed | tf_op | source)
XLA Modules:
  0.0 158.7 jit_solution(10045174835852965603)
XLA Ops:
  0.6 4.0 %shard_map.119 = (bf16[16,1280]{1,0:T(8,128)(2,1)}, bf16[16,1280]{1,0:T(8,128)(2,1)}, f32[2,64,256]{2,1,0:T(8,128)}, f32[2,64,256]{2,1,0:T(8,128)}) custom-call(s32[1]{0:T(128)} %bitcast.z_ref, s32[1]{0:T(128)} %bitcast.1.column_ref, s32[1]{0:T(128)} %bitcast.2.core_ref, bf16[2,256,1280]{2,1,0:T(8,128)(2,1)} %tokens_ref.2, ...), custom_call_target="tpu_custom_call" | custom-call | tf_op jit(solution)/shard_map/pallas_call | solution.py:103
  4.6 1.9 %collective-permute-start = (bf16[16,1280]{1,0:T(8,128)(2,1)}, bf16[16,1280]{1,0:T(8,128)(2,1)S(1)}, u32[]{:S(2)}, u32[]{:S(2)}) collective-permute-start(bf16[16,1280]{1,0:T(8,128)(2,1)} %get-tuple-element.38), channel_id=1, source_target_pairs={{0,1},{1,0},{2,3},{3,2},{4,5},{5,4},{6,7},{7,6},{8,9},{9,8},{10,11... | collective-permute-start | bytes 122888 | tf_op jit(solution)/shard_map/ppermute | solution.py:206
  6.6 1.4 collective-permute-done
  7.9 0.0 copy-start.2
  7.9 0.0 copy-start.3
  7.9 0.9 add.118
  8.9 20.0 %collective-permute-start.1 = (bf16[16,1280]{1,0:T(8,128)(2,1)S(1)}, bf16[16,1280]{1,0:T(8,128)(2,1)S(1)}, u32[]{:S(2)}, u32[]{:S(2)}) collective-permute-start(bf16[16,1280]{1,0:T(8,128)(2,1)S(1)} %add.118), channel_id=1, source_target_pairs={{0,0},{1,1},{2,2},{3,3},{4,4},{5,5},{6,6},{7,7},{8,8},{9,9},{10,10... | collective-permute-start | bytes 122888 | tf_op jit(solution)/shard_map/ppermute | solution.py:31
  28.9 0.1 fusion.17
  29.0 1.5 convert_element_type.65
  30.5 1.5 convert_element_type.66
  32.1 0.0 collective-permute-done.1
  32.1 18.3 %all_to_all.25 = bf16[16,16,1280]{2,1,0:T(8,128)(2,1)S(1)} all-to-all(bf16[16,16,1280]{2,1,0:T(8,128)(2,1)S(1)} %broadcast_in_dim.10), channel_id=1, replica_groups=mesh['y'=4,'zh'=2,'x'=4,'zq'=4,'zr'=4,'c'=2] {'y','x'}, dimensions={0} | all-to-all | bytes 1310720 | tf_op jit(solution)/shard_map/all_to_all | solution.py:68
  50.5 0.0 copy-done.2
  50.5 0.0 copy-done.3
  50.5 0.0 copy-start.10
  50.5 0.0 copy-start.1
  50.5 1.9 %shard_map.120 = (bf16[256,1280]{1,0:T(8,128)(2,1)S(1)}, bf16[2,128,1280]{2,1,0:T(8,128)(2,1)S(1)}, bf16[2,64,160]{2,1,0:T(8,128)(2,1)S(1)}, bf16[2,64,160]{2,1,0:T(8,128)(2,1)S(1)}) custom-call(bf16[256,1280]{1,0:T(8,128)(2,1)S(1)} %bitcast.47, bf16[2,160,1280]{2,1,0:T(8,128)(2,1)S(1)} %bitcast.48, bf16[2,160,1280]{2,1,0:T(8,128)(2,1)S(1)} %copy-done.3), custom_call_target="tpu_custom_call" | custom-call | tf_op jit(solution)/shard_map/pallas_call | solution.py:156
  52.4 0.0 copy-start
  52.4 14.1 %all_to_all.26 = bf16[16,16,1280]{2,1,0:T(8,128)(2,1)S(1)} all-to-all(bf16[16,16,1280]{2,1,0:T(8,128)(2,1)S(1)} %bitcast.49), channel_id=1, replica_groups=mesh['y'=4,'zh'=2,'x'=4,'zq'=4,'zr'=4,'c'=2] {'y','x'}, dimensions={0} | all-to-all | bytes 1310720 | tf_op jit(solution)/shard_map/all_to_all | solution.py:215
  66.4 0.0 copy-done.10
  66.4 0.2 fusion.3
  66.6 14.7 %collective-permute-start.3 = (bf16[16,1280]{1,0:T(8,128)(2,1)S(1)}, bf16[16,1280]{1,0:T(8,128)(2,1)S(1)}, u32[]{:S(2)}, u32[]{:S(2)}) collective-permute-start(bf16[16,1280]{1,0:T(8,128)(2,1)S(1)} %fusion.3), channel_id=1, source_target_pairs={{0,128},{1,129},{2,130},{3,131},{4,132},{5,133},{6,134},{7,135},{8... | collective-permute-start | bytes 122888 | tf_op jit(solution)/shard_map/ppermute | solution.py:31
  81.4 4.3 %collective-permute-start.2 = (bf16[16,1280]{1,0:T(8,128)(2,1)S(1)}, bf16[16,1280]{1,0:T(8,128)(2,1)S(1)}, u32[]{:S(2)}, u32[]{:S(2)}) collective-permute-start(bf16[16,1280]{1,0:T(8,128)(2,1)S(1)} %fusion.3), channel_id=1, source_target_pairs={{0,0},{1,1},{2,2},{3,3},{4,4},{5,5},{6,6},{7,7},{8,8},{9,9},{10,10... | collective-permute-start | bytes 122888 | tf_op jit(solution)/shard_map/ppermute | solution.py:31
  85.7 0.0 copy-done.1
  85.7 0.0 copy-done
  85.7 0.2 shard_map.121
  85.9 0.6 collective-permute-done.3
  86.5 4.6 %collective-permute-done.2 = bf16[16,1280]{1,0:T(8,128)(2,1)S(1)} collective-permute-done((bf16[16,1280]{1,0:T(8,128)(2,1)S(1)}, bf16[16,1280]{1,0:T(8,128)(2,1)S(1)}, u32[]{:S(2)}, u32[]{:S(2)}) %collective-permute-start.2) | collective-permute-done | bytes 40992 | tf_op jit(solution)/shard_map/ppermute | solution.py:31
  91.3 18.3 %all_to_all.27 = bf16[32,8,1280]{2,1,0:T(8,128)(2,1)S(1)} all-to-all(bf16[32,8,1280]{2,1,0:T(8,128)(2,1)S(1)} %bitcast.56), channel_id=1, replica_groups=mesh['y'=4,'zh'=2,'x'=4,'zq'=4,'zr'=4,'c'=2] {'y','x','c'}, dimensions={0} | all-to-all | bytes 1310720 | tf_op jit(solution)/shard_map/all_to_all | solution.py:44
  109.6 0.3 convolution_convert_fusion.4
  109.9 0.9 fusion.37
  110.8 2.1 %fusion.7 = f32[2,256,64]{1,2,0:T(8,128)S(1)} fusion(f32[2,256,64]{1,2,0:T(8,128)} %bitcast.63, bf16[2,256,1280]{2,1,0:T(8,128)(2,1)S(1)} %get-tuple-element.56, bf16[2,64,1280]{2,1,0:T(8,128)(2,1)} %bitcast.50), kind=kOutput, calls=%fused_computation.16 | convolution fusion | flops 167871040 | bytes 1900544 | tf_op jit(solution)/shard_map/sub | solution.py:230
  112.9 2.1 %fusion.10 = bf16[2,256,64]{1,2,0:T(8,128)(2,1)S(1)} fusion(f32[2,256,64]{1,2,0:T(8,128)S(1)} %fusion.7, f32[2,256,64]{1,2,0:T(8,128)} %bitcast.61, bf16[2,256,1280]{2,1,0:T(8,128)(2,1)S(1)} %get-tuple-element.52, bf16[2,64,1280]{2,1,0:T(8,128)(2,1)} %bitcast.52), kind=kOutput, calls=%fused_computation.19 | convolution fusion | flops 167936384 | bytes 1966080 | tf_op jit(solution)/shard_map/sub | solution.py:229
  115.0 0.0 copy-start.11
  115.0 0.3 fusion.2
  115.3 2.0 %collective-permute-start.4 = (bf16[16,1280]{1,0:T(8,128)(2,1)S(1)}, bf16[16,1280]{1,0:T(8,128)(2,1)S(1)}, u32[]{:S(2)}, u32[]{:S(2)}) collective-permute-start(bf16[16,1280]{1,0:T(8,128)(2,1)S(1)} %fusion.2), channel_id=1, source_target_pairs={{0,1},{1,0},{2,3},{3,2},{4,5},{5,4},{6,7},{7,6},{8,9},{9,8},{10,11... | collective-permute-start | bytes 122888 | tf_op jit(solution)/shard_map/ppermute | solution.py:234
  117.3 1.1 collective-permute-done.4
  118.5 10.5 %all_to_all.28 = bf16[4,16,1280]{2,1,0:T(8,128)(2,1)S(1)} all-to-all(bf16[4,16,1280]{2,1,0:T(8,128)(2,1)S(1)} %broadcast_in_dim.12), channel_id=1, replica_groups=mesh['y'=4,'zh'=2,'x'=4,'zq'=4,'zr'=4,'c'=2] {'zr'}, dimensions={0} | all-to-all | bytes 327680 | tf_op jit(solution)/shard_map/all_to_all | solution.py:68
  129.0 0.0 copy-done.11
  129.0 0.1 fusion.4
  129.1 0.7 collective-permute-start.5
  129.8 0.0 collective-permute-done.5
  129.8 0.9 broadcast_in_dim.14
  130.7 0.0 copy-start.6
  130.7 0.0 copy-start.5
  130.7 0.0 copy-start.7
  130.7 17.9 %all-to-all-start.4 = ((bf16[16,16,1280]{2,1,0:T(8,128)(2,1)}), bf16[16,16,1280]{2,1,0:T(8,128)(2,1)S(1)}, u32[]{:S(2)}, u32[]{:S(2)}) async-start(bf16[16,16,1280]{2,1,0:T(8,128)(2,1)} %broadcast_in_dim.14), calls=%async_computation.4 | async-start | bytes 1310720 | tf_op jit(solution)/shard_map/all_to_all | solution.py:68
  148.5 1.3 convolution_convert_fusion.3
  149.9 0.0 copy-done.6
  149.9 0.0 copy-done.5
  149.9 0.0 copy-done.7
  149.9 0.0 copy-start.4
  149.9 0.0 copy-start.8
  149.9 1.6 %convolution_convert_fusion = bf16[2,256,1280]{2,1,0:T(8,128)(2,1)} fusion(bf16[2,64,1280]{2,1,0:T(8,128)(2,1)S(1)} %broadcast_in_dim.13, bf16[2,64,1280]{2,1,0:T(8,128)(2,1)S(1)} %bitcast.53, bf16[2,256,64]{1,2,0:T(8,128)(2,1)S(1)} %fusion.10, bf16[2,256,64]{1,2,0:T(8,128)(2,1)S(1)} %copy-done.7), kind=kOutput, calls=%fused_computation.2 | convolution fusion | flops 170000384 | bytes 2097152 | tf_op jit(solution)/shard_map/itk,ikd->itd/dot_general | solution.py:247
  151.5 0.0 copy-start.9
  151.5 1.3 convolution_convert_fusion.2
  152.8 0.0 copy-done.4
  152.8 0.0 copy-done.8
  152.8 1.6 %convolution_convert_fusion.1 = bf16[2,256,1280]{2,1,0:T(8,128)(2,1)} fusion(bf16[2,256,64]{1,2,0:T(8,128)(2,1)S(1)} %copy-done.8, bf16[2,64,1280]{2,1,0:T(8,128)(2,1)S(1)} %bitcast.51), kind=kOutput, calls=%fused_computation.3 | convolution fusion | flops 84541440 | bytes 1703936 | tf_op jit(solution)/shard_map/ite,ied->itd/dot_general | solution.py:248
  154.4 3.3 %all-to-all-done.4 = bf16[16,16,1280]{2,1,0:T(8,128)(2,1)S(1)} async-done(((bf16[16,16,1280]{2,1,0:T(8,128)(2,1)}), bf16[16,16,1280]{2,1,0:T(8,128)(2,1)S(1)}, u32[]{:S(2)}, u32[]{:S(2)}) %all-to-all-start.4) | async-done | bytes 655392 | tf_op jit(solution)/shard_map/all_to_all | solution.py:68
  157.7 0.0 copy-done.9
  157.7 0.9 convolution_convert_fusion.5
  (8 shorter events, 0.2 us)
Async XLA Ops:
  4.6 3.3 %collective-permute-start = (bf16[16,1280]{1,0:T(8,128)(2,1)}, bf16[16,1280]{1,0:T(8,128)(2,1)S(1)}, u32[]{:S(2)}, u32[]{:S(2)}) collective-permute-start(bf16[16,1280]{1,0:T(8,128)(2,1)} %get-tuple-element.38), channel_id=1, source_target_pairs={{0,1},{1,0},{2,3},{3,2},{4,5},{5,4},{6,7},{7,6},{8,9},{9,8},{10,11... | collective-permute-start | bytes 122888 | tf_op jit(solution)/shard_map/ppermute | solution.py:206
  7.9 42.5 %copy-start.2 = (bf16[2,1280,160]{1,2,0:T(8,128)(2,1)S(1)}, bf16[2,1280,160]{1,2,0:T(8,128)(2,1)}, u32[]{:S(2)}) copy-start(bf16[2,1280,160]{1,2,0:T(8,128)(2,1)} %param.10) | copy-start | bytes 2457604
  7.9 42.5 %copy-start.3 = (bf16[2,160,1280]{2,1,0:T(8,128)(2,1)S(1)}, bf16[2,160,1280]{2,1,0:T(8,128)(2,1)}, u32[]{:S(2)}) copy-start(bf16[2,160,1280]{2,1,0:T(8,128)(2,1)} %second_ref.1) | copy-start | bytes 2457604
  8.9 23.2 %collective-permute-start.1 = (bf16[16,1280]{1,0:T(8,128)(2,1)S(1)}, bf16[16,1280]{1,0:T(8,128)(2,1)S(1)}, u32[]{:S(2)}, u32[]{:S(2)}) collective-permute-start(bf16[16,1280]{1,0:T(8,128)(2,1)S(1)} %add.118), channel_id=1, source_target_pairs={{0,0},{1,1},{2,2},{3,3},{4,4},{5,5},{6,6},{7,7},{8,8},{9,9},{10,10... | collective-permute-start | bytes 122888 | tf_op jit(solution)/shard_map/ppermute | solution.py:31
  50.5 16.0 %copy-start.10 = (bf16[16,256]{1,0:T(8,128)(2,1)S(1)}, bf16[16,256]{1,0:T(8,128)(2,1)}, u32[]{:S(2)}) copy-start(bf16[16,256]{1,0:T(8,128)(2,1)} %constant.128.clone) | copy-start | bytes 24580
  50.5 35.2 %copy-start.1 = (bf16[2,256,1280]{2,1,0:T(8,128)(2,1)S(1)}, bf16[2,256,1280]{2,1,0:T(8,128)(2,1)}, u32[]{:S(2)}) copy-start(bf16[2,256,1280]{2,1,0:T(8,128)(2,1)} %cotangent_ref.2) | copy-start | bytes 3932164
  52.4 33.3 %copy-start = (bf16[2,256,1280]{2,1,0:T(8,128)(2,1)S(1)}, bf16[2,256,1280]{2,1,0:T(8,128)(2,1)}, u32[]{:S(2)}) copy-start(bf16[2,256,1280]{2,1,0:T(8,128)(2,1)} %tokens_ref.2) | copy-start | bytes 3932164
  66.6 19.9 %collective-permute-start.3 = (bf16[16,1280]{1,0:T(8,128)(2,1)S(1)}, bf16[16,1280]{1,0:T(8,128)(2,1)S(1)}, u32[]{:S(2)}, u32[]{:S(2)}) collective-permute-start(bf16[16,1280]{1,0:T(8,128)(2,1)S(1)} %fusion.3), channel_id=1, source_target_pairs={{0,128},{1,129},{2,130},{3,131},{4,132},{5,133},{6,134},{7,135},{8... | collective-permute-start | bytes 122888 | tf_op jit(solution)/shard_map/ppermute | solution.py:31
  81.4 9.8 %collective-permute-start.2 = (bf16[16,1280]{1,0:T(8,128)(2,1)S(1)}, bf16[16,1280]{1,0:T(8,128)(2,1)S(1)}, u32[]{:S(2)}, u32[]{:S(2)}) collective-permute-start(bf16[16,1280]{1,0:T(8,128)(2,1)S(1)} %fusion.3), channel_id=1, source_target_pairs={{0,0},{1,1},{2,2},{3,3},{4,4},{5,5},{6,6},{7,7},{8,8},{9,9},{10,10... | collective-permute-start | bytes 122888 | tf_op jit(solution)/shard_map/ppermute | solution.py:31
  115.0 14.0 %copy-start.11 = (bf16[16,64]{1,0:T(8,128)(2,1)S(1)}, bf16[16,64]{1,0:T(8,128)(2,1)}, u32[]{:S(2)}) copy-start(bf16[16,64]{1,0:T(8,128)(2,1)} %constant.129.clone) | copy-start | bytes 6148
  115.3 3.1 %collective-permute-start.4 = (bf16[16,1280]{1,0:T(8,128)(2,1)S(1)}, bf16[16,1280]{1,0:T(8,128)(2,1)S(1)}, u32[]{:S(2)}, u32[]{:S(2)}) collective-permute-start(bf16[16,1280]{1,0:T(8,128)(2,1)S(1)} %fusion.2), channel_id=1, source_target_pairs={{0,1},{1,0},{2,3},{3,2},{4,5},{5,4},{6,7},{7,6},{8,9},{9,8},{10,11... | collective-permute-start | bytes 122888 | tf_op jit(solution)/shard_map/ppermute | solution.py:234
  129.1 0.7 collective-permute-start.5
  130.7 19.2 %copy-start.6 = (bf16[1280,64]{0,1:T(8,128)(2,1)S(1)}, bf16[1280,64]{0,1:T(8,128)(2,1)}, u32[]{:S(2)}) copy-start(bf16[1280,64]{0,1:T(8,128)(2,1)} %param.9) | copy-start | bytes 491524
  130.7 19.2 %copy-start.5 = (bf16[128,1280]{1,0:T(8,128)(2,1)S(1)}, bf16[128,1280]{1,0:T(8,128)(2,1)}, u32[]{:S(2)}) copy-start(bf16[128,1280]{1,0:T(8,128)(2,1)} %get-tuple-element.69) | copy-start | bytes 983044
  130.7 19.2 %copy-start.7 = (bf16[2,256,64]{1,2,0:T(8,128)(2,1)S(1)}, bf16[2,256,64]{1,2,0:T(8,128)(2,1)}, u32[]{:S(2)}) copy-start(bf16[2,256,64]{1,2,0:T(8,128)(2,1)} %convert_element_type.65) | copy-start | bytes 196612
  130.7 27.0 %all-to-all-start.4 = ((bf16[16,16,1280]{2,1,0:T(8,128)(2,1)}), bf16[16,16,1280]{2,1,0:T(8,128)(2,1)S(1)}, u32[]{:S(2)}, u32[]{:S(2)}) async-start(bf16[16,16,1280]{2,1,0:T(8,128)(2,1)} %broadcast_in_dim.14), calls=%async_computation.4 | async-start | bytes 1310720 | tf_op jit(solution)/shard_map/all_to_all | solution.py:68
  149.9 2.9 %copy-start.4 = (bf16[128,1280]{1,0:T(8,128)(2,1)S(1)}, bf16[128,1280]{1,0:T(8,128)(2,1)}, u32[]{:S(2)}) copy-start(bf16[128,1280]{1,0:T(8,128)(2,1)} %get-tuple-element.70) | copy-start | bytes 983044
  149.9 2.9 %copy-start.8 = (bf16[2,256,64]{1,2,0:T(8,128)(2,1)S(1)}, bf16[2,256,64]{1,2,0:T(8,128)(2,1)}, u32[]{:S(2)}) copy-start(bf16[2,256,64]{1,2,0:T(8,128)(2,1)} %convert_element_type.66) | copy-start | bytes 196612
  151.5 6.2 %copy-start.9 = (bf16[64,256]{1,0:T(8,128)(2,1)S(1)}, bf16[64,256]{1,0:T(8,128)(2,1)}, u32[]{:S(2)}) copy-start(bf16[64,256]{1,0:T(8,128)(2,1)} %constant.130.clone) | copy-start | bytes 98308
